TPU v7x, 32 devices: a whole 2x2x4 slice. The times are simulated.
32 devices in a mesh: section: 2 (over x), fsdp: 4 (over y, core), dp: 4 (over z).
Axes of the slice: x: 2, y: 2, z: 4, core: 2. Of those that a mesh axis runs over, the one named last changes fastest.
Arguments:
- ends: bfloat16 [2, 2, 4, 1024, 2048], P('section', None, 'dp', 'fsdp'), may hold values from -6 to 6
- positions: int32 [2, 4, 1024], P(None, 'dp', 'fsdp'), may hold values from 0 to 4093, as said below
- attn_gain: bfloat16 [2, 2048], P('section', 'fsdp'), may hold values from 0.5 to 1.5
- w_query: bfloat16 [2, 2048, 2048], P('section', 'fsdp'), may hold values from -0.125 to 0.125
- w_key: bfloat16 [2, 2048, 512], P('section', 'fsdp'), may hold values from -0.125 to 0.125
- w_value: bfloat16 [2, 2048, 512], P('section', 'fsdp'), may hold values from -0.125 to 0.125
- w_out: bfloat16 [2, 2048, 2048], P('section', 'fsdp'), may hold values from -1.5 to 1.5
- mlp_gain: bfloat16 [2, 2048], P('section', 'fsdp'), may hold values from 0.5 to 1.5
- w_gate: bfloat16 [2, 2048, 8192], P('section', 'fsdp'), may hold values from -0.125 to 0.125
- w_up: bfloat16 [2, 2048, 8192], P('section', 'fsdp'), may hold values from -0.125 to 0.125
- w_down: bfloat16 [2, 8192, 2048], P('section', 'fsdp'), may hold values from -0.0625 to 0.0625
Outputs:
- boundary: float32 [2, 2, 4, 1024, 2048], P('section', None, 'dp', 'fsdp')
- grad_attn_gain: float32 [2, 2048], P('section', 'fsdp')
- grad_query: float32 [2, 2048, 2048], P('section', 'fsdp')
- grad_key: float32 [2, 2048, 512], P('section', 'fsdp')
- grad_value: float32 [2, 2048, 512], P('section', 'fsdp')
- grad_out: float32 [2, 2048, 2048], P('section', 'fsdp')
- grad_mlp_gain: float32 [2, 2048], P('section', 'fsdp')
- grad_gate: float32 [2, 2048, 8192], P('section', 'fsdp')
- grad_up: float32 [2, 2048, 8192], P('section', 'fsdp')
- grad_down: float32 [2, 8192, 2048], P('section', 'fsdp')
Inputs may be any that keep to these rules, and one draw needn't show every extreme that they name: Within a sequence, positions rise by 1 to 3 from one token to the next; a sequence's first position lies from 0 to 1024.
All inputs are finite; a program needn't handle non-finite values.
Results may differ from a plain program's by a relative error of at most 0.024.
Values may be sent and summed in bfloat16 or wider, within the bound.
No kernel may reach another device: no remote copies, remote signals or barrier semaphores. Data moves between devices by JAX's collectives and lax.ppermute only.
A program may use at most 576 MiB of HBM per device.

v0:
```python
import jax
import jax.numpy as jnp
from jax import lax
from jax.sharding import PartitionSpec as P

HEAD_DIM = 64


EPSILON = 1e-05
ROPE_THETA = 500000.0


def shifted(x, axis, by):
    peers = lax.axis_size(axis)
    pairs = [(i, i + by) for i in range(peers) if 0 <= i + by < peers]
    return lax.ppermute(x, axis, pairs)


def dot_plain(left, right):
    return jnp.dot(left, right, preferred_element_type=jnp.float32)


def dot_rows(left, right):
    return lax.dot_general(
        left, right, (((0,), (0,)), ((), ())), preferred_element_type=jnp.float32
    )


def dot_cols(left, right):
    return lax.dot_general(
        left, right, (((1,), (1,)), ((), ())), preferred_element_type=jnp.float32
    )


def rms_inverse(vector):
    return lax.rsqrt(jnp.mean(vector * vector, axis=-1, keepdims=True) + EPSILON)


def rope_tables(places):
    half_dim = HEAD_DIM // 2
    frequency = jnp.exp(
        -jnp.log(ROPE_THETA) * 2.0 * jnp.arange(half_dim, dtype=jnp.float32) / HEAD_DIM
    )
    angles = places.astype(jnp.float32)[:, None] * frequency[None, :]
    return (jnp.cos(angles)[:, None, :], jnp.sin(angles)[:, None, :])


def rotate(heads, cosine_table, sine_table):
    half_dim = heads.shape[-1] // 2
    first = heads[..., :half_dim]
    second = heads[..., half_dim:]
    return jnp.concatenate(
        [first * cosine_table - second * sine_table, second * cosine_table + first * sine_table],
        axis=-1,
    )


def pick(flag, first, second):
    return jax.tree.map(lambda left, right: jnp.where(flag, left, right), first, second)


def body(
    ends, positions, attn_gain, w_query, w_key, w_value, w_out, mlp_gain, w_gate, w_up, w_down
):
    gathered = (
        lax.all_gather(attn_gain, "fsdp", axis=1, tiled=True),
        lax.all_gather(w_query, "fsdp", axis=1, tiled=True),
        lax.all_gather(w_key, "fsdp", axis=1, tiled=True),
        lax.all_gather(w_value, "fsdp", axis=1, tiled=True),
        lax.all_gather(w_out, "fsdp", axis=1, tiled=True),
        lax.all_gather(mlp_gain, "fsdp", axis=1, tiled=True),
        lax.all_gather(w_gate, "fsdp", axis=1, tiled=True),
        lax.all_gather(w_up, "fsdp", axis=1, tiled=True),
        lax.all_gather(w_down, "fsdp", axis=1, tiled=True),
    )
    gain_attn = gathered[0][0].astype(jnp.float32)
    mat_query = gathered[1][0]
    mat_key = gathered[2][0]
    mat_value = gathered[3][0]
    mat_out = gathered[4][0]
    gain_mlp = gathered[5][0].astype(jnp.float32)
    mat_gate = gathered[6][0]
    mat_up = gathered[7][0]
    mat_down = gathered[8][0]
    section_index = lax.axis_index("section")
    first_section = section_index == 0
    shard_index = lax.axis_index("fsdp")
    micro_count = ends.shape[1]
    tok_rows = ends.shape[3]
    model_width = ends.shape[4]
    length = tok_rows * lax.axis_size("fsdp")
    key_width = mat_key.shape[1]
    query_width = mat_query.shape[1]
    hidden_width = mat_gate.shape[1]
    key_heads = key_width // HEAD_DIM
    query_heads = query_width // HEAD_DIM
    group_size = query_heads // key_heads
    score_scale = HEAD_DIM ** (-0.5)
    ends_local = ends[0, :, 0]
    places_local = positions[:, 0]
    query_index = shard_index * tok_rows + jnp.arange(tok_rows, dtype=jnp.int32)
    causal = query_index[:, None] >= jnp.arange(length, dtype=jnp.int32)[None, :]

    def split_heads(queries, keys_all, values_all):
        return (
            queries.reshape(tok_rows, key_heads, group_size, HEAD_DIM).transpose(1, 0, 2, 3),
            keys_all.reshape(length, key_heads, HEAD_DIM).transpose(1, 0, 2),
            values_all.reshape(length, key_heads, HEAD_DIM).transpose(1, 0, 2),
        )

    def masked_scores(query_block, key_block):
        scores = (
            jnp.einsum("rgd,sd->grs", query_block, key_block, preferred_element_type=jnp.float32)
            * score_scale
        )
        return jnp.where(causal[None], scores, -1e30)

    def attend_group(packed):
        query_block, key_block, value_block = packed
        scores = masked_scores(query_block, key_block)
        row_max = jnp.max(scores, axis=-1, keepdims=True)
        exp_scores = jnp.exp(scores - row_max)
        row_total = jnp.sum(exp_scores, axis=-1, keepdims=True)
        attn_probs = (exp_scores / row_total).astype(jnp.bfloat16)
        attended = jnp.einsum(
            "grs,sd->rgd", attn_probs, value_block, preferred_element_type=jnp.float32
        )
        return (attended, (row_max + jnp.log(row_total))[..., 0])

    def attend_back(packed):
        query_block, key_block, value_block, log_block, grad_block = packed
        scores = masked_scores(query_block, key_block)
        attn_probs = jnp.exp(scores - log_block[..., None])
        grad_value = jnp.einsum(
            "grs,rgd->sd",
            attn_probs.astype(jnp.bfloat16),
            grad_block,
            preferred_element_type=jnp.float32,
        )
        grad_probs = jnp.einsum(
            "rgd,sd->grs", grad_block, value_block, preferred_element_type=jnp.float32
        )
        row_delta = jnp.sum(attn_probs * grad_probs, axis=-1, keepdims=True)
        grad_scores = (attn_probs * (grad_probs - row_delta)).astype(jnp.bfloat16)
        grad_query = (
            jnp.einsum("grs,sd->rgd", grad_scores, key_block, preferred_element_type=jnp.float32)
            * score_scale
        )
        grad_key = (
            jnp.einsum("grs,rgd->sd", grad_scores, query_block, preferred_element_type=jnp.float32)
            * score_scale
        )
        return (grad_query, grad_key, grad_value)

    def backward_upper(operand):
        grad_top, saved_state = operand
        (
            residual_in,
            inverse_one,
            normed_attn,
            queries,
            keys_all,
            values_all,
            log_totals,
            attended,
            residual_mid,
            inverse_two,
            normed_mlp,
            gate_pre,
            up_proj,
            hidden_act,
        ) = saved_state
        branch_grad = grad_top.astype(jnp.bfloat16)
        grad_hidden = dot_cols(branch_grad, mat_down)
        sigmoid_gate = jax.nn.sigmoid(gate_pre)
        grad_gate_pre = (
            grad_hidden * up_proj * sigmoid_gate * (1.0 + gate_pre * (1.0 - sigmoid_gate))
        ).astype(jnp.bfloat16)
        grad_up_proj = (grad_hidden * gate_pre * sigmoid_gate).astype(jnp.bfloat16)
        grad_normed = dot_cols(grad_gate_pre, mat_gate) + dot_cols(grad_up_proj, mat_up)
        base_mid = residual_mid * inverse_two
        part_gain_mlp = jnp.sum(grad_normed * base_mid, axis=0)
        scaled_grad = grad_normed * gain_mlp
        grad_mid = grad_top + inverse_two * (
            scaled_grad - base_mid * jnp.mean(scaled_grad * base_mid, axis=-1, keepdims=True)
        )
        attn_grad = grad_mid.astype(jnp.bfloat16)
        grad_attended = dot_cols(attn_grad, mat_out).astype(jnp.bfloat16)
        query_blocks, key_blocks, value_blocks = split_heads(queries, keys_all, values_all)
        grad_blocks = grad_attended.reshape(tok_rows, key_heads, group_size, HEAD_DIM).transpose(
            1, 0, 2, 3
        )
        grad_queries, grad_keys, grad_values = lax.map(
            attend_back, (query_blocks, key_blocks, value_blocks, log_totals, grad_blocks)
        )
        grad_queries = grad_queries.transpose(1, 0, 2, 3).reshape(tok_rows, query_width)
        grad_keys = grad_keys.transpose(1, 0, 2).reshape(length, key_width)
        grad_values = grad_values.transpose(1, 0, 2).reshape(length, key_width)
        return (
            grad_mid,
            grad_queries,
            grad_keys,
            grad_values,
            part_gain_mlp,
            branch_grad,
            grad_gate_pre,
            grad_up_proj,
            attn_grad,
        )

    def skip_upper(operand):
        return (
            jnp.zeros((tok_rows, model_width), jnp.float32),
            jnp.zeros((tok_rows, query_width), jnp.float32),
            jnp.zeros((length, key_width), jnp.float32),
            jnp.zeros((length, key_width), jnp.float32),
            jnp.zeros((model_width,), jnp.float32),
            jnp.zeros((tok_rows, model_width), jnp.bfloat16),
            jnp.zeros((tok_rows, hidden_width), jnp.bfloat16),
            jnp.zeros((tok_rows, hidden_width), jnp.bfloat16),
            jnp.zeros((tok_rows, model_width), jnp.bfloat16),
        )

    def backward_lower(operand):
        grad_mid, grad_queries, grad_keys, grad_values, saved_state, places = operand
        residual_in = saved_state[0]
        inverse_one = saved_state[1]
        cosine_table, sine_table = rope_tables(places)
        grad_queries = rotate(
            grad_queries.reshape(tok_rows, query_heads, HEAD_DIM), cosine_table, -sine_table
        )
        grad_queries = grad_queries.astype(jnp.bfloat16).reshape(tok_rows, query_width)
        grad_keys = rotate(
            grad_keys.reshape(tok_rows, key_heads, HEAD_DIM), cosine_table, -sine_table
        )
        grad_keys = grad_keys.astype(jnp.bfloat16).reshape(tok_rows, key_width)
        grad_values = grad_values.astype(jnp.bfloat16)
        grad_normed = (
            dot_cols(grad_queries, mat_query)
            + dot_cols(grad_keys, mat_key)
            + dot_cols(grad_values, mat_value)
        )
        base_in = residual_in * inverse_one
        part_gain_attn = jnp.sum(grad_normed * base_in, axis=0)
        scaled_grad = grad_normed * gain_attn
        grad_in = grad_mid + inverse_one * (
            scaled_grad - base_in * jnp.mean(scaled_grad * base_in, axis=-1, keepdims=True)
        )
        return (grad_in, part_gain_attn, grad_queries, grad_keys, grad_values)

    def skip_lower(operand):
        return (
            jnp.zeros((tok_rows, model_width), jnp.float32),
            jnp.zeros((model_width,), jnp.float32),
            jnp.zeros((tok_rows, query_width), jnp.bfloat16),
            jnp.zeros((tok_rows, key_width), jnp.bfloat16),
            jnp.zeros((tok_rows, key_width), jnp.bfloat16),
        )

    received = None
    tick_saved = []
    top_outputs = []
    for step_index in range(micro_count + 1):
        own_input = ends_local[min(step_index, micro_count - 1)].astype(jnp.float32)
        if step_index == 0:
            layer_input = own_input
        else:
            layer_input = jnp.where(first_section, own_input, received.astype(jnp.float32))
        places = jnp.where(
            first_section,
            places_local[min(step_index, micro_count - 1)],
            places_local[max(step_index - 1, 0)],
        )
        layer_inverse_one = rms_inverse(layer_input)
        layer_normed_attn = (layer_input * layer_inverse_one * gain_attn).astype(jnp.bfloat16)
        layer_cosine_table, layer_sine_table = rope_tables(places)
        layer_queries = rotate(
            dot_plain(layer_normed_attn, mat_query).reshape(tok_rows, query_heads, HEAD_DIM),
            layer_cosine_table,
            layer_sine_table,
        )
        layer_queries = layer_queries.astype(jnp.bfloat16).reshape(tok_rows, query_width)
        keys_local = rotate(
            dot_plain(layer_normed_attn, mat_key).reshape(tok_rows, key_heads, HEAD_DIM),
            layer_cosine_table,
            layer_sine_table,
        )
        keys_local = keys_local.astype(jnp.bfloat16).reshape(tok_rows, key_width)
        values_local = dot_plain(layer_normed_attn, mat_value).astype(jnp.bfloat16)
        layer_keys_all = lax.all_gather(keys_local, "fsdp", axis=0, tiled=True)
        layer_values_all = lax.all_gather(values_local, "fsdp", axis=0, tiled=True)
        group_out, layer_log_totals = lax.map(
            attend_group, split_heads(layer_queries, layer_keys_all, layer_values_all)
        )
        layer_attended = (
            group_out.transpose(1, 0, 2, 3).reshape(tok_rows, query_width).astype(jnp.bfloat16)
        )
        layer_residual_mid = layer_input + dot_plain(layer_attended, mat_out)
        layer_inverse_two = rms_inverse(layer_residual_mid)
        layer_normed_mlp = (layer_residual_mid * layer_inverse_two * gain_mlp).astype(jnp.bfloat16)
        layer_gate_pre = dot_plain(layer_normed_mlp, mat_gate)
        layer_up_proj = dot_plain(layer_normed_mlp, mat_up)
        layer_hidden_act = (jax.nn.silu(layer_gate_pre) * layer_up_proj).astype(jnp.bfloat16)
        output = layer_residual_mid + dot_plain(layer_hidden_act, mat_down)
        layer_saved_state = (
            layer_input,
            layer_inverse_one,
            layer_normed_attn,
            layer_queries,
            layer_keys_all,
            layer_values_all,
            layer_log_totals,
            layer_attended,
            layer_residual_mid,
            layer_inverse_two,
            layer_normed_mlp,
            layer_gate_pre,
            layer_up_proj,
            layer_hidden_act,
        )
        output, saved_state = (output, layer_saved_state)
        tick_saved.append((saved_state, places))
        top_outputs.append(output)
        if step_index < micro_count:
            received = shifted(output.astype(jnp.bfloat16), "section", 1)
    micro_saved = [
        pick(first_section, tick_saved[slot_index], tick_saved[slot_index + 1])
        for slot_index in range(micro_count)
    ]
    sum_gain_attn = jnp.zeros((model_width,), jnp.float32)
    sum_gain_mlp = jnp.zeros((model_width,), jnp.float32)
    grad_received = None
    input_grads = []
    tick_operands = []
    for step_index in range(micro_count + 1):
        micro_index = step_index - 1 + section_index
        live_tick = (micro_index >= 0) & (micro_index < micro_count)
        lower_pick = max(step_index - 1, 0)
        upper_pick = min(step_index, micro_count - 1)
        saved_state, places = pick(first_section, micro_saved[lower_pick], micro_saved[upper_pick])
        own_grad = ends_local[upper_pick].astype(jnp.float32)
        if step_index == 0:
            grad_top = own_grad
        else:
            grad_top = jnp.where(first_section, grad_received.astype(jnp.float32), own_grad)
        upper_out = lax.cond(live_tick, backward_upper, skip_upper, (grad_top, saved_state))
        grad_mid, grad_queries, grad_keys_all, grad_values_all, part_gain_mlp = upper_out[:5]
        grad_keys, grad_values = (
            lax.psum_scatter(
                grad_keys_all.astype(jnp.bfloat16), "fsdp", scatter_dimension=0, tiled=True
            ).astype(jnp.float32),
            lax.psum_scatter(
                grad_values_all.astype(jnp.bfloat16), "fsdp", scatter_dimension=0, tiled=True
            ).astype(jnp.float32),
        )
        lower_out = lax.cond(
            live_tick,
            backward_lower,
            skip_lower,
            (grad_mid, grad_queries, grad_keys, grad_values, saved_state, places),
        )
        grad_in, part_gain_attn = (lower_out[0], lower_out[1])
        sum_gain_attn = sum_gain_attn + part_gain_attn
        sum_gain_mlp = sum_gain_mlp + part_gain_mlp
        tick_operands.append(
            (
                upper_out[5],
                upper_out[6],
                upper_out[7],
                upper_out[8],
                lower_out[2],
                lower_out[3],
                lower_out[4],
            )
        )
        input_grads.append(grad_in)
        if step_index < micro_count:
            grad_received = shifted(grad_in.astype(jnp.bfloat16), "section", -1)
    live_operands = [
        pick(first_section, tick_operands[slot_index + 1], tick_operands[slot_index])
        for slot_index in range(micro_count)
    ]

    def joined(values):
        return jnp.concatenate(values, axis=0)

    normed_attn_all = joined([micro_saved[slot_index][0][2] for slot_index in range(micro_count)])
    attended_all = joined([micro_saved[slot_index][0][7] for slot_index in range(micro_count)])
    normed_mlp_all = joined([micro_saved[slot_index][0][10] for slot_index in range(micro_count)])
    hidden_all = joined([micro_saved[slot_index][0][13] for slot_index in range(micro_count)])
    branch_all, gate_all, up_all, attn_all, query_all, key_all, value_all = [
        joined([operands[member] for operands in live_operands]) for member in range(7)
    ]
    sum_down = dot_rows(hidden_all, branch_all)
    sum_gate = dot_rows(normed_mlp_all, gate_all)
    sum_up = dot_rows(normed_mlp_all, up_all)
    sum_out = dot_rows(attended_all, attn_all)
    sum_query = dot_rows(normed_attn_all, query_all)
    sum_key = dot_rows(normed_attn_all, key_all)
    sum_value = dot_rows(normed_attn_all, value_all)
    boundary = jnp.stack(
        [
            jnp.where(first_section, input_grads[slot_index + 1], top_outputs[slot_index + 1])
            for slot_index in range(micro_count)
        ]
    )
    boundary = boundary[None, :, None]
    pieces = (
        lax.psum_scatter(sum_gain_attn, ("fsdp", "dp"), scatter_dimension=0, tiled=True),
        lax.psum_scatter(sum_query, ("fsdp", "dp"), scatter_dimension=0, tiled=True),
        lax.psum_scatter(sum_key, ("fsdp", "dp"), scatter_dimension=0, tiled=True),
        lax.psum_scatter(sum_value, ("fsdp", "dp"), scatter_dimension=0, tiled=True),
        lax.psum_scatter(sum_out, ("fsdp", "dp"), scatter_dimension=0, tiled=True),
        lax.psum_scatter(sum_gain_mlp, ("fsdp", "dp"), scatter_dimension=0, tiled=True),
        lax.psum_scatter(sum_gate, ("fsdp", "dp"), scatter_dimension=0, tiled=True),
        lax.psum_scatter(sum_up, ("fsdp", "dp"), scatter_dimension=0, tiled=True),
        lax.psum_scatter(sum_down, ("fsdp", "dp"), scatter_dimension=0, tiled=True),
    )
    owned = (
        lax.all_gather(pieces[0].astype(jnp.bfloat16), "dp", axis=0, tiled=True).astype(
            jnp.float32
        ),
        lax.all_gather(pieces[1].astype(jnp.bfloat16), "dp", axis=0, tiled=True).astype(
            jnp.float32
        ),
        lax.all_gather(pieces[2].astype(jnp.bfloat16), "dp", axis=0, tiled=True).astype(
            jnp.float32
        ),
        lax.all_gather(pieces[3].astype(jnp.bfloat16), "dp", axis=0, tiled=True).astype(
            jnp.float32
        ),
        lax.all_gather(pieces[4].astype(jnp.bfloat16), "dp", axis=0, tiled=True).astype(
            jnp.float32
        ),
        lax.all_gather(pieces[5].astype(jnp.bfloat16), "dp", axis=0, tiled=True).astype(
            jnp.float32
        ),
        lax.all_gather(pieces[6].astype(jnp.bfloat16), "dp", axis=0, tiled=True).astype(
            jnp.float32
        ),
        lax.all_gather(pieces[7].astype(jnp.bfloat16), "dp", axis=0, tiled=True).astype(
            jnp.float32
        ),
        lax.all_gather(pieces[8].astype(jnp.bfloat16), "dp", axis=0, tiled=True).astype(
            jnp.float32
        ),
    )
    return (
        boundary,
        owned[0][None],
        owned[1][None],
        owned[2][None],
        owned[3][None],
        owned[4][None],
        owned[5][None],
        owned[6][None],
        owned[7][None],
        owned[8][None],
    )


def solution(mesh):
    return jax.shard_map(
        body,
        mesh=mesh,
        in_specs=(
            P("section", None, "dp", "fsdp", None),
            P(None, "dp", "fsdp"),
            P("section", "fsdp"),
            P("section", "fsdp", None),
            P("section", "fsdp", None),
            P("section", "fsdp", None),
            P("section", "fsdp", None),
            P("section", "fsdp"),
            P("section", "fsdp", None),
            P("section", "fsdp", None),
            P("section", "fsdp", None),
        ),
        out_specs=(
            P("section", None, "dp", "fsdp", None),
            P("section", "fsdp"),
            P("section", "fsdp", None),
            P("section", "fsdp", None),
            P("section", "fsdp", None),
            P("section", "fsdp", None),
            P("section", "fsdp"),
            P("section", "fsdp", None),
            P("section", "fsdp", None),
            P("section", "fsdp", None),
        ),
        check_vma=False,
    )
```

profile of v0, /device:TPU:0, one launch (start us, length us, event | category | flops | bytes accessed | tf_op | source)
XLA Modules:
  0.0 5007.5 jit_solution(17366620203407889579)
XLA Ops:
  17.2 17.7 all-gather.21.cloned.1.call-done
  40.2 18.9 all-gather.25.cloned.1.call-done
  80.6 16.2 all-gather.27.cloned.1.call-done
  99.0 57.5 %all-gather.29.cloned.1.call-done = bf16[1,2048,2048]{2,1,0:T(8,128)(2,1)} async-done(((bf16[1,512,2048]{2,1,0:T(8,128)(2,1)}), bf16[1,2048,2048]{2,1,0:T(8,128)(2,1)}) %all-gather.29.cloned.1.call-update) | async-done | bytes 8388624 | tf_op jit(solution)/shard_map/all_gather | solution.py:67
  156.5 12.4 copy.154
  177.0 40.8 while.81
  225.3 194.1 %all-gather.33.cloned.1.call-done = bf16[1,2048,8192]{2,1,0:T(8,128)(2,1)} async-done(((bf16[1,512,8192]{2,1,0:T(8,128)(2,1)}), bf16[1,2048,8192]{2,1,0:T(8,128)(2,1)}) %all-gather.33.cloned.1.call-update) | async-done | bytes 33554448 | tf_op jit(solution)/shard_map/all_gather | solution.py:72
  419.4 23.3 fusion.270
  442.7 179.8 %all-gather.35.cloned.1.call-done = bf16[1,2048,8192]{2,1,0:T(8,128)(2,1)} async-done(((bf16[1,512,8192]{2,1,0:T(8,128)(2,1)}), bf16[1,2048,8192]{2,1,0:T(8,128)(2,1)}) %all-gather.35.cloned.1.call-update) | async-done | bytes 33554448 | tf_op jit(solution)/shard_map/all_gather | solution.py:73
  622.5 29.4 multiply_convert_fusion.8
  651.9 173.7 %all-gather.37.cloned.1.call-done = bf16[1,8192,2048]{2,1,0:T(8,128)(2,1)} async-done(((bf16[1,2048,2048]{2,1,0:T(8,128)(2,1)}), bf16[1,8192,2048]{2,1,0:T(8,128)(2,1)}) %all-gather.37.cloned.1.call-update) | async-done | bytes 33554448 | tf_op jit(solution)/shard_map/all_gather | solution.py:74
  825.6 16.9 fusion.201
  846.2 22.8 collective-permute-done
  893.9 16.6 all-gather.39.cloned.1.call-done
  913.9 45.9 while.82
  967.9 17.4 fusion.268
  985.3 27.9 broadcast_select_fusion.3
  1013.2 17.2 fusion.287
  1033.4 22.7 collective-permute-done.1
  1083.9 15.9 all-gather.43.cloned.1.call-done
  1102.2 40.8 while.83
  1158.8 28.3 broadcast_select_fusion.8
  1187.1 28.3 broadcast_select_fusion.9
  1215.4 22.9 conditional.6
  1240.9 154.3 %reduce-scatter.14.cloned.1.call-done = bf16[256,512]{0,1:T(8,128)(2,1)} async-done(((bf16[1024,512]{0,1:T(8,128)(2,1)}), bf16[256,512]{0,1:T(8,128)(2,1)}) %reduce-scatter.14.cloned.1.call-update) | async-done | bytes 262160 | tf_op jit(solution)/shard_map/reduce_scatter | solution.py:349
  1396.3 26.5 reduce-scatter.16.cloned.1.call-done
  1428.4 42.2 collective-permute-done.2
  1477.2 203.3 %conditional.8 = (f32[256,2048]{1,0:T(8,128)}, f32[256,2048]{0,1:T(8,128)}, bf16[1024,512]{0,1:T(8,128)(2,1)}, bf16[1024,512]{0,1:T(8,128)(2,1)}, f32[2048]{0:T(...) conditional(s32[]{:T(128)} %convert_element_type.383, () %tuple.83, ...), branch_computations={%region_31.32_spmd, %region_32.38_spmd} | conditional | flops 28646182912 | bytes 267946592 | solution.py:346
  1506.6 28.7 multiply_convert_fusion.2
  1535.3 16.9 fusion.293
  1552.3 17.7 multiply_reduce_fusion.4
  1581.6 98.9 %while.79 = (s32[]{:T(128)}, f32[8,256,4,64]{1,3,2,0:T(8,128)}, bf16[8,1024,64]{1,2,0:T(8,128)(2,1)}, bf16[8,1024,64]{1,2,0:T(8,128)(2,1)}, bf16[8,1024,64]{1,2,...) while((s32[]{:T(128)}, f32[8,256,4,64]{1,3,2,0:T(8,128)}, ...), condition=%wide.region_36.36_spmd, body=%wide.region_34.35_spmd.sunk | while | flops 686947328 | bytes 33981560 | solution.py:193
  1683.1 21.5 reduce-scatter.18.cloned.1.call-done
  1706.4 26.2 reduce-scatter.20.cloned.1.call-done
  1732.7 21.7 conditional.9
  1761.6 25.8 collective-permute-done.3
  1790.2 154.8 %conditional.10 = (f32[256,2048]{1,0:T(8,128)}, f32[256,2048]{0,1:T(8,128)}, bf16[1024,512]{0,1:T(8,128)(2,1)}, bf16[1024,512]{0,1:T(8,128)(2,1)}, f32[2048]{0:T...) conditional(s32[]{:T(128)} %convert_element_type.433, () %tuple.92, ...), branch_computations={%region_44.45_spmd, %region_45.51_spmd} | conditional | flops 28640407552 | bytes 219610464 | solution.py:346
  1793.1 22.5 multiply_convert_fusion.4
  1815.5 16.9 fusion.292
  1832.4 18.7 multiply_reduce_fusion.8
  1867.8 76.8 %while.80 = (s32[]{:T(128)}, f32[8,256,4,64]{1,3,2,0:T(8,128)}, bf16[8,1024,64]{1,2,0:T(8,128)(2,1)}, bf16[8,1024,64]{1,2,0:T(8,128)(2,1)}, bf16[8,1024,64]{1,2,...) while((s32[]{:T(128)}, f32[8,256,4,64]{1,3,2,0:T(8,128)}, ...), condition=%wide.region_49.49_spmd, body=%wide.region_47.48_spmd.sunk | while | flops 686947328 | bytes 33981560 | solution.py:193
  1970.2 27.2 reduce-scatter.24.cloned.1.call-done
  1997.4 20.9 conditional.11
  2043.1 29.7 fusion.195
  2072.8 12.8 broadcast_select_fusion.5
  2085.7 29.5 fusion.191
  2115.5 29.9 fusion.187
  2154.0 26.5 reduce-scatter.32.cloned.1.call-done
  2182.7 180.2 %reduce-scatter.26.cloned.1.call-done = f32[128,2048]{1,0:T(8,128)} async-done(((f32[2048,2048]{1,0:T(8,128)}), f32[128,2048]{1,0:T(8,128)}) %reduce-scatter.26.cloned.1.call-update) | async-done | bytes 1048592 | tf_op jit(solution)/shard_map/reduce_scatter | solution.py:410
  2365.0 638.1 %reduce-scatter.38.cloned.1.call-done = f32[512,2048]{1,0:T(8,128)} async-done(((f32[8192,2048]{1,0:T(8,128)}), f32[512,2048]{1,0:T(8,128)}) %reduce-scatter.38.cloned.1.call-update) | async-done | bytes 4194320 | tf_op jit(solution)/shard_map/reduce_scatter | solution.py:417
  3007.0 635.9 %reduce-scatter.36.cloned.1.call-done = f32[128,8192]{1,0:T(8,128)} async-done(((f32[2048,8192]{1,0:T(8,128)}), f32[128,8192]{1,0:T(8,128)}) %reduce-scatter.36.cloned.1.call-update) | async-done | bytes 4194320 | tf_op jit(solution)/shard_map/reduce_scatter | solution.py:416
  3646.8 635.9 %reduce-scatter.34.cloned.1.call-done = f32[128,8192]{1,0:T(8,128)} async-done(((f32[2048,8192]{1,0:T(8,128)}), f32[128,8192]{1,0:T(8,128)}) %reduce-scatter.34.cloned.1.call-update) | async-done | bytes 4194320 | tf_op jit(solution)/shard_map/reduce_scatter | solution.py:415
  4289.1 60.6 %all-reduce.2 = (bf16[2048]{0:T(1024)(128)(2,1)S(1)}, bf16[2048]{0:T(1024)(128)(2,1)S(1)}) all-reduce(f32[2048]{0:T(1024)S(1)} %add_add_fusion.1, f32[2048]{0:T(1024)S(1)} %add_add_fusion), channel_id=8, replica_groups=mesh['section'=2,'fsdp'=4,'dp'=4] {'fsdp','dp'}, use_global_device_ids=true, to_apply=%region_57.58.clone | all-reduce | flops 4096 | bytes 24576
  4368.3 20.2 fusion.200
  4393.4 41.8 reduce-scatter.28.cloned.1.call-done
  4436.2 18.7 all_gather.90
  4454.9 21.0 all_gather.89
  4478.1 14.2 all-gather.49.cloned.1.call-done
  4496.4 42.3 all-gather.47.cloned.1.call-done
  4542.8 145.8 %all-gather.55.cloned.1.call-done = bf16[2048,2048]{1,0:T(8,128)(2,1)} async-done(((bf16[512,2048]{1,0:T(8,128)(2,1)}), bf16[2048,2048]{1,0:T(8,128)(2,1)}) %all-gather.55.cloned.1.call-update) | async-done | bytes 8388624 | tf_op jit(solution)/shard_map/all_gather | solution.py:444
  4688.7 13.1 bitcast_convert_fusion
  4701.7 136.8 %all-gather.53.cloned.1.call-done = bf16[512,8192]{1,0:T(8,128)(2,1)} async-done(((bf16[128,8192]{1,0:T(8,128)(2,1)}), bf16[512,8192]{1,0:T(8,128)(2,1)}) %all-gather.53.cloned.1.call-update) | async-done | bytes 8388624 | tf_op jit(solution)/shard_map/all_gather | solution.py:441
  4838.6 13.1 bitcast_convert_fusion.1
  4851.7 136.9 %all-gather.51.cloned.1.call-done = bf16[512,8192]{1,0:T(8,128)(2,1)} async-done(((bf16[128,8192]{1,0:T(8,128)(2,1)}), bf16[512,8192]{1,0:T(8,128)(2,1)}) %all-gather.51.cloned.1.call-update) | async-done | bytes 8388624 | tf_op jit(solution)/shard_map/all_gather | solution.py:438
  (685 shorter events, 718.6 us)
Async XLA Ops:
  7.2 31.3 copy-start.101
  7.2 27.7 all-gather.21.cloned.1.call-start
  7.9 51.2 %all-gather.25.cloned.1.call-start = ((), (), s32[]{:S(2)}) async-start(), calls=%async_computation.15 | async-start | bytes 2621440 | tf_op jit(solution)/shard_map/all_gather | solution.py:68
  8.7 69.4 %all-gather.23.cloned.1.call-start = ((), (), s32[]{:S(2)}) async-start(), calls=%async_computation.14 | async-start | bytes 1310720 | tf_op jit(solution)/shard_map/all_gather | solution.py:291
  15.0 1044.8 %copy-start.73 = (f32[1,2048]{1,0:T(1,128)}, f32[1,2048]{1,0:T(1,128)S(1)}, u32[]{:S(2)}) copy-start(f32[1,2048]{1,0:T(1,128)S(1)} %mul.1058) | copy-start | bytes 24580
  38.5 58.3 %all-gather.27.cloned.1.call-start = ((), (), s32[]{:S(2)}) async-start(), calls=%async_computation.16 | async-start | bytes 1310720 | tf_op jit(solution)/shard_map/all_gather | solution.py:290
  66.4 90.1 %all-gather.29.cloned.1.call-start = ((), (), s32[]{:S(2)}) async-start(), calls=%async_computation.17 | async-start | bytes 10485760 | tf_op jit(solution)/shard_map/all_gather | solution.py:67
  67.0 150.8 %all-gather.31.cloned.1.call-start = ((), (), s32[]{:S(2)}) async-start(), calls=%async_computation.18 | async-start | bytes 10485760 | tf_op jit(solution)/shard_map/all_gather | solution.py:70
  67.6 351.8 %all-gather.33.cloned.1.call-start = ((), (), s32[]{:S(2)}) async-start(), calls=%async_computation.19 | async-start | bytes 41943040 | tf_op jit(solution)/shard_map/all_gather | solution.py:72
  68.3 554.2 %all-gather.35.cloned.1.call-start = ((), (), s32[]{:S(2)}) async-start(), calls=%async_computation.20 | async-start | bytes 41943040 | tf_op jit(solution)/shard_map/all_gather | solution.py:73
  69.1 756.6 %all-gather.37.cloned.1.call-start = ((), (), s32[]{:S(2)}) async-start(), calls=%async_computation.21 | async-start | bytes 41943040 | tf_op jit(solution)/shard_map/all_gather | solution.py:74
  69.8 821.8 %all-gather.41.cloned.1.call-start = ((), (), s32[]{:S(2)}) async-start(), calls=%async_computation.23 | async-start | bytes 1310720 | tf_op jit(solution)/shard_map/all_gather | solution.py:290
  225.3 217.4 %copy-start.94 = (f32[256]{0:T(256)}, f32[256]{0:T(256)S(1)}, u32[]{:S(2)}) copy-start(f32[256]{0:T(256)S(1)} %get-tuple-element.1369) | copy-start | bytes 3076
  842.6 29.5 copy-start.62
  842.6 26.3 collective-permute-start
  873.8 36.8 all-gather.39.cloned.1.call-start
  877.2 204.3 %all-gather.45.cloned.1.call-start = ((), (), s32[]{:S(2)}) async-start(), calls=%async_computation.27 | async-start | bytes 1310720 | tf_op jit(solution)/shard_map/all_gather | solution.py:290
  966.2 47.0 copy-start.10
  1030.4 28.8 copy-start.93
  1030.4 29.4 copy-start.44
  1030.4 25.7 collective-permute-start.1
  1063.5 36.3 all-gather.43.cloned.1.call-start
  1067.5 327.7 %reduce-scatter.14.cloned.1.call-start = ((), (), s32[]{:S(2)}) async-start(), calls=%async_computation.24 | async-start | bytes 1310720 | tf_op jit(solution)/shard_map/reduce_scatter | solution.py:349
  1238.3 184.4 %copy-start.1 = (bf16[1,2048,512]{2,1,0:T(8,128)(2,1)S(1)}, bf16[1,2048,512]{2,1,0:T(8,128)(2,1)}, u32[]{:S(2)}) copy-start(bf16[1,2048,512]{2,1,0:T(8,128)(2,1)} %all-gather.25.cloned.1.call-done) | copy-start | bytes 6291460
  1238.3 184.4 %copy-start.74 = (f32[1,2048]{1,0:T(1,128)S(1)}, f32[1,2048]{1,0:T(1,128)}, u32[]{:S(2)}) copy-start(f32[1,2048]{1,0:T(1,128)} %copy-done.73) | copy-start | bytes 24580
  1238.3 184.4 %copy-start.89 = (f32[256]{0:T(256)S(1)}, f32[256]{0:T(256)}, u32[]{:S(2)}) copy-start(f32[256]{0:T(256)} %get-tuple-element.1364) | copy-start | bytes 3076
  1238.4 184.4 %copy-start.99 = (s32[256]{0:T(256)S(1)}, s32[256]{0:T(256)}, u32[]{:S(2)}) copy-start(s32[256]{0:T(256)} %get-tuple-element.1349) | copy-start | bytes 3076
  1238.4 184.3 %reduce-scatter.16.cloned.1.call-start = ((), (), s32[]{:S(2)}) async-start(), calls=%async_computation.25 | async-start | bytes 1310720 | tf_op jit(solution)/shard_map/reduce_scatter | solution.py:352
  1240.9 463.8 %reduce-scatter.18.cloned.1.call-start = ((), (), s32[]{:S(2)}) async-start(), calls=%async_computation.28 | async-start | bytes 1310720 | tf_op jit(solution)/shard_map/reduce_scatter | solution.py:349
  1427.0 50.1 %copy-start.21 = (bf16[256,32,64]{0,2,1:T(8,128)(2,1)S(1)}, bf16[256,32,64]{0,2,1:T(8,128)(2,1)}, u32[]{:S(2)}) copy-start(bf16[256,32,64]{0,2,1:T(8,128)(2,1)} %get-tuple-element.1334) | copy-start | bytes 3145732
  1427.0 50.1 %copy-start.78 = (f32[4,8,256]{2,1,0:T(8,128)S(1)}, f32[4,8,256]{2,1,0:T(8,128)}, u32[]{:S(2)}) copy-start(f32[4,8,256]{2,1,0:T(8,128)} %get-tuple-element.1438) | copy-start | bytes 98308
  1427.0 50.1 %copy-start.96 = (f32[256]{0:T(256)S(1)}, f32[256]{0:T(256)}, u32[]{:S(2)}) copy-start(f32[256]{0:T(256)} %get-tuple-element.1360) | copy-start | bytes 3076
  1427.0 43.6 collective-permute-start.2
  1680.5 52.2 %copy-start.81 = (f32[2048]{0:T(1024)}, f32[2048]{0:T(1024)S(1)}, u32[]{:S(2)}) copy-start(f32[2048]{0:T(1024)S(1)} %get-tuple-element.685) | copy-start | bytes 24580
  1680.5 52.2 %copy-start.90 = (f32[256]{0:T(256)S(1)}, f32[256]{0:T(256)}, u32[]{:S(2)}) copy-start(f32[256]{0:T(256)} %get-tuple-element.1363) | copy-start | bytes 3076
  1680.5 52.2 %copy-start.97 = (s32[256]{0:T(256)S(1)}, s32[256]{0:T(256)}, u32[]{:S(2)}) copy-start(s32[256]{0:T(256)} %get-tuple-element.1348) | copy-start | bytes 3076
  1680.5 52.1 %reduce-scatter.20.cloned.1.call-start = ((), (), s32[]{:S(2)}) async-start(), calls=%async_computation.29 | async-start | bytes 1310720 | tf_op jit(solution)/shard_map/reduce_scatter | solution.py:352
  1682.9 286.3 %reduce-scatter.22.cloned.1.call-start = ((), (), s32[]{:S(2)}) async-start(), calls=%async_computation.30 | async-start | bytes 1310720 | tf_op jit(solution)/shard_map/reduce_scatter | solution.py:349
  1754.4 35.8 copy-start.85
  1755.7 34.5 copy-start.8
  1760.4 27.1 collective-permute-start.3
  1945.1 52.3 %reduce-scatter.24.cloned.1.call-start = ((), (), s32[]{:S(2)}) async-start(), calls=%async_computation.31 | async-start | bytes 1310720 | tf_op jit(solution)/shard_map/reduce_scatter | solution.py:352
  1947.6 232.9 %reduce-scatter.32.cloned.1.call-start = ((), (), s32[]{:S(2)}) async-start(), calls=%async_computation.36 | async-start | bytes 17825792 | tf_op jit(solution)/shard_map/reduce_scatter | solution.py:413
  1961.8 35.5 copy-start.2
  1961.8 35.5 copy-start.75
  1961.8 35.5 copy-start.91
  1961.9 35.5 copy-start.98
  1961.9 401.0 %reduce-scatter.26.cloned.1.call-start = ((), (), s32[]{:S(2)}) async-start(), calls=%async_computation.32 | async-start | bytes 17825792 | tf_op jit(solution)/shard_map/reduce_scatter | solution.py:410
  2030.9 972.1 %reduce-scatter.38.cloned.1.call-start = ((), (), s32[]{:S(2)}) async-start(), calls=%async_computation.42 | async-start | bytes 71303168 | tf_op jit(solution)/shard_map/reduce_scatter | solution.py:417
  2072.8 1570.1 %reduce-scatter.36.cloned.1.call-start = ((), (), s32[]{:S(2)}) async-start(), calls=%async_computation.40 | async-start | bytes 71303168 | tf_op jit(solution)/shard_map/reduce_scatter | solution.py:416
  2115.2 2167.4 %reduce-scatter.34.cloned.1.call-start = ((), (), s32[]{:S(2)}) async-start(), calls=%async_computation.38 | async-start | bytes 71303168 | tf_op jit(solution)/shard_map/reduce_scatter | solution.py:415
  2145.4 2247.0 %reduce-scatter.30.cloned.1.call-start = ((), (), s32[]{:S(2)}) async-start(), calls=%async_computation.35 | async-start | bytes 4456448 | tf_op jit(solution)/shard_map/reduce_scatter | solution.py:412
  2150.6 2284.7 %reduce-scatter.28.cloned.1.call-start = ((), (), s32[]{:S(2)}) async-start(), calls=%async_computation.34 | async-start | bytes 4456448 | tf_op jit(solution)/shard_map/reduce_scatter | solution.py:411
  2153.9 2338.3 %all-gather.49.cloned.1.call-start = ((), (), s32[]{:S(2)}) async-start(), calls=%async_computation.37 | async-start | bytes 2621440 | tf_op jit(solution)/shard_map/all_gather | solution.py:432
  2182.6 2356.1 %all-gather.47.cloned.1.call-start = ((), (), s32[]{:S(2)}) async-start(), calls=%async_computation.33 | async-start | bytes 2621440 | tf_op jit(solution)/shard_map/all_gather | solution.py:423
  2364.9 2323.7 %all-gather.55.cloned.1.call-start = ((), (), s32[]{:S(2)}) async-start(), calls=%async_computation.43 | async-start | bytes 10485760 | tf_op jit(solution)/shard_map/all_gather | solution.py:444
  3006.9 1831.6 %all-gather.53.cloned.1.call-start = ((), (), s32[]{:S(2)}) async-start(), calls=%async_computation.41 | async-start | bytes 10485760 | tf_op jit(solution)/shard_map/all_gather | solution.py:441
  3646.7 639.8 %copy-start.102 = (u32[32]{0:T(128)S(1)}, u32[32]{0:T(128)}, u32[]{:S(2)}) copy-start(u32[32]{0:T(128)} %constant.283) | copy-start | bytes 388
  3646.7 641.0 %copy-start.82 = (f32[2048]{0:T(1024)S(1)}, f32[2048]{0:T(1024)}, u32[]{:S(2)}) copy-start(f32[2048]{0:T(1024)} %copy-done.81) | copy-start | bytes 24580
  3646.7 641.0 %copy-start.84 = (f32[2048]{0:T(1024)S(1)}, f32[2048]{0:T(1024)}, u32[]{:S(2)}) copy-start(f32[2048]{0:T(1024)} %copy-done.83) | copy-start | bytes 24580
  3646.7 641.7 %copy-start.86 = (f32[2048]{0:T(1024)S(1)}, f32[2048]{0:T(1024)}, u32[]{:S(2)}) copy-start(f32[2048]{0:T(1024)} %copy-done.85) | copy-start | bytes 24580
  3646.7 641.7 %copy-start.88 = (f32[2048]{0:T(1024)S(1)}, f32[2048]{0:T(1024)}, u32[]{:S(2)}) copy-start(f32[2048]{0:T(1024)} %copy-done.87) | copy-start | bytes 24580
  3646.7 721.6 %copy-start.30 = (f32[256,2048]{1,0:T(8,128)S(1)}, f32[256,2048]{1,0:T(8,128)}, u32[]{:S(2)}) copy-start(f32[256,2048]{1,0:T(8,128)} %copy-done.29) | copy-start | bytes 6291460
  3646.7 1341.9 %all-gather.51.cloned.1.call-start = ((), (), s32[]{:S(2)}) async-start(), calls=%async_computation.39 | async-start | bytes 10485760 | tf_op jit(solution)/shard_map/all_gather | solution.py:438
  (66 other events, 375.2 us)
Sparse Core Ops, SparseCore 0:
  9.6 25.2 all-gather.20
  36.5 22.5 all-gather.24
  61.2 16.7 all-gather.22
  80.0 16.7 all-gather.26
  98.2 58.2 all-gather.28
  157.9 58.2 all-gather.30
  217.8 201.5 all-gather.32
  420.9 201.5 all-gather.34
  624.1 201.5 all-gather.36
  873.9 17.7 all-gather.40
  893.8 16.7 all-gather.38
  1063.6 17.7 all-gather.44
  1083.0 16.7 all-gather.42
  1238.5 156.7 reduce-scatter.13
  1397.8 24.8 reduce-scatter.15
  1680.6 23.9 reduce-scatter.17
  1707.7 24.8 reduce-scatter.19
  1945.2 23.9 reduce-scatter.21
  1972.5 24.8 reduce-scatter.23
  2001.9 178.5 reduce-scatter.31
  2185.2 177.6 reduce-scatter.25
  2367.1 635.9 reduce-scatter.37
  3007.3 635.5 reduce-scatter.35
  3647.0 635.6 reduce-scatter.33
  4287.1 71.8 reduce-scatter.29
  4363.7 71.4 reduce-scatter.27
  4436.7 55.5 all-gather.48
  4493.8 44.8 all-gather.46
  4540.3 148.3 all-gather.54
  4690.7 147.8 all-gather.52
  4840.7 147.8 all-gather.50
where the time goes:
time: 5010 us
  waiting for transfers between devices  3720 us (74%)
  matrix products  788 us (16%)
  other arithmetic  228 us (5%)
  blocking collectives  129 us (3%)
  local copies, waits for them, and re-layouts  104 us (2%)
    reduce_scatter x1, waiting for transfers between devices, body(): lax.psum_scatter(sum_down, ('fsdp', 'dp'), scatter_dimension=0, tiled=True)  638 us
    reduce_scatter x1, waiting for transfers between devices, body(): lax.psum_scatter(sum_gate, ('fsdp', 'dp'), scatter_dimension=0, tiled=True)  636 us
    reduce_scatter x1, waiting for transfers between devices, body(): lax.psum_scatter(sum_up, ('fsdp', 'dp'), scatter_dimension=0, tiled=True)  636 us
    dot_general x21, matrix products, dot_plain(): return jnp.dot(left, right, preferred_element_type=jnp.float32)  263 us
    all_gather x1, waiting for transfers between devices, body(): lax.all_gather(w_gate, 'fsdp', axis=1, tiled=True)  194 us
    reduce_scatter x3, waiting for transfers between devices, body(): lax.psum_scatter(grad_keys_all.astype(jnp.bfloat16), 'fsdp', scatter_dime...  183 us
    reduce_scatter x1, waiting for transfers between devices, body(): lax.psum_scatter(sum_query, ('fsdp', 'dp'), scatter_dimension=0, tiled=True)  180 us
    all_gather x1, waiting for transfers between devices, body(): lax.all_gather(w_up, 'fsdp', axis=1, tiled=True)  180 us
  transfers between devices with their start and end apart: 35, of which 33 were waited for; matrix products, arithmetic and copies ran while one was open for 9% of the time, Pallas kernels for 0%

commit v1 on v0

v1 whole, which is shorter than its diff:
```python
import jax
import jax.numpy as jnp
from jax import lax
from jax.sharding import PartitionSpec as P

HEAD_DIM = 64
EPSILON = 1e-05
ROPE_THETA = 500000.0
CHUNK_ROWS = 512
CHUNK_COLS = 1024
STREAMS = 2
BF = jnp.bfloat16
F32 = jnp.float32


def dot_plain(left, right):
    return jnp.dot(left, right, preferred_element_type=F32)


def dot_rows(left, right):
    return lax.dot_general(left, right, (((0,), (0,)), ((), ())), preferred_element_type=F32)


def dot_cols(left, right):
    return lax.dot_general(left, right, (((1,), (1,)), ((), ())), preferred_element_type=F32)


def rms_inverse(vector):
    return lax.rsqrt(jnp.mean(vector * vector, axis=-1, keepdims=True) + EPSILON)


def rope_tables(places):
    half_dim = HEAD_DIM // 2
    frequency = jnp.exp(-jnp.log(ROPE_THETA) * 2.0 * jnp.arange(half_dim, dtype=F32) / HEAD_DIM)
    angles = places.astype(F32)[:, None] * frequency[None, :]
    return (jnp.cos(angles)[:, None, :], jnp.sin(angles)[:, None, :])


def rotate(heads, cosine_table, sine_table):
    half_dim = heads.shape[-1] // 2
    first = heads[..., :half_dim]
    second = heads[..., half_dim:]
    return jnp.concatenate(
        [first * cosine_table - second * sine_table, second * cosine_table + first * sine_table],
        axis=-1,
    )


def core_swap(x):
    return lax.ppermute(x, "fsdp", [(0, 1), (1, 0), (2, 3), (3, 2)])


def chip_swap(x):
    return lax.ppermute(x, "fsdp", [(0, 2), (2, 0), (1, 3), (3, 1)])


def after(value, *others):
    return lax.optimization_barrier((value, *others))[0]


def column_block(x, index, width):
    return lax.dynamic_slice_in_dim(x, index * width, width, axis=1)


def swapped_columns(x, shard):
    width = x.shape[1] // 4
    return jnp.concatenate([column_block(x, shard ^ k, width) for k in range(4)], axis=1)


def replica_chain(chunks):
    peers = lax.axis_size("dp")
    place = lax.axis_index("dp")
    root = (peers - 1) // 2
    delay = max(root, peers - 1 - root)
    up_pairs = [(i, i + 1) for i in range(peers - 1)]
    down_pairs = [(i + 1, i) for i in range(peers - 1)]
    shape = chunks[0].shape
    streams = [chunks[q::STREAMS] for q in range(STREAMS)]
    counts = [len(stream) for stream in streams]
    ups = [[] for _ in streams]
    downs = [[] for _ in streams]
    sent = [[] for _ in streams]
    order = []

    def nth(items, index):
        return items[index].astype(F32) if 0 <= index < len(items) else 0.0

    for step in range(max(counts) + 2 * delay):
        for q in range(STREAMS):
            if step >= counts[q] + 2 * delay:
                continue
            own = 0.0
            for position in range(peers):
                if position < root:
                    index = step - position
                elif position == root:
                    index = step - delay
                else:
                    index = step - (peers - 1 - position)
                if 0 <= index < counts[q]:
                    own = jnp.where(place == position, streams[q][index].astype(F32), own)
            from_below = nth(ups[q], step - 1)
            from_above = nth(downs[q], step - 1)
            below_held = nth(ups[q], step - 1 - (delay - root))
            above_held = nth(downs[q], step - 1 - (delay - (peers - 1 - root)))
            total = own + below_held + above_held
            up = jnp.where(place == root, total, from_below + jnp.where(place < root, own, 0.0))
            down = jnp.where(place == root, total, from_above + jnp.where(place > root, own, 0.0))
            up = jnp.broadcast_to(up, shape).astype(BF)
            down = jnp.broadcast_to(down, shape).astype(BF)
            if len(order) > STREAMS:
                up, down = lax.optimization_barrier((up, down, *order[-(STREAMS + 1)]))[:2]
            sent[q].append((up, down))
            if step < counts[q] + 2 * delay - 1:
                ups[q].append(lax.ppermute(up, "dp", up_pairs))
                downs[q].append(lax.ppermute(down, "dp", down_pairs))
                order.append((ups[q][-1], downs[q][-1]))
    distance = jnp.abs(place - root)
    totals = [None] * len(chunks)
    for q in range(STREAMS):
        for index in range(counts[q]):
            total = None
            for hops in range(delay + 1):
                up, down = sent[q][index + delay + hops]
                value = jnp.where(place >= root, up, down)
                total = value if total is None else jnp.where(distance == hops, value, total)
            totals[q + index * STREAMS] = total
    return totals


def gather_weights(w_query, w_key, w_value, w_out, w_gate, w_up, w_down):
    replica = lax.axis_index("dp")
    replicas = lax.axis_size("dp")

    def part(x):
        rows = x.shape[0] // replicas
        return lax.dynamic_slice_in_dim(x, replica * rows, rows, axis=0)

    def spread(x):
        return lax.all_gather(x, "dp", axis=0, tiled=True)

    half = w_down.shape[0] // 2
    qkv = jnp.concatenate([w_query, w_key, w_value], axis=1)
    sends = [part(w_gate), qkv, part(w_up), w_out, w_down[:half], part(w_down[half:])]
    got = []
    for index, send in enumerate(sends):
        if index >= 2:
            send = after(send, got[index - 2])
        got.append(chip_swap(send))
    other_gate = spread(got[0])
    other_up = spread(got[2])
    other_down = spread(got[5])
    table = [
        (qkv, got[1]),
        (w_gate, other_gate),
        (w_out, got[3]),
        (w_up, other_up),
        (w_down[:half], got[4]),
        (w_down[half:], other_down),
    ]
    whole = []
    for own, other in table:
        whole.append((own, core_swap(own), other, core_swap(other)))
    down = []
    for k in range(4):
        down += [whole[4][k], whole[5][k]]
    return tuple(jnp.concatenate(p, axis=0) for p in (*whole[:4], down))


def body(
    ends, positions, attn_gain, w_query, w_key, w_value, w_out, mlp_gain, w_gate, w_up, w_down
):
    shard = lax.axis_index("fsdp")
    first_section = lax.axis_index("section") == 0
    gain_attn = lax.all_gather(attn_gain, "fsdp", axis=1, tiled=True)[0].astype(F32)
    gain_mlp = lax.all_gather(mlp_gain, "fsdp", axis=1, tiled=True)[0].astype(F32)
    mat_qkv, mat_gate, mat_out, mat_up, mat_down = gather_weights(
        w_query[0], w_key[0], w_value[0], w_out[0], w_gate[0], w_up[0], w_down[0]
    )
    tok_rows = ends.shape[3]
    model_width = ends.shape[4]
    length = tok_rows * lax.axis_size("fsdp")
    key_width = w_key.shape[2]
    query_width = w_query.shape[2]
    key_heads = key_width // HEAD_DIM
    query_heads = query_width // HEAD_DIM
    group_size = query_heads // key_heads
    score_scale = HEAD_DIM ** (-0.5)
    ends_local = ends[0, :, 0]
    places_local = positions[:, 0]
    query_index = shard * tok_rows + jnp.arange(tok_rows, dtype=jnp.int32)
    causal = query_index[:, None] >= jnp.arange(length, dtype=jnp.int32)[None, :]
    tables = [rope_tables(places_local[micro]) for micro in range(2)]

    def pick(first, second):
        return jax.tree.map(lambda left, right: jnp.where(first_section, left, right), first, second)

    def split_heads(queries, keys_all, values_all):
        return (
            queries.reshape(tok_rows, key_heads, group_size, HEAD_DIM).transpose(1, 0, 2, 3),
            keys_all.reshape(length, key_heads, HEAD_DIM).transpose(1, 0, 2),
            values_all.reshape(length, key_heads, HEAD_DIM).transpose(1, 0, 2),
        )

    def masked_scores(query_block, key_block):
        scores = (
            jnp.einsum("rgd,sd->grs", query_block, key_block, preferred_element_type=F32)
            * score_scale
        )
        return jnp.where(causal[None], scores, -1e30)

    def attend_group(packed):
        query_block, key_block, value_block = packed
        scores = masked_scores(query_block, key_block)
        row_max = jnp.max(scores, axis=-1, keepdims=True)
        exp_scores = jnp.exp(scores - row_max)
        row_total = jnp.sum(exp_scores, axis=-1, keepdims=True)
        attn_probs = (exp_scores / row_total).astype(BF)
        attended = jnp.einsum("grs,sd->rgd", attn_probs, value_block, preferred_element_type=F32)
        return (attended, (row_max + jnp.log(row_total))[..., 0])

    def attend_back(packed):
        query_block, key_block, value_block, log_block, grad_block = packed
        scores = masked_scores(query_block, key_block)
        attn_probs = jnp.exp(scores - log_block[..., None])
        grad_value = jnp.einsum(
            "grs,rgd->sd", attn_probs.astype(BF), grad_block, preferred_element_type=F32
        )
        grad_probs = jnp.einsum("rgd,sd->grs", grad_block, value_block, preferred_element_type=F32)
        row_delta = jnp.sum(attn_probs * grad_probs, axis=-1, keepdims=True)
        grad_scores = (attn_probs * (grad_probs - row_delta)).astype(BF)
        grad_query = (
            jnp.einsum("grs,sd->rgd", grad_scores, key_block, preferred_element_type=F32)
            * score_scale
        )
        grad_key = (
            jnp.einsum("grs,rgd->sd", grad_scores, query_block, preferred_element_type=F32)
            * score_scale
        )
        return (grad_query, grad_key, grad_value)

    def forward(layer_input, table):
        cosine_table, sine_table = table
        inverse_one = rms_inverse(layer_input)
        normed_attn = (layer_input * inverse_one * gain_attn).astype(BF)
        qkv = dot_plain(swapped_columns(normed_attn, shard), mat_qkv)
        queries = rotate(
            qkv[:, :query_width].reshape(tok_rows, query_heads, HEAD_DIM), cosine_table, sine_table
        )
        queries = queries.astype(BF).reshape(tok_rows, query_width)
        keys = rotate(
            qkv[:, query_width : query_width + key_width].reshape(tok_rows, key_heads, HEAD_DIM),
            cosine_table,
            sine_table,
        )
        keys = keys.astype(BF).reshape(tok_rows, key_width)
        values = qkv[:, query_width + key_width :].astype(BF)
        pair_all = lax.all_gather(
            jnp.concatenate([keys, values], axis=1), "fsdp", axis=0, tiled=True
        )
        keys_all, values_all = (pair_all[:, :key_width], pair_all[:, key_width:])
        group_out, log_totals = lax.map(attend_group, split_heads(queries, keys_all, values_all))
        attended = group_out.transpose(1, 0, 2, 3).reshape(tok_rows, query_width).astype(BF)
        residual_mid = layer_input + dot_plain(swapped_columns(attended, shard), mat_out)
        inverse_two = rms_inverse(residual_mid)
        normed_mlp = (residual_mid * inverse_two * gain_mlp).astype(BF)
        normed_swapped = swapped_columns(normed_mlp, shard)
        gate_pre = dot_plain(normed_swapped, mat_gate)
        up_proj = dot_plain(normed_swapped, mat_up)
        hidden_act = (jax.nn.silu(gate_pre) * up_proj).astype(BF)
        output = residual_mid + dot_plain(swapped_columns(hidden_act, shard), mat_down)
        return output, (
            layer_input,
            inverse_one,
            normed_attn,
            queries,
            keys_all,
            values_all,
            log_totals,
            attended,
            residual_mid,
            inverse_two,
            normed_mlp,
            gate_pre.astype(BF),
            up_proj.astype(BF),
            hidden_act,
        )

    def backward(grad_top, saved_state, table):
        (
            residual_in,
            inverse_one,
            normed_attn,
            queries,
            keys_all,
            values_all,
            log_totals,
            attended,
            residual_mid,
            inverse_two,
            normed_mlp,
            gate_pre,
            up_proj,
            hidden_act,
        ) = saved_state
        branch_grad = grad_top.astype(BF)
        grad_top = grad_top.astype(F32)
        grad_hidden = swapped_columns(dot_cols(branch_grad, mat_down), shard)
        gate_pre = gate_pre.astype(F32)
        sigmoid_gate = jax.nn.sigmoid(gate_pre)
        grad_gate_pre = (
            grad_hidden
            * up_proj.astype(F32)
            * sigmoid_gate
            * (1.0 + gate_pre * (1.0 - sigmoid_gate))
        ).astype(BF)
        grad_up_proj = (grad_hidden * gate_pre * sigmoid_gate).astype(BF)
        grad_normed = swapped_columns(
            dot_cols(grad_gate_pre, mat_gate) + dot_cols(grad_up_proj, mat_up), shard
        )
        base_mid = residual_mid * inverse_two
        part_gain_mlp = jnp.sum(grad_normed * base_mid, axis=0)
        scaled_grad = grad_normed * gain_mlp
        grad_mid = grad_top + inverse_two * (
            scaled_grad - base_mid * jnp.mean(scaled_grad * base_mid, axis=-1, keepdims=True)
        )
        attn_grad = grad_mid.astype(BF)
        grad_attended = swapped_columns(dot_cols(attn_grad, mat_out).astype(BF), shard)
        query_blocks, key_blocks, value_blocks = split_heads(queries, keys_all, values_all)
        grad_blocks = grad_attended.reshape(tok_rows, key_heads, group_size, HEAD_DIM).transpose(
            1, 0, 2, 3
        )
        grad_queries, grad_keys, grad_values = lax.map(
            attend_back, (query_blocks, key_blocks, value_blocks, log_totals, grad_blocks)
        )
        grad_queries = grad_queries.transpose(1, 0, 2, 3).reshape(tok_rows, query_width)
        grad_keys = grad_keys.transpose(1, 0, 2).reshape(length, key_width)
        grad_values = grad_values.transpose(1, 0, 2).reshape(length, key_width)
        grad_pair = lax.psum_scatter(
            jnp.concatenate([grad_keys, grad_values], axis=1).astype(BF),
            "fsdp",
            scatter_dimension=0,
            tiled=True,
        )
        cosine_table, sine_table = table
        grad_queries = rotate(
            grad_queries.reshape(tok_rows, query_heads, HEAD_DIM), cosine_table, -sine_table
        )
        grad_queries = grad_queries.astype(BF).reshape(tok_rows, query_width)
        grad_keys = rotate(
            grad_pair[:, :key_width].astype(F32).reshape(tok_rows, key_heads, HEAD_DIM),
            cosine_table,
            -sine_table,
        )
        grad_keys = grad_keys.astype(BF).reshape(tok_rows, key_width)
        grad_qkv = jnp.concatenate([grad_queries, grad_keys, grad_pair[:, key_width:]], axis=1)
        grad_normed = swapped_columns(dot_cols(grad_qkv, mat_qkv), shard)
        base_in = residual_in * inverse_one
        part_gain_attn = jnp.sum(grad_normed * base_in, axis=0)
        scaled_grad = grad_normed * gain_attn
        grad_in = grad_mid + inverse_one * (
            scaled_grad - base_in * jnp.mean(scaled_grad * base_in, axis=-1, keepdims=True)
        )
        return (
            grad_in,
            part_gain_attn,
            part_gain_mlp,
            (branch_grad, grad_gate_pre, grad_up_proj, attn_grad, grad_qkv),
        )

    def ahead(x):
        return lax.ppermute(x.astype(BF), "section", [(0, 1)])

    def back(x):
        return lax.ppermute(x.astype(BF), "section", [(1, 0)])

    output, _ = forward(ends_local[0].astype(F32), tables[0])
    received = ahead(output)
    output_one, saved_one = forward(
        jnp.where(first_section, ends_local[1], received).astype(F32), pick(tables[1], tables[0])
    )
    received = ahead(output_one)
    output_two, saved_two = forward(
        jnp.where(first_section, ends_local[0], received).astype(F32), pick(tables[0], tables[1])
    )
    grad_in, _, _, _ = backward(ends_local[0], saved_one, pick(tables[1], tables[0]))
    received = back(grad_in)
    grad_one, gain_attn_one, gain_mlp_one, work_one = backward(
        jnp.where(first_section, received, ends_local[1]), saved_two, pick(tables[0], tables[1])
    )
    received = back(grad_one)
    grad_two, gain_attn_two, gain_mlp_two, work_two = backward(
        jnp.where(first_section, received, ends_local[0]), saved_one, pick(tables[1], tables[0])
    )

    def paired(member):
        own = jnp.concatenate([work_two[member], work_one[member]], axis=0)
        return jnp.concatenate([own, core_swap(own)], axis=0)

    def shares(member):
        x = jnp.concatenate([saved_one[member], saved_two[member]], axis=0)
        width = x.shape[1] // 4
        kept = [column_block(x, shard, width), column_block(x, shard ^ 2, width)]
        given = [
            core_swap(column_block(x, shard ^ 1, width)),
            core_swap(column_block(x, shard ^ 3, width)),
        ]
        return [jnp.concatenate([a, b], axis=0) for a, b in zip(kept, given)]

    chunks = []

    def add_chunks(left, right):
        own_left, other_left = left
        for row in range(0, own_left.shape[1], CHUNK_ROWS):
            for col in range(0, right.shape[1], CHUNK_COLS):
                columns = right[:, col : col + CHUNK_COLS]
                other = dot_rows(other_left[:, row : row + CHUNK_ROWS], columns).astype(BF)
                other = chip_swap(other)
                own = dot_rows(own_left[:, row : row + CHUNK_ROWS], columns)
                chunks.append((own + other.astype(F32)).astype(BF))

    add_chunks(shares(13), paired(0))
    normed = shares(10)
    add_chunks(normed, paired(1))
    add_chunks(normed, paired(2))
    add_chunks(shares(7), paired(3))
    add_chunks(shares(2), paired(4))
    totals = replica_chain(chunks)

    def assembled(rows, cols):
        count = (rows // CHUNK_ROWS) * (cols // CHUNK_COLS)
        taken, totals[:] = totals[:count], totals[count:]
        across = cols // CHUNK_COLS
        lines = [
            jnp.concatenate(taken[at : at + across], axis=1) for at in range(0, count, across)
        ]
        return jnp.concatenate(lines, axis=0).astype(F32)

    grad_down = assembled(w_down.shape[1], w_down.shape[2])
    grad_gate = assembled(w_gate.shape[1], w_gate.shape[2])
    grad_up = assembled(w_up.shape[1], w_up.shape[2])
    grad_out = assembled(w_out.shape[1], w_out.shape[2])
    grad_qkv = assembled(w_query.shape[1], mat_qkv.shape[1])
    gains = jnp.stack([gain_attn_one + gain_attn_two, gain_mlp_one + gain_mlp_two])
    gains = jnp.sum(lax.all_gather(gains, ("fsdp", "dp"), axis=0), axis=0)
    gains = column_block(gains, shard, model_width // 4)
    boundary = jnp.where(
        first_section, jnp.stack([grad_one, grad_two]), jnp.stack([output_one, output_two])
    )
    return (
        boundary[None, :, None],
        gains[0][None],
        grad_qkv[:, :query_width][None],
        grad_qkv[:, query_width : query_width + key_width][None],
        grad_qkv[:, query_width + key_width :][None],
        grad_out[None],
        gains[1][None],
        grad_gate[None],
        grad_up[None],
        grad_down[None],
    )


def solution(mesh):
    return jax.shard_map(
        body,
        mesh=mesh,
        in_specs=(
            P("section", None, "dp", "fsdp", None),
            P(None, "dp", "fsdp"),
            P("section", "fsdp"),
            P("section", "fsdp", None),
            P("section", "fsdp", None),
            P("section", "fsdp", None),
            P("section", "fsdp", None),
            P("section", "fsdp"),
            P("section", "fsdp", None),
            P("section", "fsdp", None),
            P("section", "fsdp", None),
        ),
        out_specs=(
            P("section", None, "dp", "fsdp", None),
            P("section", "fsdp"),
            P("section", "fsdp", None),
            P("section", "fsdp", None),
            P("section", "fsdp", None),
            P("section", "fsdp", None),
            P("section", "fsdp"),
            P("section", "fsdp", None),
            P("section", "fsdp", None),
            P("section", "fsdp", None),
        ),
        check_vma=False,
    )
```

time: 5010 us -> 2800 us (0.56)
  waiting for transfers between devices: 3720 us -> 848 us
  starting transfers between devices: 11.2 us -> 267 us
  matrix products: 788 us -> 1040 us
  other arithmetic: 228 us -> 347 us
  local copies, waits for them, and re-layouts: 104 us -> 198 us
  blocking collectives: 129 us -> 62.2 us
    reduce_scatter x13 -> x3, waiting for transfers between devices: 2420 us -> 14.3 us  [backward(): lax.psum_scatter(jnp.concatenate([grad_keys, grad_values], axis=1).astype...]
    all_gather x18 -> x6, waiting for transfers between devices: 1180 us -> 171 us  [the longest x3 158 us: spread(): return lax.all_gather(x, 'dp', axis=0, tiled=True)]
    ppermute x4 -> x134, waiting for transfers between devices: 113 us -> 663 us  [the longest x35 449 us: chip_swap(): return lax.ppermute(x, 'fsdp', [(0, 2), (2, 0), (1, 3), (3, 1)])]
    ppermute x4 -> x134, starting transfers between devices: 9.22 us -> 266 us  [the longest x35 157 us: replica_chain(): ups[q].append(lax.ppermute(up, 'dp', up_pairs))]
    concatenate x0 -> x33, other arithmetic: none -> 151 us  [the longest x2 42.8 us: gather_weights(): return tuple((jnp.concatenate(p, axis=0) for p in (*whole[:4], down)))]
    dot_general x7 -> x58, matrix products: 114 us -> 249 us  [dot_rows(): lax.dot_general(left, right, (((0,), (0,)), ((), ())), preferred_element_...]
    unnamed x1 -> x0, blocking collectives: 60.6 us -> none
    unnamed x161 -> x561, local copies, waits for them, and re-layouts: 7.98 us -> 63.1 us
  transfers between devices with their start and end apart: 35 -> 143, of which waited for: 33 -> 74; matrix products, arithmetic and copies ran while one was open for 9% -> 32% of each run, Pallas kernels for 0% -> 0%
where the time goes in v1:
time: 2800 us; the launch traced here: 2780 us
  matrix products  1040 us (37%)
  waiting for transfers between devices  848 us (30%)
  other arithmetic  347 us (12%)
  starting transfers between devices  267 us (10%)
  local copies, waits for them, and re-layouts  198 us (7%)
  blocking collectives  62.2 us (2%)
    ppermute x35, waiting for transfers between devices, chip_swap(): return lax.ppermute(x, 'fsdp', [(0, 2), (2, 0), (1, 3), (3, 1)])  449 us
    dot_general x58, matrix products, dot_rows(): lax.dot_general(left, right, (((0,), (0,)), ((), ())), preferred_element_...  249 us
    dot_general x15, matrix products, dot_plain(): return jnp.dot(left, right, preferred_element_type=F32)  214 us
    dot_general x15, matrix products, dot_cols(): lax.dot_general(left, right, (((1,), (1,)), ((), ())), preferred_element_...  201 us
    all_gather x3, waiting for transfers between devices, spread(): return lax.all_gather(x, 'dp', axis=0, tiled=True)  158 us
    ppermute x35, starting transfers between devices, replica_chain(): ups[q].append(lax.ppermute(up, 'dp', up_pairs))  157 us
    ppermute x35, waiting for transfers between devices, replica_chain(): ups[q].append(lax.ppermute(up, 'dp', up_pairs))  80.1 us
    ppermute x35, waiting for transfers between devices, replica_chain(): downs[q].append(lax.ppermute(down, 'dp', down_pairs))  78.7 us
  transfers between devices with their start and end apart: 143, of which 74 were waited for; matrix products, arithmetic and copies ran while one was open for 32% of the time, Pallas kernels for 0%

profile of v1, /device:TPU:0, one launch (start us, length us, event | category | flops | bytes accessed | tf_op | source)
XLA Modules:
  0.0 2778.2 jit_solution(13771678192014678745)
XLA Ops:
  13.6 68.4 %collective-permute-done.1 = bf16[512,3072]{1,0:T(8,128)(2,1)} collective-permute-done((bf16[512,3072]{1,0:T(8,128)(2,1)}, bf16[512,3072]{1,0:T(8,128)(2,1)}, u32[]{:S(2)}, u32[]{:S(2)}) %collective-permute-start.1) | collective-permute-done | bytes 3145760 | tf_op jit(solution)/shard_map/ppermute | solution.py:54
  92.3 19.9 pad_maximum_fusion.4
  126.6 21.5 collective-permute-done.4
  150.5 21.7 collective-permute-done.15
  176.9 43.5 %collective-permute-done.7 = bf16[128,8192]{1,0:T(8,128)(2,1)S(1)} collective-permute-done((bf16[128,8192]{1,0:T(8,128)(2,1)S(1)}, bf16[128,8192]{1,0:T(8,128)(2,1)S(1)}, u32[]{:S(2)}, u32[]{:S(2)}) %collective-permute-start.7) | collective-permute-done | bytes 2097184 | tf_op jit(solution)/shard_map/ppermute | solution.py:54
  225.1 43.0 %collective-permute-done.10 = bf16[128,8192]{1,0:T(8,128)(2,1)S(1)} collective-permute-done((bf16[128,8192]{1,0:T(8,128)(2,1)S(1)}, bf16[128,8192]{1,0:T(8,128)(2,1)S(1)}, u32[]{:S(2)}, u32[]{:S(2)}) %collective-permute-start.10) | collective-permute-done | bytes 2097184 | tf_op jit(solution)/shard_map/ppermute | solution.py:54
  271.3 87.1 %collective-permute-done.14 = bf16[1024,2048]{1,0:T(8,128)(2,1)} collective-permute-done((bf16[1024,2048]{1,0:T(8,128)(2,1)}, bf16[1024,2048]{1,0:T(8,128)(2,1)}, u32[]{:S(2)}, u32[]{:S(2)}) %collective-permute-start.14) | collective-permute-done | bytes 4194336 | tf_op jit(solution)/shard_map/ppermute | solution.py:54
  398.1 7.9 all-gather.11.cloned.1.call-done
  406.1 149.8 %all-gather.13.cloned.1.call-done = bf16[512,8192]{1,0:T(8,128)(2,1)} async-done(((bf16[128,8192]{1,0:T(8,128)(2,1)}), bf16[512,8192]{1,0:T(8,128)(2,1)}) %all-gather.13.cloned.1.call-update) | async-done | bytes 8388624 | tf_op jit(solution)/shard_map/all_gather | solution.py:140
  556.0 58.8 %while.82 = (s32[]{:T(128)}, bf16[8,256,4,64]{1,3,2,0:T(8,128)(2,1)S(1)}, bf16[8,1024,64]{1,2,0:T(8,128)(2,1)}, bf16[8,1024,64]{1,2,0:T(8,128)(2,1)S(1)}, bf16[8...) while((s32[]{:T(128)}, bf16[8,256,4,64]{1,3,2,0:T(8,128)(2,1)S(1)}, ...), condition=%wide.region_4.5_spmd.clone, body=%wide.region_1.4_spmd.clone.sunk | while | flops 274990080 | bytes 9579605 | solution.py:262
  635.2 17.0 fusion.759
  652.2 22.9 pad_maximum_fusion.1
  675.1 19.8 multiply_convert_fusion.2
  698.8 16.7 fusion.295
  720.0 22.3 collective-permute-done.18
  759.3 18.0 fusion.722
  777.3 7.3 dynamic-slice_bitcast_fusion.6
  796.1 40.3 %while.83 = (s32[]{:T(128)}, bf16[8,256,4,64]{1,3,2,0:T(8,128)(2,1)S(1)}, f32[8,4,256]{2,1,0:T(4,128)S(1)}, bf16[8,1024,64]{1,2,0:T(8,128)(2,1)}, bf16[8,1024,64...) while((s32[]{:T(128)}, ...), condition=%wide.region_10.11_spmd.clone, body=%wide.region_7.10_spmd.clone.sunk | while | flops 281279488 | bytes 14322785 | solution.py:262
  843.8 17.2 fusion.756
  861.0 26.5 multiply_convert_fusion.1
  887.4 18.8 fusion.233
  906.2 23.2 fusion.280
  944.5 100.5 %while.84 = (s32[]{:T(128)}, f32[8,256,4,64]{1,3,2,0:T(8,128)}, bf16[8,1024,64]{1,2,0:T(8,128)(2,1)S(1)}, bf16[8,1024,64]{1,2,0:T(8,128)(2,1)}, bf16[8,1024,64]{...) while((s32[]{:T(128)}, f32[8,256,4,64]{1,3,2,0:T(8,128)}, ...), condition=%wide.region_15.16_spmd.clone, body=%wide.region_13.15_spmd.clone.sunk | while | flops 687209472 | bytes 34244728 | solution.py:333
  1051.8 18.2 fusion.832
  1077.8 20.1 collective-permute-done.20
  1135.6 13.0 all-gather.19.cloned.1.call-done
  1156.1 50.9 %while.85 = (s32[]{:T(128)}, bf16[8,256,4,64]{1,3,2,0:T(8,128)(2,1)}, f32[8,4,256]{2,1,0:T(4,128)S(1)}, bf16[8,1024,64]{1,2,0:T(8,128)(2,1)}, bf16[8,1024,64]{1,...) while((s32[]{:T(128)}, ...), condition=%wide.region_22.23_spmd.clone, body=%wide.region_19.22_spmd.clone.sunk | while | flops 281279488 | bytes 22711448 | solution.py:262
  1218.1 17.6 fusion.754
  1235.7 8.6 collective-permute-done.19
  1245.6 18.0 fusion.833
  1270.1 32.1 %multiply_convert_fusion = (bf16[256,8192]{1,0:T(8,128)(2,1)}, bf16[256,8192]{1,0:T(8,128)(2,1)}, bf16[256,8192]{1,0:T(8,128)(2,1)}) fusion(f32[256,8192]{1,0:T(8,128)} %fusion.754, f32[256,2048]{1,0:T(8,128)} %get-tuple-element.746, f32[256,2048]{1,0:T(8,128)} %get-tuple-element.747, f32[256,2048]{1,0:T(8,128)} %get-tuple-element.748, ...), kind=kOutput, calls=%fused_computation.263 | convolution fusion | flops 8648654848 | bytes 63963136 | tf_op jit(solution)/shard_map/dot_general | solution.py:17
  1302.2 15.3 fusion.834
  1317.5 16.8 convolution_add_fusion.1
  1352.4 105.6 %while.86 = (s32[]{:T(128)}, f32[8,256,4,64]{1,3,2,0:T(8,128)}, bf16[8,1024,64]{1,2,0:T(8,128)(2,1)}, bf16[8,1024,64]{1,2,0:T(8,128)(2,1)}, bf16[8,1024,64]{1,2,...) while((s32[]{:T(128)}, f32[8,256,4,64]{1,3,2,0:T(8,128)}, ...), condition=%wide.region_27.28_spmd.clone, body=%wide.region_25.27_spmd.clone.sunk | while | flops 687209472 | bytes 34244728 | solution.py:333
  1477.4 14.3 reduce-scatter.6.cloned.1.call-done
  1505.8 17.6 fusion.286
  1533.0 18.0 fusion.835
  1556.6 7.6 fusion.216
  1564.2 17.5 fusion.836
  1581.7 17.6 convolution_add_fusion
  1614.8 95.3 %while.87 = (s32[]{:T(128)}, f32[8,256,4,64]{1,3,2,0:T(8,128)}, bf16[8,1024,64]{1,2,0:T(8,128)(2,1)S(1)}, bf16[8,1024,64]{1,2,0:T(8,128)(2,1)S(1)}, bf16[8,1024,...) while((s32[]{:T(128)}, f32[8,256,4,64]{1,3,2,0:T(8,128)}, ...), condition=%wide.region_33.34_spmd.clone, body=%wide.region_31.33_spmd.clone.sunk | while | flops 687209472 | bytes 34244728 | solution.py:333
  1714.9 8.2 pad_maximum_fusion.10
  1723.1 8.1 pad_maximum_fusion.9
  1778.7 32.0 %collective-permute-done.54 = bf16[512,1024]{1,0:T(8,128)(2,1)S(1)} collective-permute-done((bf16[512,1024]{1,0:T(8,128)(2,1)S(1)}, bf16[512,1024]{1,0:T(8,128)(2,1)S(1)}, u32[]{:S(2)}, u32[]{:S(2)}) %collective-permute-start.54) | collective-permute-done | bytes 1048608 | tf_op jit(solution)/shard_map/ppermute | solution.py:54
  1841.5 14.1 maximum_maximum_fusion
  1867.1 11.0 collective-permute-done.46
  1891.8 8.8 collective-permute-done.64
  1900.6 22.2 collective-permute-done.69
  1934.4 15.1 collective-permute-done.57
  1955.2 50.4 %all-gather.1 = f32[16,2,2048]{2,1,0:T(2,128)S(1)} all-gather(f32[1,2,2048]{2,1,0:T(2,128)S(1)} %maximum_bitcast_fusion.7), channel_id=2, replica_groups=mesh['section'=2,'fsdp'=4,'dp'=4] {'fsdp','dp'}, dimensions={0}, use_global_device_ids=true | all-gather | bytes 278528 | tf_op jit(solution)/shard_map/all_gather | solution.py:445
  2006.4 7.2 fusion.311
  2019.7 18.2 pad_maximum_fusion.11
  2134.6 12.4 collective-permute-done.71
  2157.9 11.3 collective-permute-done.41
  2181.7 9.9 collective-permute-done.79
  2224.1 7.1 fusion.337
  2308.8 7.0 maximum_convert_fusion
  2572.2 7.7 collective-permute-done.113
  2615.8 9.0 collective-permute-done.117
  2640.6 11.7 convert_element_type.1555
  2665.3 8.1 collective-permute-done.122
  2705.4 12.8 collective-permute-done.127
  2731.6 11.7 convert_element_type.1556
  2747.4 9.7 collective-permute-done.132
  (1433 shorter events, 1520.4 us)
Async XLA Ops:
  7.2 387.0 %all-gather.9.cloned.1.call-start = ((), (), s32[]{:S(2)}) async-start(), calls=%async_computation.3 | async-start | bytes 2621440 | tf_op jit(solution)/shard_map/all_gather | solution.py:258
  10.6 71.4 %collective-permute-start.1 = (bf16[512,3072]{1,0:T(8,128)(2,1)}, bf16[512,3072]{1,0:T(8,128)(2,1)}, u32[]{:S(2)}, u32[]{:S(2)}) collective-permute-start(bf16[512,3072]{1,0:T(8,128)(2,1)} %pad_maximum_fusion.14), channel_id=1, source_target_pairs={{0,8},{8,0},{4,12},{12,4},{1,9},{9,1},{5,13},{13,5},{2,10},{10,2},... | collective-permute-start | bytes 9437192 | tf_op jit(solution)/shard_map/ppermute | solution.py:54
  13.6 78.7 %collective-permute-start = (bf16[512,3072]{1,0:T(8,128)(2,1)}, bf16[512,3072]{1,0:T(8,128)(2,1)}, u32[]{:S(2)}, u32[]{:S(2)}) collective-permute-start(bf16[512,3072]{1,0:T(8,128)(2,1)} %pad_maximum_fusion.14), channel_id=1, source_target_pairs={{0,4},{4,0},{8,12},{12,8},{1,5},{5,1},{9,13},{13,9},{2,6},{6,2},{1... | collective-permute-start | bytes 9437192 | tf_op jit(solution)/shard_map/ppermute | solution.py:50
  90.5 57.6 %collective-permute-start.4 = (bf16[512,2048]{1,0:T(8,128)(2,1)}, bf16[512,2048]{1,0:T(8,128)(2,1)}, u32[]{:S(2)}, u32[]{:S(2)}) collective-permute-start(bf16[512,2048]{1,0:T(8,128)(2,1)} %bitcast.20), channel_id=1, source_target_pairs={{0,8},{8,0},{4,12},{12,4},{1,9},{9,1},{5,13},{13,5},{2,10},{10,2},... | collective-permute-start | bytes 6291464 | tf_op jit(solution)/shard_map/ppermute | solution.py:54
  120.0 277.7 %all-gather.15.cloned.1.call-start = ((), (), s32[]{:S(2)}) async-start(), calls=%async_computation.6 | async-start | bytes 5242880 | tf_op jit(solution)/shard_map/all_gather | solution.py:140
  173.3 232.7 %all-gather.11.cloned.1.call-start = ((), (), s32[]{:S(2)}) async-start(), calls=%async_computation.4 | async-start | bytes 10485760 | tf_op jit(solution)/shard_map/all_gather | solution.py:140
  175.1 45.4 %collective-permute-start.7 = (bf16[128,8192]{1,0:T(8,128)(2,1)S(1)}, bf16[128,8192]{1,0:T(8,128)(2,1)S(1)}, u32[]{:S(2)}, u32[]{:S(2)}) collective-permute-start(bf16[128,8192]{1,0:T(8,128)(2,1)S(1)} %dynamic-slice_bitcast_fusion.8), channel_id=1, source_target_pairs={{0,8},{8,0},{4,12},{12,4},{1,9},{9,1},{5,13},{13,5},{2,10},{10,2},... | collective-permute-start | bytes 6291464 | tf_op jit(solution)/shard_map/ppermute | solution.py:54
  221.8 334.1 %all-gather.13.cloned.1.call-start = ((), (), s32[]{:S(2)}) async-start(), calls=%async_computation.5 | async-start | bytes 10485760 | tf_op jit(solution)/shard_map/all_gather | solution.py:140
  223.6 44.5 %collective-permute-start.10 = (bf16[128,8192]{1,0:T(8,128)(2,1)S(1)}, bf16[128,8192]{1,0:T(8,128)(2,1)S(1)}, u32[]{:S(2)}, u32[]{:S(2)}) collective-permute-start(bf16[128,8192]{1,0:T(8,128)(2,1)S(1)} %dynamic-slice_bitcast_fusion.7), channel_id=1, source_target_pairs={{0,8},{8,0},{4,12},{12,4},{1,9},{9,1},{5,13},{13,5},{2,10},{10,2},... | collective-permute-start | bytes 6291464 | tf_op jit(solution)/shard_map/ppermute | solution.py:54
  269.5 518.9 %all-gather.17.cloned.1.call-start = ((), (), s32[]{:S(2)}) async-start(), calls=%async_computation.7 | async-start | bytes 2621440 | tf_op jit(solution)/shard_map/all_gather | solution.py:258
  269.5 88.9 %collective-permute-start.14 = (bf16[1024,2048]{1,0:T(8,128)(2,1)}, bf16[1024,2048]{1,0:T(8,128)(2,1)}, u32[]{:S(2)}, u32[]{:S(2)}) collective-permute-start(bf16[1024,2048]{1,0:T(8,128)(2,1)} %get-tuple-element.355), channel_id=1, source_target_pairs={{0,8},{8,0},{4,12},{12,4},{1,9},{9,1},{5,13},{13,5},{2,10},{10,2},... | collective-permute-start | bytes 12582920 | tf_op jit(solution)/shard_map/ppermute | solution.py:54
  270.8 103.7 %collective-permute-start.12 = (bf16[1024,2048]{1,0:T(8,128)(2,1)}, bf16[1024,2048]{1,0:T(8,128)(2,1)}, u32[]{:S(2)}, u32[]{:S(2)}) collective-permute-start(bf16[1024,2048]{1,0:T(8,128)(2,1)} %get-tuple-element.355), channel_id=1, source_target_pairs={{0,4},{4,0},{8,12},{12,8},{1,5},{5,1},{9,13},{13,9},{2,6},{6,2},{1... | collective-permute-start | bytes 12582920 | tf_op jit(solution)/shard_map/ppermute | solution.py:50
  270.8 108.8 %collective-permute-start.13 = (bf16[1024,2048]{1,0:T(8,128)(2,1)}, bf16[1024,2048]{1,0:T(8,128)(2,1)}, u32[]{:S(2)}, u32[]{:S(2)}) collective-permute-start(bf16[1024,2048]{1,0:T(8,128)(2,1)} %get-tuple-element.756), channel_id=1, source_target_pairs={{0,4},{4,0},{8,12},{12,8},{1,5},{5,1},{9,13},{13,9},{2,6},{6,2},{1... | collective-permute-start | bytes 12582920 | tf_op jit(solution)/shard_map/ppermute | solution.py:50
  358.4 47.7 %collective-permute-start.16 = (bf16[1024,2048]{1,0:T(8,128)(2,1)}, bf16[1024,2048]{1,0:T(8,128)(2,1)}, u32[]{:S(2)}, u32[]{:S(2)}) collective-permute-start(bf16[1024,2048]{1,0:T(8,128)(2,1)} %collective-permute-done.14), channel_id=1, source_target_pairs={{0,4},{4,0},{8,12},{12,8},{1,5},{5,1},{9,13},{13,9},{2,6},{6,2},{1... | collective-permute-start | bytes 12582920 | tf_op jit(solution)/shard_map/ppermute | solution.py:50
  374.5 260.8 %collective-permute-start.6 = (bf16[512,8192]{1,0:T(8,128)(2,1)}, bf16[512,8192]{1,0:T(8,128)(2,1)}, u32[]{:S(2)}, u32[]{:S(2)}) collective-permute-start(bf16[512,8192]{1,0:T(8,128)(2,1)} %bitcast.824), channel_id=1, source_target_pairs={{0,4},{4,0},{8,12},{12,8},{1,5},{5,1},{9,13},{13,9},{2,6},{6,2},{1... | collective-permute-start | bytes 25165832 | tf_op jit(solution)/shard_map/ppermute | solution.py:50
  379.6 272.6 %collective-permute-start.9 = (bf16[512,8192]{1,0:T(8,128)(2,1)}, bf16[512,8192]{1,0:T(8,128)(2,1)}, u32[]{:S(2)}, u32[]{:S(2)}) collective-permute-start(bf16[512,8192]{1,0:T(8,128)(2,1)} %bitcast.746), channel_id=1, source_target_pairs={{0,4},{4,0},{8,12},{12,8},{1,5},{5,1},{9,13},{13,9},{2,6},{6,2},{1... | collective-permute-start | bytes 25165832 | tf_op jit(solution)/shard_map/ppermute | solution.py:50
  397.8 232.7 %collective-permute-start.17 = (bf16[1024,2048]{1,0:T(8,128)(2,1)}, bf16[1024,2048]{1,0:T(8,128)(2,1)}, u32[]{:S(2)}, u32[]{:S(2)}) collective-permute-start(bf16[1024,2048]{1,0:T(8,128)(2,1)} %all-gather.15.cloned.1.call-done), channel_id=1, source_target_pairs={{0,4},{4,0},{8,12},{12,8},{1,5},{5,1},{9,13},{13,9},{2,6},{6,2},{1... | collective-permute-start | bytes 12582920 | tf_op jit(solution)/shard_map/ppermute | solution.py:50
  406.0 229.2 %collective-permute-start.8 = (bf16[512,8192]{1,0:T(8,128)(2,1)}, bf16[512,8192]{1,0:T(8,128)(2,1)}, u32[]{:S(2)}, u32[]{:S(2)}) collective-permute-start(bf16[512,8192]{1,0:T(8,128)(2,1)} %all-gather.11.cloned.1.call-done), channel_id=1, source_target_pairs={{0,4},{4,0},{8,12},{12,8},{1,5},{5,1},{9,13},{13,9},{2,6},{6,2},{1... | collective-permute-start | bytes 25165832 | tf_op jit(solution)/shard_map/ppermute | solution.py:50
  555.9 96.3 %collective-permute-start.11 = (bf16[512,8192]{1,0:T(8,128)(2,1)}, bf16[512,8192]{1,0:T(8,128)(2,1)}, u32[]{:S(2)}, u32[]{:S(2)}) collective-permute-start(bf16[512,8192]{1,0:T(8,128)(2,1)} %all-gather.13.cloned.1.call-done), channel_id=1, source_target_pairs={{0,4},{4,0},{8,12},{12,8},{1,5},{5,1},{9,13},{13,9},{2,6},{6,2},{1... | collective-permute-start | bytes 25165832 | tf_op jit(solution)/shard_map/ppermute | solution.py:50
  759.3 340.1 %reduce-scatter.4.cloned.1.call-start = ((), (), s32[]{:S(2)}) async-start(), calls=%async_computation.8 | async-start | bytes 2621440 | tf_op jit(solution)/shard_map/reduce_scatter | solution.py:339
  1047.7 100.9 %all-gather.19.cloned.1.call-start = ((), (), s32[]{:S(2)}) async-start(), calls=%async_computation.9 | async-start | bytes 2621440 | tf_op jit(solution)/shard_map/all_gather | solution.py:258
  1126.4 365.3 %reduce-scatter.6.cloned.1.call-start = ((), (), s32[]{:S(2)}) async-start(), calls=%async_computation.10 | async-start | bytes 2621440 | tf_op jit(solution)/shard_map/reduce_scatter | solution.py:339
  1461.0 357.4 %reduce-scatter.8.cloned.1.call-start = ((), (), s32[]{:S(2)}) async-start(), calls=%async_computation.11 | async-start | bytes 2621440 | tf_op jit(solution)/shard_map/reduce_scatter | solution.py:339
  1465.6 293.4 %collective-permute-start.29 = (bf16[512,512]{0,1:T(8,128)(2,1)}, bf16[512,512]{0,1:T(8,128)(2,1)}, u32[]{:S(2)}, u32[]{:S(2)}) collective-permute-start(bf16[512,512]{0,1:T(8,128)(2,1)} %get-tuple-element.865), channel_id=1, source_target_pairs={{0,4},{4,0},{8,12},{12,8},{1,5},{5,1},{9,13},{13,9},{2,6},{6,2},{1... | collective-permute-start | bytes 1572872 | tf_op jit(solution)/shard_map/ppermute | solution.py:50
  1473.4 50.0 %collective-permute-start.45 = (bf16[512,2048]{1,0:T(8,128)(2,1)}, bf16[512,2048]{1,0:T(8,128)(2,1)}, u32[]{:S(2)}, u32[]{:S(2)}) collective-permute-start(bf16[512,2048]{1,0:T(8,128)(2,1)} %get-tuple-element.740), channel_id=1, source_target_pairs={{0,4},{4,0},{8,12},{12,8},{1,5},{5,1},{9,13},{13,9},{2,6},{6,2},{1... | collective-permute-start | bytes 6291464 | tf_op jit(solution)/shard_map/ppermute | solution.py:50
  1473.4 52.5 %collective-permute-start.43 = (bf16[512,2048]{1,0:T(8,128)(2,1)}, bf16[512,2048]{1,0:T(8,128)(2,1)}, u32[]{:S(2)}, u32[]{:S(2)}) collective-permute-start(bf16[512,2048]{1,0:T(8,128)(2,1)} %get-tuple-element.738), channel_id=1, source_target_pairs={{0,4},{4,0},{8,12},{12,8},{1,5},{5,1},{9,13},{13,9},{2,6},{6,2},{1... | collective-permute-start | bytes 6291464 | tf_op jit(solution)/shard_map/ppermute | solution.py:50
  1739.7 89.2 %collective-permute-start.48 = (bf16[512,1024]{1,0:T(8,128)(2,1)}, bf16[512,1024]{1,0:T(8,128)(2,1)}, u32[]{:S(2)}, u32[]{:S(2)}) collective-permute-start(bf16[512,1024]{1,0:T(8,128)(2,1)} %convolution_convert_fusion.8), channel_id=1, source_target_pairs={{0,8},{8,0},{4,12},{12,4},{1,9},{9,1},{5,13},{13,5},{2,10},{10,2},... | collective-permute-start | bytes 3145736 | tf_op jit(solution)/shard_map/ppermute | solution.py:54
  1741.3 69.4 %collective-permute-start.54 = (bf16[512,1024]{1,0:T(8,128)(2,1)S(1)}, bf16[512,1024]{1,0:T(8,128)(2,1)S(1)}, u32[]{:S(2)}, u32[]{:S(2)}) collective-permute-start(bf16[512,1024]{1,0:T(8,128)(2,1)S(1)} %convolution_convert_fusion.6), channel_id=1, source_target_pairs={{0,8},{8,0},{4,12},{12,4},{1,9},{9,1},{5,13},{13,5},{2,10},{10,2},... | collective-permute-start | bytes 3145736 | tf_op jit(solution)/shard_map/ppermute | solution.py:54
  1751.8 85.4 %collective-permute-start.59 = (bf16[512,1024]{1,0:T(8,128)(2,1)}, bf16[512,1024]{1,0:T(8,128)(2,1)}, u32[]{:S(2)}, u32[]{:S(2)}) collective-permute-start(bf16[512,1024]{1,0:T(8,128)(2,1)} %convolution_convert_fusion.5), channel_id=1, source_target_pairs={{0,8},{8,0},{4,12},{12,4},{1,9},{9,1},{5,13},{13,5},{2,10},{10,2},... | collective-permute-start | bytes 3145736 | tf_op jit(solution)/shard_map/ppermute | solution.py:54
  1772.4 56.5 %collective-permute-start.50 = (bf16[512,1024]{1,0:T(8,128)(2,1)}, bf16[512,1024]{1,0:T(8,128)(2,1)}, u32[]{:S(2)}, u32[]{:S(2)}) collective-permute-start(bf16[512,1024]{1,0:T(8,128)(2,1)} %get-tuple-element.907), channel_id=1, source_target_pairs={{1,0},{2,1},{3,2},{5,4},{6,5},{7,6},{9,8},{10,9},{11,10},{13,12},{... | collective-permute-start | bytes 3145736 | tf_op jit(solution)/shard_map/ppermute | solution.py:116
  1773.7 56.3 %collective-permute-start.51 = (bf16[512,1024]{1,0:T(8,128)(2,1)}, bf16[512,1024]{1,0:T(8,128)(2,1)S(1)}, u32[]{:S(2)}, u32[]{:S(2)}) collective-permute-start(bf16[512,1024]{1,0:T(8,128)(2,1)} %get-tuple-element.908), channel_id=1, source_target_pairs={{0,1},{1,2},{2,3},{4,5},{5,6},{6,7},{8,9},{9,10},{10,11},{12,13},{... | collective-permute-start | bytes 3145736 | tf_op jit(solution)/shard_map/ppermute | solution.py:115
  1828.9 217.8 %collective-permute-start.38 = (bf16[512,8192]{1,0:T(8,128)(2,1)}, bf16[512,8192]{1,0:T(8,128)(2,1)}, u32[]{:S(2)}, u32[]{:S(2)}) collective-permute-start(bf16[512,8192]{1,0:T(8,128)(2,1)} %pad_maximum_fusion.10), channel_id=1, source_target_pairs={{0,4},{4,0},{8,12},{12,8},{1,5},{5,1},{9,13},{13,9},{2,6},{6,2},{1... | collective-permute-start | bytes 25165832 | tf_op jit(solution)/shard_map/ppermute | solution.py:50
  1878.1 44.6 %collective-permute-start.69 = (bf16[512,1024]{1,0:T(8,128)(2,1)S(1)}, bf16[512,1024]{1,0:T(8,128)(2,1)S(1)}, u32[]{:S(2)}, u32[]{:S(2)}) collective-permute-start(bf16[512,1024]{1,0:T(8,128)(2,1)S(1)} %copy-done.214), channel_id=1, source_target_pairs={{0,8},{8,0},{4,12},{12,4},{1,9},{9,1},{5,13},{13,5},{2,10},{10,2},... | collective-permute-start | bytes 3145736 | tf_op jit(solution)/shard_map/ppermute | solution.py:54
  1879.2 44.9 %collective-permute-start.60 = (bf16[512,1024]{1,0:T(8,128)(2,1)S(1)}, bf16[512,1024]{1,0:T(8,128)(2,1)S(1)}, u32[]{:S(2)}, u32[]{:S(2)}) collective-permute-start(bf16[512,1024]{1,0:T(8,128)(2,1)S(1)} %get-tuple-element.372), channel_id=1, source_target_pairs={{0,1},{1,2},{2,3},{4,5},{5,6},{6,7},{8,9},{9,10},{10,11},{12,13},{... | collective-permute-start | bytes 3145736 | tf_op jit(solution)/shard_map/ppermute | solution.py:115
  1885.0 43.7 %collective-permute-start.61 = (bf16[512,1024]{1,0:T(8,128)(2,1)S(1)}, bf16[512,1024]{1,0:T(8,128)(2,1)S(1)}, u32[]{:S(2)}, u32[]{:S(2)}) collective-permute-start(bf16[512,1024]{1,0:T(8,128)(2,1)S(1)} %get-tuple-element.373), channel_id=1, source_target_pairs={{1,0},{2,1},{3,2},{5,4},{6,5},{7,6},{9,8},{10,9},{11,10},{13,12},{... | collective-permute-start | bytes 3145736 | tf_op jit(solution)/shard_map/ppermute | solution.py:116
  1900.6 118.9 %collective-permute-start.23 = (bf16[512,3072]{0,1:T(8,128)(2,1)}, bf16[512,3072]{0,1:T(8,128)(2,1)}, u32[]{:S(2)}, u32[]{:S(2)}) collective-permute-start(bf16[512,3072]{0,1:T(8,128)(2,1)} %maximum_maximum_fusion), channel_id=1, source_target_pairs={{0,4},{4,0},{8,12},{12,8},{1,5},{5,1},{9,13},{13,9},{2,6},{6,2},{1... | collective-permute-start | bytes 9437192 | tf_op jit(solution)/shard_map/ppermute | solution.py:50
  1928.7 156.1 %collective-permute-start.32 = (bf16[512,8192]{1,0:T(8,128)(2,1)}, bf16[512,8192]{1,0:T(8,128)(2,1)}, u32[]{:S(2)}, u32[]{:S(2)}) collective-permute-start(bf16[512,8192]{1,0:T(8,128)(2,1)} %pad_maximum_fusion.9), channel_id=1, source_target_pairs={{0,4},{4,0},{8,12},{12,8},{1,5},{5,1},{9,13},{13,9},{2,6},{6,2},{1... | collective-permute-start | bytes 25165832 | tf_op jit(solution)/shard_map/ppermute | solution.py:50
  1949.5 64.1 %collective-permute-start.65 = (bf16[512,1024]{1,0:T(8,128)(2,1)}, bf16[512,1024]{1,0:T(8,128)(2,1)}, u32[]{:S(2)}, u32[]{:S(2)}) collective-permute-start(bf16[512,1024]{1,0:T(8,128)(2,1)} %get-tuple-element.376), channel_id=1, source_target_pairs={{0,1},{1,2},{2,3},{4,5},{5,6},{6,7},{8,9},{9,10},{10,11},{12,13},{... | collective-permute-start | bytes 3145736 | tf_op jit(solution)/shard_map/ppermute | solution.py:115
  1953.9 59.8 %collective-permute-start.66 = (bf16[512,1024]{1,0:T(8,128)(2,1)}, bf16[512,1024]{1,0:T(8,128)(2,1)}, u32[]{:S(2)}, u32[]{:S(2)}) collective-permute-start(bf16[512,1024]{1,0:T(8,128)(2,1)} %get-tuple-element.377), channel_id=1, source_target_pairs={{1,0},{2,1},{3,2},{5,4},{6,5},{7,6},{9,8},{10,9},{11,10},{13,12},{... | collective-permute-start | bytes 3145736 | tf_op jit(solution)/shard_map/ppermute | solution.py:116
  2013.7 44.3 %collective-permute-start.33 = (bf16[512,512]{1,0:T(8,128)(2,1)S(1)}, bf16[512,512]{1,0:T(8,128)(2,1)}, u32[]{:S(2)}, u32[]{:S(2)}) collective-permute-start(bf16[512,512]{1,0:T(8,128)(2,1)S(1)} %copy-done.171), channel_id=1, source_target_pairs={{0,4},{4,0},{8,12},{12,8},{1,5},{5,1},{9,13},{13,9},{2,6},{6,2},{1... | collective-permute-start | bytes 1572872 | tf_op jit(solution)/shard_map/ppermute | solution.py:50
  2019.5 99.2 %collective-permute-start.31 = (bf16[512,512]{1,0:T(8,128)(2,1)S(1)}, bf16[512,512]{1,0:T(8,128)(2,1)}, u32[]{:S(2)}, u32[]{:S(2)}) collective-permute-start(bf16[512,512]{1,0:T(8,128)(2,1)S(1)} %copy-done.169), channel_id=1, source_target_pairs={{0,4},{4,0},{8,12},{12,8},{1,5},{5,1},{9,13},{13,9},{2,6},{6,2},{1... | collective-permute-start | bytes 1572872 | tf_op jit(solution)/shard_map/ppermute | solution.py:50
  2037.9 82.4 %collective-permute-start.63 = (bf16[512,1024]{1,0:T(8,128)(2,1)S(1)}, bf16[512,1024]{1,0:T(8,128)(2,1)}, u32[]{:S(2)}, u32[]{:S(2)}) collective-permute-start(bf16[512,1024]{1,0:T(8,128)(2,1)S(1)} %get-tuple-element.375), channel_id=1, source_target_pairs={{1,0},{2,1},{3,2},{5,4},{6,5},{7,6},{9,8},{10,9},{11,10},{13,12},{... | collective-permute-start | bytes 3145736 | tf_op jit(solution)/shard_map/ppermute | solution.py:116
  2046.6 79.1 %collective-permute-start.62 = (bf16[512,1024]{1,0:T(8,128)(2,1)S(1)}, bf16[512,1024]{1,0:T(8,128)(2,1)S(1)}, u32[]{:S(2)}, u32[]{:S(2)}) collective-permute-start(bf16[512,1024]{1,0:T(8,128)(2,1)S(1)} %get-tuple-element.374), channel_id=1, source_target_pairs={{0,1},{1,2},{2,3},{4,5},{5,6},{6,7},{8,9},{9,10},{10,11},{12,13},{... | collective-permute-start | bytes 3145736 | tf_op jit(solution)/shard_map/ppermute | solution.py:115
  2058.1 75.2 %collective-permute-start.70 = (bf16[512,1024]{1,0:T(8,128)(2,1)S(1)}, bf16[512,1024]{1,0:T(8,128)(2,1)S(1)}, u32[]{:S(2)}, u32[]{:S(2)}) collective-permute-start(bf16[512,1024]{1,0:T(8,128)(2,1)S(1)} %get-tuple-element.380), channel_id=1, source_target_pairs={{0,1},{1,2},{2,3},{4,5},{5,6},{6,7},{8,9},{9,10},{10,11},{12,13},{... | collective-permute-start | bytes 3145736 | tf_op jit(solution)/shard_map/ppermute | solution.py:115
  2125.7 43.5 %collective-permute-start.41 = (bf16[512,1024]{1,0:T(8,128)(2,1)}, bf16[512,1024]{1,0:T(8,128)(2,1)S(1)}, u32[]{:S(2)}, u32[]{:S(2)}) collective-permute-start(bf16[512,1024]{1,0:T(8,128)(2,1)} %fusion.593), channel_id=1, source_target_pairs={{0,8},{8,0},{4,12},{12,4},{1,9},{9,1},{5,13},{13,5},{2,10},{10,2},... | collective-permute-start | bytes 3145736 | tf_op jit(solution)/shard_map/ppermute | solution.py:54
  2125.8 65.9 %collective-permute-start.79 = (bf16[512,1024]{1,0:T(8,128)(2,1)}, bf16[512,1024]{1,0:T(8,128)(2,1)S(1)}, u32[]{:S(2)}, u32[]{:S(2)}) collective-permute-start(bf16[512,1024]{1,0:T(8,128)(2,1)} %fusion.602), channel_id=1, source_target_pairs={{0,8},{8,0},{4,12},{12,4},{1,9},{9,1},{5,13},{13,5},{2,10},{10,2},... | collective-permute-start | bytes 3145736 | tf_op jit(solution)/shard_map/ppermute | solution.py:54
  2172.1 42.0 %collective-permute-start.40 = (bf16[512,1024]{1,0:T(8,128)(2,1)}, bf16[512,1024]{1,0:T(8,128)(2,1)S(1)}, u32[]{:S(2)}, u32[]{:S(2)}) collective-permute-start(bf16[512,1024]{1,0:T(8,128)(2,1)} %fusion.590), channel_id=1, source_target_pairs={{0,8},{8,0},{4,12},{12,4},{1,9},{9,1},{5,13},{13,5},{2,10},{10,2},... | collective-permute-start | bytes 3145736 | tf_op jit(solution)/shard_map/ppermute | solution.py:54
  2174.2 62.5 %collective-permute-start.84 = (bf16[512,1024]{1,0:T(8,128)(2,1)}, bf16[512,1024]{1,0:T(8,128)(2,1)}, u32[]{:S(2)}, u32[]{:S(2)}) collective-permute-start(bf16[512,1024]{1,0:T(8,128)(2,1)} %fusion.605), channel_id=1, source_target_pairs={{0,8},{8,0},{4,12},{12,4},{1,9},{9,1},{5,13},{13,5},{2,10},{10,2},... | collective-permute-start | bytes 3145736 | tf_op jit(solution)/shard_map/ppermute | solution.py:54
  2216.5 42.5 %collective-permute-start.39 = (bf16[512,1024]{1,0:T(8,128)(2,1)}, bf16[512,1024]{1,0:T(8,128)(2,1)S(1)}, u32[]{:S(2)}, u32[]{:S(2)}) collective-permute-start(bf16[512,1024]{1,0:T(8,128)(2,1)} %fusion.587), channel_id=1, source_target_pairs={{0,8},{8,0},{4,12},{12,4},{1,9},{9,1},{5,13},{13,5},{2,10},{10,2},... | collective-permute-start | bytes 3145736 | tf_op jit(solution)/shard_map/ppermute | solution.py:54
  2222.1 59.5 %collective-permute-start.89 = (bf16[512,1024]{1,0:T(8,128)(2,1)}, bf16[512,1024]{1,0:T(8,128)(2,1)S(1)}, u32[]{:S(2)}, u32[]{:S(2)}) collective-permute-start(bf16[512,1024]{1,0:T(8,128)(2,1)} %fusion.608), channel_id=1, source_target_pairs={{0,8},{8,0},{4,12},{12,4},{1,9},{9,1},{5,13},{13,5},{2,10},{10,2},... | collective-permute-start | bytes 3145736 | tf_op jit(solution)/shard_map/ppermute | solution.py:54
  2261.7 45.7 %collective-permute-start.37 = (bf16[512,1024]{1,0:T(8,128)(2,1)}, bf16[512,1024]{1,0:T(8,128)(2,1)}, u32[]{:S(2)}, u32[]{:S(2)}) collective-permute-start(bf16[512,1024]{1,0:T(8,128)(2,1)} %fusion.584), channel_id=1, source_target_pairs={{0,8},{8,0},{4,12},{12,4},{1,9},{9,1},{5,13},{13,5},{2,10},{10,2},... | collective-permute-start | bytes 3145736 | tf_op jit(solution)/shard_map/ppermute | solution.py:54
  2268.2 58.4 %collective-permute-start.94 = (bf16[512,1024]{1,0:T(8,128)(2,1)}, bf16[512,1024]{1,0:T(8,128)(2,1)}, u32[]{:S(2)}, u32[]{:S(2)}) collective-permute-start(bf16[512,1024]{1,0:T(8,128)(2,1)} %fusion.611), channel_id=1, source_target_pairs={{0,8},{8,0},{4,12},{12,4},{1,9},{9,1},{5,13},{13,5},{2,10},{10,2},... | collective-permute-start | bytes 3145736 | tf_op jit(solution)/shard_map/ppermute | solution.py:54
  2317.1 54.3 %collective-permute-start.99 = (bf16[512,1024]{1,0:T(8,128)(2,1)S(1)}, bf16[512,1024]{1,0:T(8,128)(2,1)S(1)}, u32[]{:S(2)}, u32[]{:S(2)}) collective-permute-start(bf16[512,1024]{1,0:T(8,128)(2,1)S(1)} %copy-done.211), channel_id=1, source_target_pairs={{0,8},{8,0},{4,12},{12,4},{1,9},{9,1},{5,13},{13,5},{2,10},{10,2},... | collective-permute-start | bytes 3145736 | tf_op jit(solution)/shard_map/ppermute | solution.py:54
  2358.7 57.8 %collective-permute-start.104 = (bf16[512,1024]{1,0:T(8,128)(2,1)S(1)}, bf16[512,1024]{1,0:T(8,128)(2,1)}, u32[]{:S(2)}, u32[]{:S(2)}) collective-permute-start(bf16[512,1024]{1,0:T(8,128)(2,1)S(1)} %copy-done.209), channel_id=1, source_target_pairs={{0,8},{8,0},{4,12},{12,4},{1,9},{9,1},{5,13},{13,5},{2,10},{10,2},... | collective-permute-start | bytes 3145736 | tf_op jit(solution)/shard_map/ppermute | solution.py:54
  2403.8 57.6 %collective-permute-start.109 = (bf16[512,1024]{1,0:T(8,128)(2,1)S(1)}, bf16[512,1024]{1,0:T(8,128)(2,1)}, u32[]{:S(2)}, u32[]{:S(2)}) collective-permute-start(bf16[512,1024]{1,0:T(8,128)(2,1)S(1)} %copy-done.207), channel_id=1, source_target_pairs={{0,8},{8,0},{4,12},{12,4},{1,9},{9,1},{5,13},{13,5},{2,10},{10,2},... | collective-permute-start | bytes 3145736 | tf_op jit(solution)/shard_map/ppermute | solution.py:54
  2461.4 44.9 %collective-permute-start.114 = (bf16[512,1024]{1,0:T(8,128)(2,1)}, bf16[512,1024]{1,0:T(8,128)(2,1)}, u32[]{:S(2)}, u32[]{:S(2)}) collective-permute-start(bf16[512,1024]{1,0:T(8,128)(2,1)} %fusion.623), channel_id=1, source_target_pairs={{0,8},{8,0},{4,12},{12,4},{1,9},{9,1},{5,13},{13,5},{2,10},{10,2},... | collective-permute-start | bytes 3145736 | tf_op jit(solution)/shard_map/ppermute | solution.py:54
  2506.3 44.9 %collective-permute-start.119 = (bf16[512,1024]{1,0:T(8,128)(2,1)S(1)}, bf16[512,1024]{1,0:T(8,128)(2,1)}, u32[]{:S(2)}, u32[]{:S(2)}) collective-permute-start(bf16[512,1024]{1,0:T(8,128)(2,1)S(1)} %copy-done.205), channel_id=1, source_target_pairs={{0,8},{8,0},{4,12},{12,4},{1,9},{9,1},{5,13},{13,5},{2,10},{10,2},... | collective-permute-start | bytes 3145736 | tf_op jit(solution)/shard_map/ppermute | solution.py:54
  2526.1 46.2 %collective-permute-start.25 = (bf16[512,1024]{1,0:T(8,128)(2,1)S(1)}, bf16[512,1024]{1,0:T(8,128)(2,1)S(1)}, u32[]{:S(2)}, u32[]{:S(2)}) collective-permute-start(bf16[512,1024]{1,0:T(8,128)(2,1)S(1)} %copy-done.204), channel_id=1, source_target_pairs={{0,8},{8,0},{4,12},{12,4},{1,9},{9,1},{5,13},{13,5},{2,10},{10,2},... | collective-permute-start | bytes 3145736 | tf_op jit(solution)/shard_map/ppermute | solution.py:54
  2608.5 47.1 %collective-permute-start.125 = (bf16[512,1024]{1,0:T(8,128)(2,1)}, bf16[512,1024]{1,0:T(8,128)(2,1)}, u32[]{:S(2)}, u32[]{:S(2)}) collective-permute-start(bf16[512,1024]{1,0:T(8,128)(2,1)} %get-tuple-element.425), channel_id=1, source_target_pairs={{1,0},{2,1},{3,2},{5,4},{6,5},{7,6},{9,8},{10,9},{11,10},{13,12},{... | collective-permute-start | bytes 3145736 | tf_op jit(solution)/shard_map/ppermute | solution.py:116
  2609.8 45.9 %collective-permute-start.124 = (bf16[512,1024]{1,0:T(8,128)(2,1)}, bf16[512,1024]{1,0:T(8,128)(2,1)}, u32[]{:S(2)}, u32[]{:S(2)}) collective-permute-start(bf16[512,1024]{1,0:T(8,128)(2,1)} %get-tuple-element.424), channel_id=1, source_target_pairs={{0,1},{1,2},{2,3},{4,5},{5,6},{6,7},{8,9},{9,10},{10,11},{12,13},{... | collective-permute-start | bytes 3145736 | tf_op jit(solution)/shard_map/ppermute | solution.py:115
  2631.0 42.3 %collective-permute-start.122 = (bf16[512,1024]{1,0:T(8,128)(2,1)}, bf16[512,1024]{1,0:T(8,128)(2,1)}, u32[]{:S(2)}, u32[]{:S(2)}) collective-permute-start(bf16[512,1024]{1,0:T(8,128)(2,1)} %get-tuple-element.422), channel_id=1, source_target_pairs={{0,1},{1,2},{2,3},{4,5},{5,6},{6,7},{8,9},{9,10},{10,11},{12,13},{... | collective-permute-start | bytes 3145736 | tf_op jit(solution)/shard_map/ppermute | solution.py:115
  2676.0 42.2 %collective-permute-start.127 = (bf16[512,1024]{1,0:T(8,128)(2,1)S(1)}, bf16[512,1024]{1,0:T(8,128)(2,1)S(1)}, u32[]{:S(2)}, u32[]{:S(2)}) collective-permute-start(bf16[512,1024]{1,0:T(8,128)(2,1)S(1)} %get-tuple-element.427), channel_id=1, source_target_pairs={{0,1},{1,2},{2,3},{4,5},{5,6},{6,7},{8,9},{9,10},{10,11},{12,13},{... | collective-permute-start | bytes 3145736 | tf_op jit(solution)/shard_map/ppermute | solution.py:115
  2698.1 46.9 %collective-permute-start.130 = (bf16[512,1024]{1,0:T(8,128)(2,1)S(1)}, bf16[512,1024]{1,0:T(8,128)(2,1)}, u32[]{:S(2)}, u32[]{:S(2)}) collective-permute-start(bf16[512,1024]{1,0:T(8,128)(2,1)S(1)} %get-tuple-element.432), channel_id=1, source_target_pairs={{1,0},{2,1},{3,2},{5,4},{6,5},{7,6},{9,8},{10,9},{11,10},{13,12},{... | collective-permute-start | bytes 3145736 | tf_op jit(solution)/shard_map/ppermute | solution.py:116
  2699.4 45.6 %collective-permute-start.131 = (bf16[512,1024]{1,0:T(8,128)(2,1)S(1)}, bf16[512,1024]{1,0:T(8,128)(2,1)}, u32[]{:S(2)}, u32[]{:S(2)}) collective-permute-start(bf16[512,1024]{1,0:T(8,128)(2,1)S(1)} %get-tuple-element.433), channel_id=1, source_target_pairs={{0,1},{1,2},{2,3},{4,5},{5,6},{6,7},{8,9},{9,10},{10,11},{12,13},{... | collective-permute-start | bytes 3145736 | tf_op jit(solution)/shard_map/ppermute | solution.py:115
  (372 other events, 5746.8 us)
Sparse Core Ops, SparseCore 0:
  120.2 31.1 all-gather.8
  173.4 82.2 all-gather.14
  257.8 148.1 all-gather.10
  408.0 147.8 all-gather.12
  759.4 23.0 all-gather.16
  1047.8 31.8 reduce-scatter.3
  1126.6 21.9 all-gather.18
  1461.2 30.4 reduce-scatter.5
  1711.7 38.0 reduce-scatter.7

commit v2 on v1

v2 whole, which is shorter than its diff:
```python
import jax
import jax.numpy as jnp
from jax import lax
from jax.experimental import pallas as pl
from jax.experimental.pallas import tpu as pltpu
from jax.sharding import PartitionSpec as P

HEAD_DIM = 64
GROUP = 4
EPSILON = 1e-05
ROPE_THETA = 500000.0
NEGATIVE = -1e30
LANES = 128
CHUNK_ROWS = 512
CHUNK_COLS = 1024
STREAMS = 2
LEAD = 3
AHEAD = 2
ATTEND_AT = 4
LOWER_AT = 14
VMEM = 56 * 1024 * 1024
BF = jnp.bfloat16
F32 = jnp.float32


def mm(left, right):
    return lax.dot_general(left, right, (((1,), (0,)), ((), ())), preferred_element_type=F32)


def mm_tn(left, right):
    return lax.dot_general(left, right, (((0,), (0,)), ((), ())), preferred_element_type=F32)


def mm_nt(left, right):
    return lax.dot_general(left, right, (((1,), (1,)), ((), ())), preferred_element_type=F32)


def rms_inverse(vector):
    return lax.rsqrt(jnp.mean(vector * vector, axis=-1, keepdims=True) + EPSILON)


def turn(tile, cosine, sine, lane):
    swapped = jnp.where(
        lane % HEAD_DIM < HEAD_DIM // 2,
        pltpu.roll(tile, LANES - HEAD_DIM // 2, axis=1),
        pltpu.roll(tile, HEAD_DIM // 2, axis=1),
    )
    return tile * cosine + swapped * sine


def project_kernel(a_ref, w_ref, cos_ref, sin_ref, q_ref, pair_ref):
    step = pl.program_id(0)
    value = mm(a_ref[...], w_ref[...])
    cosine, sine = cos_ref[...], sin_ref[...]
    lane = lax.broadcasted_iota(jnp.int32, cosine.shape, 1)
    tiles = [value[:, at : at + LANES] for at in range(0, value.shape[1], LANES)]

    @pl.when(step < pl.num_programs(0) - 2)
    def _():
        for index, tile in enumerate(tiles):
            q_ref[:, index * LANES : (index + 1) * LANES] = turn(tile, cosine, sine, lane).astype(BF)

    @pl.when(step >= pl.num_programs(0) - 2)
    def _():
        for index, tile in enumerate(tiles):
            if index % 2 == 0:
                tile = turn(tile, cosine, sine, lane)
            pair_ref[:, index * LANES : (index + 1) * LANES] = tile.astype(BF)


def project(a, weights, cosine, sine, key_width):
    rows, width = a.shape
    total = weights.shape[1]
    tile = key_width
    steps = total // tile
    own = pl.BlockSpec((rows, LANES), lambda t: (0, 0))
    return pl.pallas_call(
        project_kernel,
        grid=(steps,),
        in_specs=[
            pl.BlockSpec((rows, width), lambda t: (0, 0)),
            pl.BlockSpec((width, tile), lambda t: (0, t)),
            own,
            own,
        ],
        out_specs=[
            pl.BlockSpec((rows, tile), lambda t: (0, jnp.minimum(t, steps - 3))),
            pl.BlockSpec((rows, tile), lambda t: (0, jnp.maximum(t - (steps - 2), 0))),
        ],
        out_shape=[
            jax.ShapeDtypeStruct((rows, total - 2 * key_width), BF),
            jax.ShapeDtypeStruct((rows, 2 * key_width), BF),
        ],
        compiler_params=pltpu.CompilerParams(vmem_limit_bytes=VMEM),
        cost_estimate=pl.CostEstimate(flops=1, bytes_accessed=1, transcendentals=0),
    )(a, weights, cosine, sine)


def mm(left, right):
    return lax.dot_general(left, right, (((1,), (0,)), ((), ())), preferred_element_type=F32)


def mm_nt(left, right):
    return lax.dot_general(left, right, (((1,), (1,)), ((), ())), preferred_element_type=F32)


def side_by_side(block):
    turned = block.T
    count = block.shape[1] // HEAD_DIM
    return jnp.concatenate(
        [turned[h * HEAD_DIM : (h + 1) * HEAD_DIM] for h in range(count)], axis=1
    )


def stacked(block):
    count = block.shape[1] // HEAD_DIM
    return jnp.concatenate(
        [block[:, h * HEAD_DIM : (h + 1) * HEAD_DIM] for h in range(count)], axis=0
    )


def causal_scores(keys, queries_t, rows, blocks):
    scores = mm(keys, queries_t)
    tail = scores[(blocks - 1) * rows :]
    key_at = lax.broadcasted_iota(jnp.int32, tail.shape, 0)
    query_at = lax.broadcasted_iota(jnp.int32, tail.shape, 1) % rows
    tail = jnp.where(key_at <= query_at, tail, NEGATIVE)
    if blocks == 1:
        return tail
    return jnp.concatenate([scores[: (blocks - 1) * rows], tail], axis=0)


def attend_kernel(shard_ref, q_ref, kv_ref, o_ref, lse_ref):
    rows = q_ref.shape[0]
    span = GROUP * HEAD_DIM
    pair = 2 * HEAD_DIM
    for blocks in range(1, kv_ref.shape[0] // rows + 1):

        @pl.when(shard_ref[0] == blocks - 1)
        def _():
            for half in range(2):
                at = half * HEAD_DIM
                queries = q_ref[:, half * span : (half + 1) * span]
                keys = kv_ref[: blocks * rows, at : at + HEAD_DIM]
                values = kv_ref[: blocks * rows, pair + at : pair + at + HEAD_DIM]
                queries_t = side_by_side(queries) * jnp.asarray(HEAD_DIM**-0.5, BF)
                scores = causal_scores(keys, queries_t, rows, blocks)
                top = jnp.max(scores, axis=0, keepdims=True)
                weights = jnp.exp(scores - top)
                total = jnp.sum(weights, axis=0, keepdims=True)
                out_t = mm(values.T, weights.astype(BF)) / total
                out_t = jnp.concatenate(
                    [out_t[:, h * rows : (h + 1) * rows] for h in range(GROUP)], axis=0
                )
                o_ref[:, half * span : (half + 1) * span] = out_t.T.astype(BF)
                lse_ref[0, half : half + 1, :] = top + jnp.log(total)


def attend(shard, queries, pairs):
    rows, width = queries.shape
    length, pair_width = pairs.shape
    steps = pair_width // (4 * HEAD_DIM)
    span = 2 * GROUP * HEAD_DIM
    return pl.pallas_call(
        attend_kernel,
        grid_spec=pltpu.PrefetchScalarGridSpec(
            num_scalar_prefetch=1,
            grid=(steps,),
            in_specs=[
                pl.BlockSpec((rows, span), lambda p, s: (0, p)),
                pl.BlockSpec((length, 4 * HEAD_DIM), lambda p, s: (0, p)),
            ],
            out_specs=[
                pl.BlockSpec((rows, span), lambda p, s: (0, p)),
                pl.BlockSpec((1, 2, GROUP * rows), lambda p, s: (p, 0, 0)),
            ],
        ),
        out_shape=[
            jax.ShapeDtypeStruct((rows, width), BF),
            jax.ShapeDtypeStruct((steps, 2, GROUP * rows), F32),
        ],
        compiler_params=pltpu.CompilerParams(vmem_limit_bytes=VMEM),
        cost_estimate=pl.CostEstimate(flops=1, bytes_accessed=1, transcendentals=0),
    )(shard, queries, pairs)


def attend_back_kernel(
    shard_ref, q_ref, kv_ref, lse_ref, do_ref, cos_ref, sin_ref, kcos_ref, ksin_ref, dq_ref, dkv_ref
):
    rows = q_ref.shape[0]
    span = GROUP * HEAD_DIM
    pair = 2 * HEAD_DIM
    wide = HEAD_DIM // 2
    scale = HEAD_DIM**-0.5
    for blocks in range(1, kv_ref.shape[0] // rows + 1):

        @pl.when(shard_ref[0] == blocks - 1)
        def _():
            seen = blocks * rows
            key_grads = []
            for half in range(2):
                at = half * HEAD_DIM
                queries = q_ref[:, half * span : (half + 1) * span]
                grads = do_ref[:, half * span : (half + 1) * span]
                keys = kv_ref[:seen, at : at + HEAD_DIM]
                values = kv_ref[:seen, pair + at : pair + at + HEAD_DIM]
                queries_t = side_by_side(queries) * jnp.asarray(scale, BF)
                grads_t = side_by_side(grads)
                scores = causal_scores(keys, queries_t, rows, blocks)
                weights = jnp.exp(scores - lse_ref[0, half : half + 1, :])
                moved = mm(values, grads_t)
                product = weights * moved
                delta = jnp.sum(product, axis=0, keepdims=True)
                grad_scores = (product - weights * delta).astype(BF)
                dkv_ref[:seen, pair + at : pair + at + HEAD_DIM] = mm(
                    weights.astype(BF), stacked(grads)
                ).astype(BF)
                key_grads.append(mm(grad_scores, stacked(queries)) * scale)
                grad_t = mm(keys.T, grad_scores) * scale
                turned = []
                for h in range(GROUP):
                    block = grad_t[:, h * rows : (h + 1) * rows]
                    first, second = block[:wide], block[wide:]
                    turned.append(first * cos_ref[...] + second * sin_ref[...])
                    turned.append(second * cos_ref[...] - first * sin_ref[...])
                dq_ref[:, half * span : (half + 1) * span] = (
                    jnp.concatenate(turned, axis=0).T.astype(BF)
                )
            key_grads = jnp.concatenate(key_grads, axis=1)
            lane = lax.broadcasted_iota(jnp.int32, key_grads.shape, 1)
            dkv_ref[:seen, :pair] = turn(
                key_grads, kcos_ref[:seen, :], -ksin_ref[:seen, :], lane
            ).astype(BF)
            if seen < kv_ref.shape[0]:
                dkv_ref[seen:, :] = jnp.zeros((kv_ref.shape[0] - seen, 2 * pair), BF)


def attend_back(shard, queries, pairs, lse, grads, cosine, sine, key_cosine, key_sine):
    rows, width = queries.shape
    length, pair_width = pairs.shape
    steps = pair_width // (4 * HEAD_DIM)
    span = 2 * GROUP * HEAD_DIM
    table = pl.BlockSpec((HEAD_DIM // 2, rows), lambda p, s: (0, 0))
    key_table = pl.BlockSpec((length, LANES), lambda p, s: (0, 0))
    return pl.pallas_call(
        attend_back_kernel,
        grid_spec=pltpu.PrefetchScalarGridSpec(
            num_scalar_prefetch=1,
            grid=(steps,),
            in_specs=[
                pl.BlockSpec((rows, span), lambda p, s: (0, p)),
                pl.BlockSpec((length, 4 * HEAD_DIM), lambda p, s: (0, p)),
                pl.BlockSpec((1, 2, GROUP * rows), lambda p, s: (p, 0, 0)),
                pl.BlockSpec((rows, span), lambda p, s: (0, p)),
                table,
                table,
                key_table,
                key_table,
            ],
            out_specs=[
                pl.BlockSpec((rows, span), lambda p, s: (0, p)),
                pl.BlockSpec((length, 4 * HEAD_DIM), lambda p, s: (0, p)),
            ],
        ),
        out_shape=[
            jax.ShapeDtypeStruct((rows, width), BF),
            jax.ShapeDtypeStruct((length, pair_width), BF),
        ],
        compiler_params=pltpu.CompilerParams(vmem_limit_bytes=VMEM),
        cost_estimate=pl.CostEstimate(flops=1, bytes_accessed=1, transcendentals=0),
    )(shard, queries, pairs, lse, grads, cosine, sine, key_cosine, key_sine)


def widen_kernel(shard_ref, b_ref, *refs):
    gates, ups = refs[:4], refs[4:8]
    z_ref, g_ref, u_ref = refs[8:]
    depth = gates[0].shape[0]
    gate = up = None
    for k in range(4):
        at = pl.multiple_of((shard_ref[0] ^ k) * depth, depth)
        left = b_ref[:, pl.ds(at, depth)]
        g, u = mm(left, gates[k][...]), mm(left, ups[k][...])
        gate, up = (g, u) if gate is None else (gate + g, up + u)
    z_ref[...] = (gate * jax.nn.sigmoid(gate) * up).astype(BF)
    g_ref[...] = gate.astype(BF)
    u_ref[...] = up.astype(BF)


def widen(shard, b, gates, ups, tile=512):
    rows, width = b.shape
    depth, hidden = gates[0].shape
    out = pl.BlockSpec((rows, tile), lambda t, s: (0, t))
    return pl.pallas_call(
        widen_kernel,
        grid_spec=pltpu.PrefetchScalarGridSpec(
            num_scalar_prefetch=1,
            grid=(hidden // tile,),
            in_specs=[pl.BlockSpec((rows, width), lambda t, s: (0, 0))]
            + [pl.BlockSpec((depth, tile), lambda t, s: (0, t))] * 8,
            out_specs=[out] * 3,
        ),
        out_shape=[jax.ShapeDtypeStruct((rows, hidden), BF)] * 3,
        compiler_params=pltpu.CompilerParams(vmem_limit_bytes=VMEM),
        cost_estimate=pl.CostEstimate(flops=1, bytes_accessed=1, transcendentals=0),
    )(shard, b, *gates, *ups)


def narrow_kernel(shard_ref, z_ref, m_ref, *refs):
    lows, highs, y_ref = refs[:4], refs[4:8], refs[8]
    step = pl.program_id(0)
    depth = lows[0].shape[0]

    def one(downs):
        total = m_ref[...]
        for k in range(4):
            at = pl.multiple_of((shard_ref[0] ^ k) * depth, depth)
            total = total + mm(z_ref[:, pl.ds(at, depth)], downs[k][...])
        y_ref[...] = total

    @pl.when(step < pl.num_programs(0) // 2)
    def _():
        one(lows)

    @pl.when(step >= pl.num_programs(0) // 2)
    def _():
        one(highs)


def narrow(shard, z, m, lows, highs, tile=256):
    rows, hidden = z.shape
    depth, half = lows[0].shape
    width = 2 * half
    per = half // tile
    block = pl.BlockSpec((rows, tile), lambda t, s: (0, t))
    low = pl.BlockSpec((depth, tile), lambda t, s: (0, jnp.minimum(t, per - 1)))
    high = pl.BlockSpec((depth, tile), lambda t, s: (0, jnp.maximum(t - per, 0)))
    return pl.pallas_call(
        narrow_kernel,
        grid_spec=pltpu.PrefetchScalarGridSpec(
            num_scalar_prefetch=1,
            grid=(2 * per,),
            in_specs=[pl.BlockSpec((rows, hidden), lambda t, s: (0, 0)), block]
            + [low] * 4
            + [high] * 4,
            out_specs=block,
        ),
        out_shape=jax.ShapeDtypeStruct((rows, width), F32),
        compiler_params=pltpu.CompilerParams(vmem_limit_bytes=VMEM),
        cost_estimate=pl.CostEstimate(flops=1, bytes_accessed=1, transcendentals=0),
    )(shard, z, m, *lows, *highs)


def hidden_back_kernel(shard_ref, dy_ref, g_ref, u_ref, *refs):
    lows, highs, gates, ups = refs[:4], refs[4:8], refs[8:12], refs[12:16]
    dg_ref, du_ref, db_ref, total = refs[16:]
    middle = lows[0].shape[1]
    step = pl.program_id(0)
    per = pl.num_programs(0) // 4
    depth = gates[0].shape[0]

    def one(low, high):
        dz = mm_nt(dy_ref[:, :middle], low[...]) + mm_nt(dy_ref[:, middle:], high[...])
        gate = g_ref[...].astype(F32)
        up = u_ref[...].astype(F32)
        slope = jax.nn.sigmoid(gate)
        dg = (dz * up * slope * (1.0 + gate * (1.0 - slope))).astype(BF)
        du = (dz * gate * slope).astype(BF)
        dg_ref[...] = dg
        du_ref[...] = du
        for k in range(4):
            part = mm_nt(dg, gates[k][...]) + mm_nt(du, ups[k][...])
            at = pl.multiple_of((shard_ref[0] ^ k) * depth, depth)

            @pl.when(step == 0)
            def _():
                total[:, pl.ds(at, depth)] = part

            @pl.when(step > 0)
            def _():
                total[:, pl.ds(at, depth)] += part

    for k in range(4):

        @pl.when(step // per == k)
        def _():
            one(lows[k], highs[k])

    @pl.when(step == pl.num_programs(0) - 1)
    def _():
        db_ref[...] = total[...]


def hidden_back(shard, dy, g, u, lows, highs, gates, ups, tile=512):
    rows, width = dy.shape
    hidden = g.shape[1]
    depth = gates[0].shape[0]
    per = hidden // 4 // tile

    def natural(t, s):
        return (0, (s[0] ^ (t // per)) * per + t % per)

    def piece(k):
        return lambda t, s: (jnp.clip(t - k * per, 0, per - 1), 0)

    cols = pl.BlockSpec((rows, tile), natural)
    whole = pl.BlockSpec((rows, width), lambda t, s: (0, 0))
    return pl.pallas_call(
        hidden_back_kernel,
        grid_spec=pltpu.PrefetchScalarGridSpec(
            num_scalar_prefetch=1,
            grid=(hidden // tile,),
            in_specs=[whole, cols, cols]
            + [pl.BlockSpec((tile, width // 2), piece(k)) for k in (0, 1, 2, 3, 0, 1, 2, 3)]
            + [pl.BlockSpec((depth, tile), natural)] * 8,
            out_specs=[cols, cols, whole],
            scratch_shapes=[pltpu.VMEM((rows, width), F32)],
        ),
        out_shape=[
            jax.ShapeDtypeStruct((rows, hidden), BF),
            jax.ShapeDtypeStruct((rows, hidden), BF),
            jax.ShapeDtypeStruct((rows, width), F32),
        ],
        compiler_params=pltpu.CompilerParams(vmem_limit_bytes=VMEM),
        cost_estimate=pl.CostEstimate(flops=1, bytes_accessed=1, transcendentals=0),
    )(shard, dy, g, u, *lows, *highs, *gates, *ups)


def outer(x, row, parts, column, width, added=None, earlier=None, tile=512):
    per = (CHUNK_COLS if added is not None else width) // tile
    count = width // tile // per
    first = column // tile
    at = row // CHUNK_ROWS
    held = [] if added is None else [added]
    extra = [] if earlier is None else [earlier]

    def kernel(*refs):
        step = pl.program_id(0)
        left = jnp.concatenate([part[...] for part in refs[: len(x)]], axis=1)
        refs = refs[len(x) :]
        right = jnp.concatenate([part[...] for part in refs[: len(parts)]], axis=0)
        value = mm(left, right)
        if held:
            value = value + refs[len(parts)][...].astype(F32)
        for index in range(count):

            @pl.when(step // per == index)
            def _():
                refs[len(parts) + len(held) + len(extra) + index][...] = value.astype(BF)

    def chunk(index):
        return lambda t: (0, jnp.clip(t - index * per, 0, per - 1))

    return pl.pallas_call(
        kernel,
        grid=(count * per,),
        in_specs=[pl.BlockSpec((CHUNK_ROWS, part.shape[1]), lambda t: (at, 0)) for part in x]
        + [pl.BlockSpec((part.shape[0], tile), lambda t: (0, first + t)) for part in parts]
        + [pl.BlockSpec((CHUNK_ROWS, tile), lambda t: (0, t))] * len(held)
        + [pl.BlockSpec(memory_space=pl.ANY)] * len(extra),
        out_specs=[pl.BlockSpec((CHUNK_ROWS, tile), chunk(index)) for index in range(count)],
        out_shape=[jax.ShapeDtypeStruct((CHUNK_ROWS, per * tile), BF)] * count,
        compiler_params=pltpu.CompilerParams(vmem_limit_bytes=VMEM),
        cost_estimate=pl.CostEstimate(flops=1, bytes_accessed=1, transcendentals=0),
    )(*x, *parts, *held, *extra)


def core_swap(x):
    return lax.ppermute(x, "fsdp", [(0, 1), (1, 0), (2, 3), (3, 2)])


def chip_swap(x):
    return lax.ppermute(x, "fsdp", [(0, 2), (2, 0), (1, 3), (3, 1)])


def after(value, other):
    always = lax.axis_index("dp") > -7
    return jnp.where(always, value, other.reshape(-1)[0].astype(value.dtype))


def nothing_kernel(*refs):
    pass


def hold(x, *others):
    anywhere = pl.BlockSpec(memory_space=pl.ANY)
    return pl.pallas_call(
        nothing_kernel,
        in_specs=[anywhere] * (1 + len(others)),
        out_specs=anywhere,
        out_shape=jax.ShapeDtypeStruct(x.shape, x.dtype),
        input_output_aliases={0: 0},
        compiler_params=pltpu.CompilerParams(vmem_limit_bytes=VMEM),
        cost_estimate=pl.CostEstimate(flops=1, bytes_accessed=1, transcendentals=0),
    )(x, *others)


def turned_kernel(shard_ref, *refs):
    for k in range(4):
        refs[4 + k][...] = refs[k][...].T


def turned_blocks(shard, x, tile=512):
    rows, width = x.shape
    per = width // 4 // tile

    def block(k):
        return pl.BlockSpec((rows, tile), lambda t, s: (0, (s[0] ^ k) * per + t))

    return pl.pallas_call(
        turned_kernel,
        grid_spec=pltpu.PrefetchScalarGridSpec(
            num_scalar_prefetch=1,
            grid=(per,),
            in_specs=[block(k) for k in range(4)],
            out_specs=[pl.BlockSpec((tile, rows), lambda t, s: (t, 0))] * 4,
        ),
        out_shape=[jax.ShapeDtypeStruct((width // 4, rows), x.dtype)] * 4,
        compiler_params=pltpu.CompilerParams(vmem_limit_bytes=VMEM),
        cost_estimate=pl.CostEstimate(flops=1, bytes_accessed=1, transcendentals=0),
    )(shard, x, x, x, x)


def column_block(x, index, width):
    return lax.dynamic_slice_in_dim(x, index * width, width, axis=1)


def relay_kernel(names, places, root, place_ref, *refs):
    named = dict(zip(names, refs))
    up_ref, down_ref = refs[-2:]
    place = place_ref[0]

    def read(name):
        return named[name][...].astype(F32) if name in named else 0.0

    own = 0.0
    for name, held_by in places:
        if name not in named:
            continue
        mine = held_by[0] == place
        for position in held_by[1:]:
            mine = mine | (place == position)
        own = jnp.where(mine, named[name][...].astype(F32), own)
    total = own + read("below_held") + read("above_held")
    up = jnp.where(place == root, total, read("below") + jnp.where(place < root, own, 0.0))
    down = jnp.where(place == root, total, read("above") + jnp.where(place > root, own, 0.0))
    up_ref[...] = jnp.broadcast_to(up, up_ref.shape).astype(up_ref.dtype)
    down_ref[...] = jnp.broadcast_to(down, down_ref.shape).astype(down_ref.dtype)


def relay(place, root, places, operands, earlier, shape, kind):
    names = [name for name in operands if operands[name] is not None]
    unique, at = [], {}
    for name in names:
        for index, other in enumerate(unique):
            if operands[name] is other:
                at[name] = index
        if name not in at:
            at[name] = len(unique)
            unique.append(operands[name])
    rows, cols = shape
    tile = rows // 2 if rows >= 256 else rows
    block = pl.BlockSpec((tile, cols), lambda t, s: (t, 0))

    def kernel(place_ref, *refs):
        values = refs[: len(unique)]
        relay_kernel(names, places, root, place_ref, *[values[at[n]] for n in names], *refs[-2:])

    return pl.pallas_call(
        kernel,
        grid_spec=pltpu.PrefetchScalarGridSpec(
            num_scalar_prefetch=1,
            grid=(rows // tile,),
            in_specs=[block] * len(unique) + [pl.BlockSpec(memory_space=pl.ANY)] * len(earlier),
            out_specs=[block, block],
        ),
        out_shape=[jax.ShapeDtypeStruct(shape, kind)] * 2,
        compiler_params=pltpu.CompilerParams(vmem_limit_bytes=VMEM),
        cost_estimate=pl.CostEstimate(flops=1, bytes_accessed=1, transcendentals=0),
    )(place, *unique, *earlier)


def replica_chain(count, make, shape, kind, stream_count=STREAMS, wanted=None):
    peers = lax.axis_size("dp")
    place = lax.axis_index("dp")
    place_vector = place.astype(jnp.int32).reshape(1)
    root = (peers - 1) // 2
    delay = max(root, peers - 1 - root)
    up_pairs = [(i, i + 1) for i in range(peers - 1)]
    down_pairs = [(i + 1, i) for i in range(peers - 1)]
    counts = [len(range(q, count, stream_count)) for q in range(stream_count)]
    streams = [[] for _ in counts]
    ups = [[] for _ in streams]
    downs = [[] for _ in streams]
    sent = [[] for _ in streams]
    order = []
    lags = [
        position if position < root else delay if position == root else peers - 1 - position
        for position in range(peers)
    ]

    def nth(items, index):
        return items[index] if 0 <= index < len(items) else None

    for step in range(max(counts) + 2 * delay):
        for q in range(stream_count):
            if step >= counts[q] + 2 * delay:
                continue
            if wanted is not None and order:
                wanted(len(order), order[-1][0])
            if step < counts[q]:
                before = order[-LEAD][0] if len(order) >= LEAD else None
                streams[q].append(make(q + step * stream_count, before))
            places, operands = [], {}
            for lag in sorted(set(lags)):
                name = f"own{lag}"
                operands[name] = nth(streams[q], step - lag)
                places.append((name, [p for p in range(peers) if lags[p] == lag]))
            operands["below"] = nth(ups[q], step - 1)
            operands["above"] = nth(downs[q], step - 1)
            operands["below_held"] = nth(ups[q], step - 1 - (delay - root))
            operands["above_held"] = nth(downs[q], step - 1 - (delay - (peers - 1 - root)))
            earlier = ()
            if stream_count > 1 and len(order) > stream_count:
                earlier = order[-(stream_count + 1)]
            up, down = relay(place_vector, root, places, operands, earlier, shape, kind)
            sent[q].append((up, down))
            if step < counts[q] + 2 * delay - 1:
                ups[q].append(lax.ppermute(up, "dp", up_pairs))
                downs[q].append(lax.ppermute(down, "dp", down_pairs))
                order.append((ups[q][-1], downs[q][-1]))
    distance = jnp.abs(place - root)
    totals = [None] * count
    for q in range(stream_count):
        for index in range(counts[q]):
            total = None
            for hops in range(delay + 1):
                up, down = sent[q][index + delay + hops]
                value = jnp.where(place >= root, up, down)
                total = value if total is None else jnp.where(distance == hops, value, total)
            totals[q + index * stream_count] = total
    return totals


def body(
    ends, positions, attn_gain, w_query, w_key, w_value, w_out, mlp_gain, w_gate, w_up, w_down
):
    shard = lax.axis_index("fsdp")
    shard_vector = shard.astype(jnp.int32).reshape(1)
    replica = lax.axis_index("dp")
    replicas = lax.axis_size("dp")
    first_section = lax.axis_index("section") == 0
    tok_rows = ends.shape[3]
    model_width = ends.shape[4]
    length = tok_rows * lax.axis_size("fsdp")
    key_width = w_key.shape[2]
    query_width = w_query.shape[2]
    ends_local = ends[0, :, 0]

    gains = lax.all_gather(
        jnp.concatenate([attn_gain, mlp_gain], axis=0), "fsdp", axis=1, tiled=True
    ).astype(F32)
    gain_attn, gain_mlp = gains[0], gains[1]
    places_all = lax.all_gather(positions[:, 0], "fsdp", axis=1, tiled=True)
    start = gain_attn[0] + places_all[0, 0].astype(F32)

    def rotary(micro_first, micro_second):
        places = jnp.where(first_section, places_all[micro_first], places_all[micro_second])
        half = HEAD_DIM // 2
        frequency = jnp.exp(-jnp.log(ROPE_THETA) * 2.0 * jnp.arange(half, dtype=F32) / HEAD_DIM)
        angles = places.astype(F32)[:, None] * frequency[None, :]
        cosine, sine = jnp.cos(angles), jnp.sin(angles)
        own = [lax.dynamic_slice_in_dim(x, shard * tok_rows, tok_rows, 0) for x in (cosine, sine)]
        lanes = LANES // HEAD_DIM
        wide = (
            jnp.tile(cosine, (1, 2 * lanes)),
            jnp.tile(jnp.concatenate([-sine, sine], axis=1), (1, lanes)),
        )
        wide_own = [lax.dynamic_slice_in_dim(x, shard * tok_rows, tok_rows, 0) for x in wide]
        return wide_own, (own[0].T, own[1].T), wide

    table_a = rotary(1, 0)
    table_b = rotary(0, 1)

    def part(x):
        rows = x.shape[0] // replicas
        return lax.dynamic_slice_in_dim(x, replica * rows, rows, axis=0)

    def spread(x):
        return lax.all_gather(x, "dp", axis=0, tiled=True)

    pieces = [w_query[0]]
    for at in range(0, key_width, LANES):
        pieces += [w_key[0, :, at : at + LANES], w_value[0, :, at : at + LANES]]
    own_qkv = jnp.concatenate(pieces, axis=1)
    own_out, own_gate, own_up, own_down = w_out[0], w_gate[0], w_up[0], w_down[0]
    middle = own_gate.shape[1] // 2
    sends = [part(own_gate[:, :middle]), part(own_gate[:, middle:])]
    sends += [part(own_out), own_qkv, part(own_up)]
    got = []
    spreads = []
    for index, send in enumerate(sends):
        send = after(send, (start, *got)[(0, 1, 2, 2, 3)[index]])
        if index == 4:
            send = after(send, spreads[0])
        got.append(chip_swap(send))
        if index != 3:
            spreads.append(spread(got[-1]))
    half = own_down.shape[1] // 2
    other_low = chip_swap(after(own_down[:, :half], got[3]))

    def shards(own, other):
        return (own, core_swap(own), other, core_swap(other))

    def natural(values):
        rows = values[0].shape[0]
        whole = jnp.zeros((4 * rows, values[0].shape[1]), BF)
        for k, value in enumerate(values):
            whole = lax.dynamic_update_slice(whole, value, ((shard ^ k) * rows, 0))
        return whole

    gates = shards(own_gate, jnp.concatenate(spreads[:2], axis=1))
    mat_qkv = natural(shards(own_qkv, got[3]))
    mat_out = natural(shards(own_out, spreads[2]))

    def all_rows(x):
        return shards(x, chip_swap(x))

    def summed_rows(x):
        def rows_of(index):
            return lax.dynamic_slice_in_dim(x, index * tok_rows, tok_rows, 0)

        near = rows_of(shard).astype(F32) + core_swap(rows_of(shard ^ 1)).astype(F32)
        far = rows_of(shard ^ 2).astype(F32) + core_swap(rows_of(shard ^ 3)).astype(F32)
        return (near + chip_swap(far.astype(BF)).astype(F32)).astype(BF)

    def enter(layer_input, table):
        inverse_one = rms_inverse(layer_input)
        normed_attn = (layer_input * inverse_one * gain_attn).astype(BF)
        queries, pairs = project(normed_attn, mat_qkv, *table[0], key_width)
        return inverse_one, normed_attn, queries, natural(all_rows(pairs))

    def middle_part(layer_input, entered, *waits):
        held = shard_vector
        for other in waits:
            held = after(held, other)
        attended, log_totals = attend(held, entered[2], entered[3])
        residual_mid = layer_input + mm(attended, mat_out)
        inverse_two = rms_inverse(residual_mid)
        normed_mlp = (residual_mid * inverse_two * gain_mlp).astype(BF)
        return attended, log_totals, residual_mid, inverse_two, normed_mlp

    def leave(layer_input, entered, halfway):
        inverse_one, normed_attn, queries, pairs_all = entered
        attended, log_totals, residual_mid, inverse_two, normed_mlp = halfway
        hidden_act, gate_pre, up_proj = widen(shard_vector, normed_mlp, gates, ups)
        output = narrow(shard_vector, hidden_act, residual_mid, lows, highs)
        return output, {
            "input": layer_input,
            "inverse_one": inverse_one,
            "a": normed_attn,
            "queries": queries,
            "pairs": pairs_all,
            "log": log_totals,
            "o": attended,
            "mid": residual_mid,
            "inverse_two": inverse_two,
            "b": normed_mlp,
            "gate": gate_pre,
            "up": up_proj,
            "z": hidden_act,
        }

    def back_upper(grad_top, saved):
        grad_gate_pre, grad_up_proj, grad_normed = hidden_back(
            shard_vector, grad_top, saved["gate"], saved["up"], lows, highs, gates, ups
        )
        inverse_two = saved["inverse_two"]
        base_mid = saved["mid"] * inverse_two
        part_gain_mlp = jnp.sum(grad_normed * base_mid, axis=0)
        scaled_grad = grad_normed * gain_mlp
        grad_mid = grad_top.astype(F32) + inverse_two * (
            scaled_grad - base_mid * jnp.mean(scaled_grad * base_mid, axis=-1, keepdims=True)
        )
        attn_grad = grad_mid.astype(BF)
        return grad_gate_pre, grad_up_proj, attn_grad, grad_mid, part_gain_mlp

    def back_attention(upper, saved, table, *waits):
        held = shard_vector
        for other in waits:
            held = after(held, other)
        grad_attended = mm_nt(upper[2], mat_out).astype(BF)
        grad_queries, grad_pairs = attend_back(
            held, saved["queries"], saved["pairs"], saved["log"], grad_attended, *table[1], *table[2]
        )

        def rows_of(index):
            return lax.dynamic_slice_in_dim(grad_pairs, index * tok_rows, tok_rows, 0)

        far = rows_of(shard ^ 2).astype(F32) + core_swap(rows_of(shard ^ 3)).astype(F32)
        far = chip_swap(far.astype(BF))
        near = rows_of(shard).astype(F32) + core_swap(rows_of(shard ^ 1)).astype(F32)
        return grad_queries, near, far

    def back_lower(upper, attention, saved, *waits):
        grad_queries, near, far = attention
        if waits:
            far = hold(far, *waits)
        grad_qkv = jnp.concatenate([grad_queries, (near + far.astype(F32)).astype(BF)], axis=1)
        grad_normed = mm_nt(grad_qkv, mat_qkv)
        base_in = saved["input"] * saved["inverse_one"]
        part_gain_attn = jnp.sum(grad_normed * base_in, axis=0)
        scaled_grad = grad_normed * gain_attn
        grad_in = upper[3] + saved["inverse_one"] * (
            scaled_grad - base_in * jnp.mean(scaled_grad * base_in, axis=-1, keepdims=True)
        )
        return grad_in, grad_qkv, jnp.stack([part_gain_attn, upper[4]])

    def ahead(x):
        return lax.ppermute(x.astype(BF), "section", [(0, 1)])

    def back(x):
        return lax.ppermute(x.astype(BF), "section", [(1, 0)])

    def choose(first, second):
        return jnp.where(first_section, first, second)

    layer_input = ends_local[0].astype(F32)
    entered = enter(layer_input, table_b)
    other_high = chip_swap(after(own_down[:, half:], entered[3]))
    halfway = middle_part(layer_input, entered)
    lows = shards(own_down[:, :half], hold(other_low, halfway[4]))
    ups = shards(own_up, hold(spreads[3], halfway[4], lows[2]))
    highs = shards(own_down[:, half:], hold(other_high, ups[2]))
    output, _ = leave(layer_input, entered, halfway)
    received = ahead(output)
    layer_input = choose(ends_local[1], received).astype(F32)
    entered = enter(layer_input, table_a)
    output_one, saved_a = leave(layer_input, entered, middle_part(layer_input, entered))
    received = ahead(output_one)
    turned_a = turned_blocks(shard_vector, saved_a["z"])
    layer_input = choose(ends_local[0], received).astype(F32)
    entered = enter(layer_input, table_b)
    halfway = middle_part(layer_input, entered, turned_a[0])
    output_two, saved_b = leave(layer_input, entered, halfway)
    turned_b = turned_blocks(shard_vector, saved_b["z"])

    def shares(blocks_a, blocks_b):
        near = (blocks_a[0], blocks_b[0], core_swap(blocks_a[1]), core_swap(blocks_b[1]))
        far = (blocks_a[2], blocks_b[2], core_swap(blocks_a[3]), core_swap(blocks_b[3]))
        return near, far

    def shares_of(name):
        return shares(
            turned_blocks(shard_vector, saved_a[name]), turned_blocks(shard_vector, saved_b[name])
        )

    def chip_rows(first, second):
        return (first, second, core_swap(first), core_swap(second))

    upper = back_upper(ends_local[0], saved_a)
    grad_in, _, _ = back_lower(upper, back_attention(upper, saved_a, table_a), saved_a)
    received = back(grad_in)
    top_b = choose(received, ends_local[1])
    upper_b = back_upper(top_b, saved_b)
    attention = back_attention(upper_b, saved_b, table_b)
    grad_one, grad_qkv_b, gains_b = back_lower(upper_b, attention, saved_b, turned_b[0])
    received = back(grad_one)
    top_a = choose(received, ends_local[0])

    late = {"down": (shares(turned_a, turned_b), chip_rows(top_a, top_b))}
    work = {}

    def begin_last(begun):
        work["upper"] = upper_a = back_upper(after(top_a, begun), saved_a)
        normed = shares_of("b")
        late["gate"] = (normed, chip_rows(upper_a[0], upper_b[0]))
        late["up"] = (normed, chip_rows(upper_a[1], upper_b[1]))
        late["out"] = (shares_of("o"), chip_rows(upper_a[2], upper_b[2]))

    def wanted(sends, last):
        if sends == ATTEND_AT:
            work["attention"] = back_attention(work["upper"], saved_a, table_a, last)
        if sends == LOWER_AT:
            work["done"] = back_lower(work["upper"], work["attention"], saved_a, last)
            late["attn"] = (shares_of("a"), chip_rows(work["done"][1], grad_qkv_b))

    pair = 2 * CHUNK_COLS
    hidden_width = w_gate.shape[2]
    qkv_width = query_width + 2 * key_width
    plan = []
    for row in range(0, w_down.shape[1], CHUNK_ROWS):
        plan += [("down", row, col, pair) for col in range(0, model_width, pair)]
    for name, width in (("gate", hidden_width), ("up", hidden_width), ("out", model_width)):
        plan += [(name, 0, col, pair) for col in range(0, width, pair)]
    plan += [("attn", 0, col, min(pair, qkv_width - col)) for col in range(0, qkv_width, pair)]
    crossed = []
    made = []

    def cross(earlier):
        name, row, col, width = plan[len(crossed)]
        (own, other), parts = late[name]
        (result,) = outer(other, row, parts, col, width, None, earlier)
        crossed.append(chip_swap(result))
        return result

    def make(index, earlier):
        if index == len(made):
            at = index // 2
            ahead_to = min(at + (AHEAD if at > 0 else 1), len(plan) - 1)
            while len(crossed) <= ahead_to and plan[len(crossed)][0] in late:
                result = cross(earlier)
            if index == 0:
                begin_last(result)
                earlier = work["upper"][0]
            name, row, col, width = plan[at]
            (own, other), parts = late[name]
            made.extend(outer(own, row, parts, col, width, crossed[at], earlier))
        return made[index]

    count = sum(width // CHUNK_COLS for _, _, _, width in plan)
    totals = replica_chain(count, make, (CHUNK_ROWS, CHUNK_COLS), BF, wanted=wanted)
    grad_two, _, gains_a = work["done"]

    gains = gains_a + gains_b
    gains = gains + core_swap(gains)
    gains = gains + chip_swap(gains)
    gains = column_block(gains, shard, model_width // 4)
    (gains,) = replica_chain(1, lambda index, earlier: gains, gains.shape, F32, 1)

    def assembled(rows, cols):
        count = (rows // CHUNK_ROWS) * (cols // CHUNK_COLS)
        taken, totals[:] = totals[:count], totals[count:]
        across = cols // CHUNK_COLS
        lines = [
            jnp.concatenate(taken[at : at + across], axis=1) for at in range(0, count, across)
        ]
        return jnp.concatenate(lines, axis=0).astype(F32)

    grad_down = assembled(w_down.shape[1], w_down.shape[2])
    grad_gate = assembled(w_gate.shape[1], w_gate.shape[2])
    grad_up = assembled(w_up.shape[1], w_up.shape[2])
    grad_out = assembled(w_out.shape[1], w_out.shape[2])
    grad_qkv = assembled(w_query.shape[1], mat_qkv.shape[1])
    grad_pairs = [
        grad_qkv[:, at : at + LANES] for at in range(query_width, grad_qkv.shape[1], LANES)
    ]
    boundary = choose(jnp.stack([grad_one, grad_two]), jnp.stack([output_one, output_two]))
    return (
        boundary[None, :, None],
        gains[0][None],
        grad_qkv[:, :query_width][None],
        jnp.concatenate(grad_pairs[::2], axis=1)[None],
        jnp.concatenate(grad_pairs[1::2], axis=1)[None],
        grad_out[None],
        gains[1][None],
        grad_gate[None],
        grad_up[None],
        grad_down[None],
    )


def solution(mesh):
    weight = P("section", "fsdp", None)
    gain = P("section", "fsdp")
    ends = P("section", None, "dp", "fsdp", None)
    return jax.shard_map(
        body,
        mesh=mesh,
        in_specs=(
            ends,
            P(None, "dp", "fsdp"),
            gain,
            weight,
            weight,
            weight,
            weight,
            gain,
            weight,
            weight,
            weight,
        ),
        out_specs=(
            ends,
            gain,
            weight,
            weight,
            weight,
            weight,
            gain,
            weight,
            weight,
            weight,
        ),
        check_vma=False,
    )
```

time: 2800 us -> 2260 us (0.81)
  matrix products: 1040 us -> 69.4 us
  Pallas kernels: 0 us -> 793 us
  other arithmetic: 347 us -> 196 us
  waiting for transfers between devices: 848 us -> 736 us
  local copies, waits for them, and re-layouts: 198 us -> 116 us
  blocking collectives: 62.2 us -> 11.5 us
  starting transfers between devices: 267 us -> 309 us
    dot_general x248 -> x9, matrix products: 1000 us -> 69.4 us  [the longest x6 50.8 us: mm_nt(): lax.dot_general(left, right, (((1,), (1,)), ((), ())), preferred_element_...]
    pallas_call x0 -> x103, Pallas kernels: none -> 793 us  [the longest x30 194 us: outer(): pl.pallas_call(kernel, grid=(count * per,), in_specs=[pl.BlockSpec((CHUNK...]
    concatenate x37 -> x4, other arithmetic: 143 us -> 0.99 us  [the longest x1 0.71 us: body(): jnp.concatenate([attn_gain, mlp_gain], axis=0)]
    all_gather x3 -> x4, waiting for transfers between devices: 158 us -> 31.8 us  [spread(): return lax.all_gather(x, 'dp', axis=0, tiled=True)]
    all_gather x3 -> x2, blocking collectives: 62.2 us -> 11.5 us  [the longest x1 6.14 us: body(): lax.all_gather(jnp.concatenate([attn_gain, mlp_gain], axis=0), 'fsdp', ax...]
    convert_element_type x41 -> x17, other arithmetic: 65.3 us -> 27.7 us  [the longest x2 6.16 us: back_upper(): attn_grad = grad_mid.astype(BF)]
    slice x28 -> x13, local copies, waits for them, and re-layouts: 48.7 us -> 12.4 us  [the longest x1 6.06 us: body(): sends = [part(own_gate[:, :middle]), part(own_gate[:, middle:])]]
    sub x8 -> x0, matrix products: 35.2 us -> none  [attend_group(): exp_scores = jnp.exp(scores - row_max)]
  transfers between devices with their start and end apart: 143 -> 166, of which waited for: 74 -> 65; matrix products, arithmetic and copies ran while one was open for 32% -> 12% of each run, Pallas kernels for 0% -> 24%
where the time goes in v2:
time: 2260 us; the launch traced here: 2250 us
  Pallas kernels  793 us (35%)
  waiting for transfers between devices  736 us (33%)
  starting transfers between devices  309 us (14%)
  other arithmetic  196 us (9%)
  local copies, waits for them, and re-layouts  116 us (5%)
  matrix products  69.4 us (3%)
    ppermute x29, waiting for transfers between devices, chip_swap(): return lax.ppermute(x, 'fsdp', [(0, 2), (2, 0), (1, 3), (3, 1)])  454 us
    pallas_call x30, Pallas kernels, outer(): pl.pallas_call(kernel, grid=(count * per,), in_specs=[pl.BlockSpec((CHUNK...  194 us
    pallas_call x3, Pallas kernels, hidden_back(): pl.pallas_call(hidden_back_kernel, grid_spec=pltpu.PrefetchScalarGridSpec...  170 us
    ppermute x39, starting transfers between devices, replica_chain(): ups[q].append(lax.ppermute(up, 'dp', up_pairs))  157 us
    pallas_call x42, Pallas kernels, relay(): pl.pallas_call(kernel, grid_spec=pltpu.PrefetchScalarGridSpec(num_scalar_...  154 us
    ppermute x39, waiting for transfers between devices, replica_chain(): downs[q].append(lax.ppermute(down, 'dp', down_pairs))  109 us
    pallas_call x3, Pallas kernels, widen(): pl.pallas_call(widen_kernel, grid_spec=pltpu.PrefetchScalarGridSpec(num_s...  103 us
    ppermute x29, starting transfers between devices, chip_swap(): return lax.ppermute(x, 'fsdp', [(0, 2), (2, 0), (1, 3), (3, 1)])  64.3 us
  transfers between devices with their start and end apart: 166, of which 65 were waited for; matrix products, arithmetic and copies ran while one was open for 12% of the time, Pallas kernels for 24%

profile of v2, /device:TPU:0, one launch (start us, length us, event | category | flops | bytes accessed | tf_op | source)
XLA Modules:
  0.0 2251.3 jit_solution(10803193645577771147)
XLA Ops:
  31.8 23.6 %collective-permute-done.1 = bf16[128,4096]{1,0:T(8,128)(2,1)S(1)} collective-permute-done((bf16[128,4096]{1,0:T(8,128)(2,1)S(1)}, bf16[128,4096]{1,0:T(8,128)(2,1)S(1)}, u32[]{:S(2)}, u32[]{:S(2)}) %collective-permute-start.1) | collective-permute-done | bytes 1048608 | tf_op jit(solution)/shard_map/ppermute | solution.py:472
  62.4 22.8 %collective-permute-done.2 = bf16[128,4096]{1,0:T(8,128)(2,1)S(1)} collective-permute-done((bf16[128,4096]{1,0:T(8,128)(2,1)S(1)}, bf16[128,4096]{1,0:T(8,128)(2,1)S(1)}, u32[]{:S(2)}, u32[]{:S(2)}) %collective-permute-start.2) | collective-permute-done | bytes 1048608 | tf_op jit(solution)/shard_map/ppermute | solution.py:472
  99.3 7.0 collective-permute-done.9
  107.4 31.4 %all-gather.8.cloned.1.call-done = bf16[512,4096]{1,0:T(8,128)(2,1)} async-done(((bf16[128,4096]{1,0:T(8,128)(2,1)}), bf16[512,4096]{1,0:T(8,128)(2,1)}) %all-gather.8.cloned.1.call-update) | async-done | bytes 4194320 | tf_op jit(solution)/shard_map/all_gather | solution.py:689
  160.0 34.8 %collective-permute-done.14 = bf16[128,8192]{1,0:T(8,128)(2,1)} collective-permute-done((bf16[128,8192]{1,0:T(8,128)(2,1)S(1)}, bf16[128,8192]{1,0:T(8,128)(2,1)}, u32[]{:S(2)}, u32[]{:S(2)}) %collective-permute-start.14) | collective-permute-done | bytes 2097184 | tf_op jit(solution)/shard_map/ppermute | solution.py:472
  194.9 66.2 %collective-permute-done.3 = bf16[512,3072]{1,0:T(8,128)(2,1)} collective-permute-done((bf16[512,3072]{1,0:T(8,128)(2,1)S(1)}, bf16[512,3072]{1,0:T(8,128)(2,1)}, u32[]{:S(2)}, u32[]{:S(2)}) %collective-permute-start.3) | collective-permute-done | bytes 3145760 | tf_op jit(solution)/shard_map/ppermute | solution.py:472
  284.1 10.5 shard_map.186
  300.6 8.6 collective-permute-done.6
  315.2 7.5 broadcast_select_fusion
  343.8 6.9 shard_map.187
  360.3 56.1 %collective-permute-done.15.refs_0_ = bf16[2048,1024]{1,0:T(8,128)(2,1)} collective-permute-done((bf16[2048,1024]{1,0:T(8,128)(2,1)}, bf16[2048,1024]{1,0:T(8,128)(2,1)}, u32[]{:S(2)}, u32[]{:S(2)}) %collective-permute-start.15) | collective-permute-done | bytes 4194336 | tf_op jit(solution)/shard_map/ppermute | solution.py:472
  416.8 89.1 %collective-permute-done.20.refs_0_ = bf16[2048,1024]{1,0:T(8,128)(2,1)} collective-permute-done((bf16[2048,1024]{1,0:T(8,128)(2,1)}, bf16[2048,1024]{1,0:T(8,128)(2,1)}, u32[]{:S(2)}, u32[]{:S(2)}) %collective-permute-start.20) | collective-permute-done | bytes 4194336 | tf_op jit(solution)/shard_map/ppermute | solution.py:472
  506.9 34.3 %shard_map.190 = (bf16[256,8192]{1,0:T(8,128)(2,1)}, bf16[256,8192]{1,0:T(8,128)(2,1)}, bf16[256,8192]{1,0:T(8,128)(2,1)}) custom-call(s32[1]{0:T(128)} %bitcast.2.shard_ref, bf16[256,2048]{1,0:T(8,128)(2,1)} %multiply_convert_fusion.2.refs_1_.b_ref, bf16[512,8192]{1,0:T(8,128)(2,1)} %bitcast.172, bf16[512,8192]{1,0:T(8,128)(2,1)} %collective-permute-done.11.refs_1_.refs_9_, ...), custom_call_target="tpu_custom_call" | custom-call | flops 1 | bytes 1 | tf_op jit(solution)/shard_map/pallas_call | solution.py:293
  541.2 20.4 shard_map.192
  569.8 20.9 collective-permute-done.22
  592.5 10.7 shard_map.193
  604.7 11.7 collective-permute-done.24
  635.8 34.7 %shard_map.195 = (bf16[256,8192]{1,0:T(8,128)(2,1)}, bf16[256,8192]{1,0:T(8,128)(2,1)}, bf16[256,8192]{1,0:T(8,128)(2,1)}) custom-call(s32[1]{0:T(128)} %bitcast.2.shard_ref, bf16[256,2048]{1,0:T(8,128)(2,1)} %multiply_convert_fusion.1.b_ref.refs_0_.refs_1_.refs_2_.refs_3_, bf16[512,8192]{1,0:T(8,128)(2,1)} %bitcast.173, ...), custom_call_target="tpu_custom_call" | custom-call | flops 1 | bytes 1 | tf_op jit(solution)/shard_map/pallas_call | solution.py:293
  670.4 56.6 %shard_map.196 = (bf16[256,8192]{1,0:T(8,128)(2,1)}, bf16[256,8192]{1,0:T(8,128)(2,1)}, f32[256,2048]{1,0:T(8,128)}) custom-call(s32[1]{0:T(128)} %bitcast.2.shard_ref, bf16[256,2048]{1,0:T(8,128)(2,1)} %slice_bitcast_fusion.1.dy_ref, bf16[256,8192]{1,0:T(8,128)(2,1)} %get-tuple-element.192.g_ref, bf16[256,8192]{1,0:T(8,128)(2,1)} %get-tuple-element.193.u_ref, ...), custom_call_target="tpu_custom_call" | custom-call | flops 1 | bytes 1 | tf_op jit(solution)/shard_map/pallas_call | solution.py:407
  729.2 6.8 convolution_convert_fusion.2.do_ref
  736.1 10.5 shard_map.197
  748.8 8.4 collective-permute-start.27
  760.5 17.4 collective-permute-start.28
  777.9 20.4 shard_map.198
  807.9 10.0 fusion.11
  817.9 10.4 collective-permute-done.30
  833.8 10.6 shard_map.200
  844.6 13.0 collective-permute-done.32
  885.7 9.6 collective-permute-done.29
  896.5 34.3 %shard_map.202 = (bf16[256,8192]{1,0:T(8,128)(2,1)}, bf16[256,8192]{1,0:T(8,128)(2,1)}, bf16[256,8192]{1,0:T(8,128)(2,1)}) custom-call(s32[1]{0:T(128)} %bitcast.2.shard_ref, bf16[256,2048]{1,0:T(8,128)(2,1)} %multiply_convert_fusion.b_ref.refs_0_.refs_1_.refs_2_.refs_3_, bf16[512,8192]{1,0:T(8,128)(2,1)} %bitcast.175, ...), custom_call_target="tpu_custom_call" | custom-call | flops 1 | bytes 1 | tf_op jit(solution)/shard_map/pallas_call | solution.py:293
  930.8 57.0 %shard_map.203 = (bf16[256,8192]{1,0:T(8,128)(2,1)}, bf16[256,8192]{1,0:T(8,128)(2,1)}, f32[256,2048]{1,0:T(8,128)}) custom-call(s32[1]{0:T(128)} %bitcast.2.shard_ref, bf16[256,2048]{1,0:T(8,128)(2,1)} %bitcast_select_fusion.dy_ref.refs_5_, bf16[256,8192]{1,0:T(8,128)(2,1)} %get-tuple-element.203.g_ref, bf16[256,8192]{1,0:T(8,128)(2,1)} %get-tuple-element.204.u_ref, ...), custom_call_target="tpu_custom_call" | custom-call | flops 1 | bytes 1 | tf_op jit(solution)/shard_map/pallas_call | solution.py:407
  993.1 7.1 convolution_convert_fusion.1.do_ref
  1000.1 13.3 shard_map.204
  1020.3 10.6 collective-permute-start.36
  1035.9 7.4 collective-permute-done.36.refs_0_
  1045.6 10.5 fusion.28
  1063.1 24.8 %collective-permute-done.37 = bf16[256,2048]{1,0:T(8,128)(2,1)S(1)} collective-permute-done((bf16[256,2048]{1,0:T(8,128)(2,1)S(1)}, bf16[256,2048]{1,0:T(8,128)(2,1)S(1)}, u32[]{:S(2)}, u32[]{:S(2)}) %collective-permute-start.37) | collective-permute-done | bytes 1048608 | tf_op jit(solution)/shard_map/ppermute | solution.py:822
  1109.2 56.6 %shard_map.208 = (bf16[256,8192]{1,0:T(8,128)(2,1)}, bf16[256,8192]{1,0:T(8,128)(2,1)}, f32[256,2048]{1,0:T(8,128)}) custom-call(s32[1]{0:T(128)} %bitcast.2.shard_ref, bf16[256,2048]{1,0:T(8,128)(2,1)} %broadcast_select_fusion.32.dy_ref, bf16[256,8192]{1,0:T(8,128)(2,1)} %get-tuple-element.192.g_ref, bf16[256,8192]{1,0:T(8,128)(2,1)} %get-tuple-element.193.u_ref, ...), custom_call_target="tpu_custom_call" | custom-call | flops 1 | bytes 1 | tf_op jit(solution)/shard_map/pallas_call | solution.py:407
  1199.1 16.1 collective-permute-done.44.refs_8_
  1249.5 10.7 collective-permute-done.60.refs_8_
  1269.6 6.9 shard_map.219
  1287.9 7.4 collective-permute-done.61.refs_4_.refs_7_
  1310.4 7.1 shard_map.226
  1386.3 8.7 collective-permute-done.76.refs_8_
  1406.2 14.3 collective-permute-done.79.refs_7_.refs_4_
  1421.8 6.9 shard_map.233
  1473.3 6.8 shard_map.231
  1497.5 10.4 shard_map.215
  1520.3 10.4 collective-permute-start.104
  1542.3 7.0 shard_map.251
  1559.3 28.8 %collective-permute-done.53.refs_0_ = bf16[256,1024]{1,0:T(8,128)(2,1)S(1)} collective-permute-done((bf16[256,1024]{1,0:T(8,128)(2,1)S(1)}, bf16[256,1024]{1,0:T(8,128)(2,1)S(1)}, u32[]{:S(2)}, u32[]{:S(2)}) %collective-permute-start.53) | collective-permute-done | bytes 524320 | tf_op jit(solution)/shard_map/ppermute | solution.py:472
  1620.5 9.7 fusion.21
  1630.3 36.9 %collective-permute-done.112.refs_7_.refs_4_ = bf16[512,1024]{1,0:T(8,128)(2,1)S(1)} collective-permute-done((bf16[512,1024]{1,0:T(8,128)(2,1)S(1)}, bf16[512,1024]{1,0:T(8,128)(2,1)S(1)}, u32[]{:S(2)}, u32[]{:S(2)}) %collective-permute-start.112) | collective-permute-done | bytes 1048608 | tf_op jit(solution)/shard_map/ppermute | solution.py:629
  1667.2 7.2 shard_map.249
  1683.3 20.4 shard_map.239
  1717.1 41.1 %collective-permute-done.86 = f32[2,2048]{1,0:T(2,128)S(1)} collective-permute-done((f32[2,2048]{1,0:T(2,128)S(1)}, f32[2,2048]{1,0:T(2,128)S(1)}, u32[]{:S(2)}, u32[]{:S(2)}) %collective-permute-start.86) | collective-permute-done | bytes 16416 | tf_op jit(solution)/shard_map/ppermute | solution.py:472
  1830.9 7.1 shard_map.256
  1899.0 10.1 maximum_convert_fusion
  1909.0 6.9 shard_map.269
  1953.1 6.9 shard_map.267
  1959.9 10.4 collective-permute-done.137.refs_6_.refs_3_.refs_5_
  2136.0 11.8 convert_element_type.265
  2182.1 11.7 convert_element_type.266
  2220.3 10.1 collective-permute-done.160.refs_0_
  (985 shorter events, 1007.2 us)
Async XLA Ops:
  7.2 131.6 %all-gather.8.cloned.1.call-start = ((), (), s32[]{:S(2)}) async-start(), calls=%async_computation.1 | async-start | bytes 5242880 | tf_op jit(solution)/shard_map/all_gather | solution.py:689
  56.4 268.1 %all-gather.10.cloned.1.call-start = ((), (), s32[]{:S(2)}) async-start(), calls=%async_computation.2 | async-start | bytes 5242880 | tf_op jit(solution)/shard_map/all_gather | solution.py:689
  86.3 243.0 %all-gather.6.cloned.1.call-start = ((), (), s32[]{:S(2)}) async-start(), calls=%async_computation | async-start | bytes 2621440 | tf_op jit(solution)/shard_map/all_gather | solution.py:689
  107.1 309.6 %all-gather.12.cloned.1.call-start = ((), (), s32[]{:S(2)}) async-start(), calls=%async_computation.3 | async-start | bytes 10485760 | tf_op jit(solution)/shard_map/all_gather | solution.py:689
  146.1 48.7 %collective-permute-start.14 = (bf16[128,8192]{1,0:T(8,128)(2,1)S(1)}, bf16[128,8192]{1,0:T(8,128)(2,1)}, u32[]{:S(2)}, u32[]{:S(2)}) collective-permute-start(bf16[128,8192]{1,0:T(8,128)(2,1)S(1)} %select_bitcast_fusion), channel_id=1, source_target_pairs={{0,8},{8,0},{4,12},{12,4},{1,9},{9,1},{5,13},{13,5},{2,10},{10,2},... | collective-permute-start | bytes 6291464 | tf_op jit(solution)/shard_map/ppermute | solution.py:472
  159.5 101.6 %collective-permute-start.3 = (bf16[512,3072]{1,0:T(8,128)(2,1)S(1)}, bf16[512,3072]{1,0:T(8,128)(2,1)}, u32[]{:S(2)}, u32[]{:S(2)}) collective-permute-start(bf16[512,3072]{1,0:T(8,128)(2,1)S(1)} %get-tuple-element.438), channel_id=1, source_target_pairs={{0,8},{8,0},{4,12},{12,4},{1,9},{9,1},{5,13},{13,5},{2,10},{10,2},... | collective-permute-start | bytes 9437192 | tf_op jit(solution)/shard_map/ppermute | solution.py:472
  194.9 77.4 %collective-permute-start = (bf16[512,3072]{1,0:T(8,128)(2,1)}, bf16[512,3072]{1,0:T(8,128)(2,1)}, u32[]{:S(2)}, u32[]{:S(2)}) collective-permute-start(bf16[512,3072]{1,0:T(8,128)(2,1)} %bitcast_dynamic-update-slice_fusion.17), channel_id=1, source_target_pairs={{0,4},{4,0},{8,12},{12,8},{1,5},{5,1},{9,13},{13,9},{2,6},{6,2},{1... | collective-permute-start | bytes 9437192 | tf_op jit(solution)/shard_map/ppermute | solution.py:468
  296.2 209.7 %collective-permute-start.11 = (bf16[512,8192]{1,0:T(8,128)(2,1)}, bf16[512,8192]{1,0:T(8,128)(2,1)}, u32[]{:S(2)}, u32[]{:S(2)}) collective-permute-start(bf16[512,8192]{1,0:T(8,128)(2,1)} %bitcast.171), channel_id=1, source_target_pairs={{0,4},{4,0},{8,12},{12,8},{1,5},{5,1},{9,13},{13,9},{2,6},{6,2},{1... | collective-permute-start | bytes 25165832 | tf_op jit(solution)/shard_map/ppermute | solution.py:468
  296.7 209.7 %collective-permute-start.13 = (bf16[512,8192]{1,0:T(8,128)(2,1)}, bf16[512,8192]{1,0:T(8,128)(2,1)}, u32[]{:S(2)}, u32[]{:S(2)}) collective-permute-start(bf16[512,8192]{1,0:T(8,128)(2,1)} %bitcast.178), channel_id=1, source_target_pairs={{0,4},{4,0},{8,12},{12,8},{1,5},{5,1},{9,13},{13,9},{2,6},{6,2},{1... | collective-permute-start | bytes 25165832 | tf_op jit(solution)/shard_map/ppermute | solution.py:468
  322.7 93.7 %collective-permute-start.15 = (bf16[2048,1024]{1,0:T(8,128)(2,1)}, bf16[2048,1024]{1,0:T(8,128)(2,1)}, u32[]{:S(2)}, u32[]{:S(2)}) collective-permute-start(bf16[2048,1024]{1,0:T(8,128)(2,1)} %get-tuple-element.423), channel_id=1, source_target_pairs={{0,8},{8,0},{4,12},{12,4},{1,9},{9,1},{5,13},{13,5},{2,10},{10,2},... | collective-permute-start | bytes 12582920 | tf_op jit(solution)/shard_map/ppermute | solution.py:472
  329.2 177.2 %collective-permute-start.12 = (bf16[512,8192]{1,0:T(8,128)(2,1)}, bf16[512,8192]{1,0:T(8,128)(2,1)}, u32[]{:S(2)}, u32[]{:S(2)}) collective-permute-start(bf16[512,8192]{1,0:T(8,128)(2,1)} %constant_dynamic-update-slice_fusion.refs_2_.refs_10_), channel_id=1, source_target_pairs={{0,4},{4,0},{8,12},{12,8},{1,5},{5,1},{9,13},{13,9},{2,6},{6,2},{1... | collective-permute-start | bytes 25165832 | tf_op jit(solution)/shard_map/ppermute | solution.py:468
  343.6 162.3 %collective-permute-start.20 = (bf16[2048,1024]{1,0:T(8,128)(2,1)}, bf16[2048,1024]{1,0:T(8,128)(2,1)}, u32[]{:S(2)}, u32[]{:S(2)}) collective-permute-start(bf16[2048,1024]{1,0:T(8,128)(2,1)} %get-tuple-element.420), channel_id=1, source_target_pairs={{0,8},{8,0},{4,12},{12,4},{1,9},{9,1},{5,13},{13,5},{2,10},{10,2},... | collective-permute-start | bytes 12582920 | tf_op jit(solution)/shard_map/ppermute | solution.py:472
  416.7 90.2 %collective-permute-start.16 = (bf16[512,8192]{1,0:T(8,128)(2,1)}, bf16[512,8192]{1,0:T(8,128)(2,1)}, u32[]{:S(2)}, u32[]{:S(2)}) collective-permute-start(bf16[512,8192]{1,0:T(8,128)(2,1)} %shard_map.189.refs_6_.refs_1_.refs_14_), channel_id=1, source_target_pairs={{0,4},{4,0},{8,12},{12,8},{1,5},{5,1},{9,13},{13,9},{2,6},{6,2},{1... | collective-permute-start | bytes 25165832 | tf_op jit(solution)/shard_map/ppermute | solution.py:468
  757.2 48.5 %collective-permute-start.26 = (bf16[256,1024]{1,0:T(8,128)(2,1)}, bf16[256,1024]{1,0:T(8,128)(2,1)S(1)}, u32[]{:S(2)}, u32[]{:S(2)}) collective-permute-start(bf16[256,1024]{1,0:T(8,128)(2,1)} %get-tuple-element.445), channel_id=1, source_target_pairs={{0,4},{4,0},{8,12},{12,8},{1,5},{5,1},{9,13},{13,9},{2,6},{6,2},{1... | collective-permute-start | bytes 1572872 | tf_op jit(solution)/shard_map/ppermute | solution.py:468
  760.5 45.2 %collective-permute-start.28 = (bf16[256,1024]{1,0:T(8,128)(2,1)}, bf16[256,1024]{1,0:T(8,128)(2,1)}, u32[]{:S(2)}, u32[]{:S(2)}) collective-permute-start(bf16[256,1024]{1,0:T(8,128)(2,1)} %add_convert_fusion.5), channel_id=1, source_target_pairs={{0,8},{8,0},{4,12},{12,4},{1,9},{9,1},{5,13},{13,5},{2,10},{10,2},... | collective-permute-start | bytes 1572872 | tf_op jit(solution)/shard_map/ppermute | solution.py:472
  1062.6 132.5 %collective-permute-start.57 = (bf16[256,8192]{1,0:T(8,128)(2,1)S(1)}, bf16[256,8192]{1,0:T(8,128)(2,1)}, u32[]{:S(2)}, u32[]{:S(2)}) collective-permute-start(bf16[256,8192]{1,0:T(8,128)(2,1)S(1)} %copy-done.1), channel_id=1, source_target_pairs={{0,4},{4,0},{8,12},{12,8},{1,5},{5,1},{9,13},{13,9},{2,6},{6,2},{1... | collective-permute-start | bytes 12582920 | tf_op jit(solution)/shard_map/ppermute | solution.py:468
  1088.1 78.3 %collective-permute-start.42 = (bf16[2048,256]{1,0:T(8,128)(2,1)}, bf16[2048,256]{1,0:T(8,128)(2,1)}, u32[]{:S(2)}, u32[]{:S(2)}) collective-permute-start(bf16[2048,256]{1,0:T(8,128)(2,1)} %get-tuple-element.216), channel_id=1, source_target_pairs={{0,4},{4,0},{8,12},{12,8},{1,5},{5,1},{9,13},{13,9},{2,6},{6,2},{1... | collective-permute-start | bytes 3145736 | tf_op jit(solution)/shard_map/ppermute | solution.py:468
  1106.0 70.9 %collective-permute-start.45 = (bf16[512,2048]{1,0:T(8,128)(2,1)}, bf16[512,2048]{1,0:T(8,128)(2,1)}, u32[]{:S(2)}, u32[]{:S(2)}) collective-permute-start(bf16[512,2048]{1,0:T(8,128)(2,1)} %shard_map.210), channel_id=1, source_target_pairs={{0,8},{8,0},{4,12},{12,4},{1,9},{9,1},{5,13},{13,5},{2,10},{10,2},... | collective-permute-start | bytes 6291464 | tf_op jit(solution)/shard_map/ppermute | solution.py:472
  1165.8 95.7 %collective-permute-start.56 = (bf16[256,8192]{1,0:T(8,128)(2,1)}, bf16[256,8192]{1,0:T(8,128)(2,1)}, u32[]{:S(2)}, u32[]{:S(2)}) collective-permute-start(bf16[256,8192]{1,0:T(8,128)(2,1)} %get-tuple-element.219.refs_9_.refs_4_), channel_id=1, source_target_pairs={{0,4},{4,0},{8,12},{12,8},{1,5},{5,1},{9,13},{13,9},{2,6},{6,2},{1... | collective-permute-start | bytes 12582920 | tf_op jit(solution)/shard_map/ppermute | solution.py:468
  1166.4 48.8 %collective-permute-start.44 = (bf16[512,2048]{1,0:T(8,128)(2,1)}, bf16[512,2048]{1,0:T(8,128)(2,1)}, u32[]{:S(2)}, u32[]{:S(2)}) collective-permute-start(bf16[512,2048]{1,0:T(8,128)(2,1)} %shard_map.207), channel_id=1, source_target_pairs={{0,8},{8,0},{4,12},{12,4},{1,9},{9,1},{5,13},{13,5},{2,10},{10,2},... | collective-permute-start | bytes 6291464 | tf_op jit(solution)/shard_map/ppermute | solution.py:472
  1194.6 65.5 %collective-permute-start.60 = (bf16[512,2048]{1,0:T(8,128)(2,1)}, bf16[512,2048]{1,0:T(8,128)(2,1)}, u32[]{:S(2)}, u32[]{:S(2)}) collective-permute-start(bf16[512,2048]{1,0:T(8,128)(2,1)} %shard_map.218), channel_id=1, source_target_pairs={{0,8},{8,0},{4,12},{12,4},{1,9},{9,1},{5,13},{13,5},{2,10},{10,2},... | collective-permute-start | bytes 6291464 | tf_op jit(solution)/shard_map/ppermute | solution.py:472
  1224.2 80.9 %collective-permute-start.67 = (bf16[512,2048]{1,0:T(8,128)(2,1)}, bf16[512,2048]{1,0:T(8,128)(2,1)}, u32[]{:S(2)}, u32[]{:S(2)}) collective-permute-start(bf16[512,2048]{1,0:T(8,128)(2,1)} %shard_map.225), channel_id=1, source_target_pairs={{0,8},{8,0},{4,12},{12,4},{1,9},{9,1},{5,13},{13,5},{2,10},{10,2},... | collective-permute-start | bytes 6291464 | tf_op jit(solution)/shard_map/ppermute | solution.py:472
  1269.0 81.0 %collective-permute-start.66 = (bf16[512,2048]{1,0:T(8,128)(2,1)}, bf16[512,2048]{1,0:T(8,128)(2,1)}, u32[]{:S(2)}, u32[]{:S(2)}) collective-permute-start(bf16[512,2048]{1,0:T(8,128)(2,1)} %shard_map.223), channel_id=1, source_target_pairs={{0,8},{8,0},{4,12},{12,4},{1,9},{9,1},{5,13},{13,5},{2,10},{10,2},... | collective-permute-start | bytes 6291464 | tf_op jit(solution)/shard_map/ppermute | solution.py:472
  1333.6 61.4 %collective-permute-start.76 = (bf16[512,2048]{1,0:T(8,128)(2,1)}, bf16[512,2048]{1,0:T(8,128)(2,1)}, u32[]{:S(2)}, u32[]{:S(2)}) collective-permute-start(bf16[512,2048]{1,0:T(8,128)(2,1)} %shard_map.232), channel_id=1, source_target_pairs={{0,8},{8,0},{4,12},{12,4},{1,9},{9,1},{5,13},{13,5},{2,10},{10,2},... | collective-permute-start | bytes 6291464 | tf_op jit(solution)/shard_map/ppermute | solution.py:472
  1355.3 129.2 %collective-permute-start.102 = (bf16[256,8192]{1,0:T(8,128)(2,1)S(1)}, bf16[256,8192]{1,0:T(8,128)(2,1)}, u32[]{:S(2)}, u32[]{:S(2)}) collective-permute-start(bf16[256,8192]{1,0:T(8,128)(2,1)S(1)} %copy-done), channel_id=1, source_target_pairs={{0,4},{4,0},{8,12},{12,8},{1,5},{5,1},{9,13},{13,9},{2,6},{6,2},{1... | collective-permute-start | bytes 12582920 | tf_op jit(solution)/shard_map/ppermute | solution.py:468
  1368.8 70.3 %collective-permute-start.65 = (bf16[512,2048]{1,0:T(8,128)(2,1)}, bf16[512,2048]{1,0:T(8,128)(2,1)}, u32[]{:S(2)}, u32[]{:S(2)}) collective-permute-start(bf16[512,2048]{1,0:T(8,128)(2,1)} %shard_map.222), channel_id=1, source_target_pairs={{0,8},{8,0},{4,12},{12,4},{1,9},{9,1},{5,13},{13,5},{2,10},{10,2},... | collective-permute-start | bytes 6291464 | tf_op jit(solution)/shard_map/ppermute | solution.py:472
  1386.3 122.9 %collective-permute-start.101 = (bf16[256,8192]{1,0:T(8,128)(2,1)}, bf16[256,8192]{1,0:T(8,128)(2,1)}, u32[]{:S(2)}, u32[]{:S(2)}) collective-permute-start(bf16[256,8192]{1,0:T(8,128)(2,1)} %get-tuple-element.286.refs_4_), channel_id=1, source_target_pairs={{0,4},{4,0},{8,12},{12,8},{1,5},{5,1},{9,13},{13,9},{2,6},{6,2},{1... | collective-permute-start | bytes 12582920 | tf_op jit(solution)/shard_map/ppermute | solution.py:468
  1401.8 39.5 %collective-permute-start.75 = (bf16[512,1024]{1,0:T(8,128)(2,1)}, bf16[512,1024]{1,0:T(8,128)(2,1)S(1)}, u32[]{:S(2)}, u32[]{:S(2)}) collective-permute-start(bf16[512,1024]{1,0:T(8,128)(2,1)} %get-tuple-element.255), channel_id=1, source_target_pairs={{0,1},{1,2},{2,3},{4,5},{5,6},{6,7},{8,9},{9,10},{10,11},{12,13},{... | collective-permute-start | bytes 3145736 | tf_op jit(solution)/shard_map/ppermute | solution.py:628
  1451.1 88.5 %collective-permute-start.105 = (bf16[512,2048]{1,0:T(8,128)(2,1)}, bf16[512,2048]{1,0:T(8,128)(2,1)}, u32[]{:S(2)}, u32[]{:S(2)}) collective-permute-start(bf16[512,2048]{1,0:T(8,128)(2,1)} %shard_map.250), channel_id=1, source_target_pairs={{0,8},{8,0},{4,12},{12,4},{1,9},{9,1},{5,13},{13,5},{2,10},{10,2},... | collective-permute-start | bytes 6291464 | tf_op jit(solution)/shard_map/ppermute | solution.py:472
  1462.7 56.2 %collective-permute-start.80 = (bf16[512,1024]{1,0:T(8,128)(2,1)}, bf16[512,1024]{1,0:T(8,128)(2,1)}, u32[]{:S(2)}, u32[]{:S(2)}) collective-permute-start(bf16[512,1024]{1,0:T(8,128)(2,1)} %get-tuple-element.262), channel_id=1, source_target_pairs={{0,1},{1,2},{2,3},{4,5},{5,6},{6,7},{8,9},{9,10},{10,11},{12,13},{... | collective-permute-start | bytes 3145736 | tf_op jit(solution)/shard_map/ppermute | solution.py:628
  1468.1 52.2 %collective-permute-start.81 = (bf16[512,1024]{1,0:T(8,128)(2,1)}, bf16[512,1024]{1,0:T(8,128)(2,1)}, u32[]{:S(2)}, u32[]{:S(2)}) collective-permute-start(bf16[512,1024]{1,0:T(8,128)(2,1)} %get-tuple-element.263), channel_id=1, source_target_pairs={{1,0},{2,1},{3,2},{5,4},{6,5},{7,6},{9,8},{10,9},{11,10},{13,12},{... | collective-permute-start | bytes 3145736 | tf_op jit(solution)/shard_map/ppermute | solution.py:629
  1484.5 57.6 %collective-permute-start.107 = (bf16[512,1024]{1,0:T(8,128)(2,1)}, bf16[512,1024]{1,0:T(8,128)(2,1)S(1)}, u32[]{:S(2)}, u32[]{:S(2)}) collective-permute-start(bf16[512,1024]{1,0:T(8,128)(2,1)} %get-tuple-element.292), channel_id=1, source_target_pairs={{0,1},{1,2},{2,3},{4,5},{5,6},{6,7},{8,9},{9,10},{10,11},{12,13},{... | collective-permute-start | bytes 3145736 | tf_op jit(solution)/shard_map/ppermute | solution.py:628
  1520.3 97.5 %collective-permute-start.104 = (bf16[512,2048]{1,0:T(8,128)(2,1)}, bf16[512,2048]{1,0:T(8,128)(2,1)}, u32[]{:S(2)}, u32[]{:S(2)}) collective-permute-start(bf16[512,2048]{1,0:T(8,128)(2,1)} %shard_map.248), channel_id=1, source_target_pairs={{0,8},{8,0},{4,12},{12,4},{1,9},{9,1},{5,13},{13,5},{2,10},{10,2},... | collective-permute-start | bytes 6291464 | tf_op jit(solution)/shard_map/ppermute | solution.py:472
  1535.0 57.9 %collective-permute-start.84 = (bf16[512,1024]{1,0:T(8,128)(2,1)}, bf16[512,1024]{1,0:T(8,128)(2,1)S(1)}, u32[]{:S(2)}, u32[]{:S(2)}) collective-permute-start(bf16[512,1024]{1,0:T(8,128)(2,1)} %get-tuple-element.267), channel_id=1, source_target_pairs={{0,1},{1,2},{2,3},{4,5},{5,6},{6,7},{8,9},{9,10},{10,11},{12,13},{... | collective-permute-start | bytes 3145736 | tf_op jit(solution)/shard_map/ppermute | solution.py:628
  1539.6 53.7 %collective-permute-start.106 = (bf16[512,1024]{1,0:T(8,128)(2,1)}, bf16[512,1024]{1,0:T(8,128)(2,1)S(1)}, u32[]{:S(2)}, u32[]{:S(2)}) collective-permute-start(bf16[512,1024]{1,0:T(8,128)(2,1)} %get-tuple-element.290), channel_id=1, source_target_pairs={{1,0},{2,1},{3,2},{5,4},{6,5},{7,6},{9,8},{10,9},{11,10},{13,12},{... | collective-permute-start | bytes 3145736 | tf_op jit(solution)/shard_map/ppermute | solution.py:629
  1542.2 45.9 %collective-permute-start.53 = (bf16[256,1024]{1,0:T(8,128)(2,1)S(1)}, bf16[256,1024]{1,0:T(8,128)(2,1)S(1)}, u32[]{:S(2)}, u32[]{:S(2)}) collective-permute-start(bf16[256,1024]{1,0:T(8,128)(2,1)S(1)} %add_convert_fusion.1), channel_id=1, source_target_pairs={{0,8},{8,0},{4,12},{12,4},{1,9},{9,1},{5,13},{13,5},{2,10},{10,2},... | collective-permute-start | bytes 1572872 | tf_op jit(solution)/shard_map/ppermute | solution.py:472
  1554.7 64.4 %collective-permute-start.111 = (bf16[512,1024]{1,0:T(8,128)(2,1)}, bf16[512,1024]{1,0:T(8,128)(2,1)S(1)}, u32[]{:S(2)}, u32[]{:S(2)}) collective-permute-start(bf16[512,1024]{1,0:T(8,128)(2,1)} %get-tuple-element.297), channel_id=1, source_target_pairs={{0,1},{1,2},{2,3},{4,5},{5,6},{6,7},{8,9},{9,10},{10,11},{12,13},{... | collective-permute-start | bytes 3145736 | tf_op jit(solution)/shard_map/ppermute | solution.py:628
  1611.4 67.2 %collective-permute-start.129 = (bf16[512,256]{1,0:T(8,128)(2,1)S(1)}, bf16[512,256]{1,0:T(8,128)(2,1)S(1)}, u32[]{:S(2)}, u32[]{:S(2)}) collective-permute-start(bf16[512,256]{1,0:T(8,128)(2,1)S(1)} %copy-done.206), channel_id=1, source_target_pairs={{0,4},{4,0},{8,12},{12,8},{1,5},{5,1},{9,13},{13,9},{2,6},{6,2},{1... | collective-permute-start | bytes 786440 | tf_op jit(solution)/shard_map/ppermute | solution.py:468
  1611.7 146.5 %collective-permute-start.114 = (bf16[512,2048]{1,0:T(8,128)(2,1)}, bf16[512,2048]{1,0:T(8,128)(2,1)}, u32[]{:S(2)}, u32[]{:S(2)}) collective-permute-start(bf16[512,2048]{1,0:T(8,128)(2,1)} %shard_map.257), channel_id=1, source_target_pairs={{0,8},{8,0},{4,12},{12,4},{1,9},{9,1},{5,13},{13,5},{2,10},{10,2},... | collective-permute-start | bytes 6291464 | tf_op jit(solution)/shard_map/ppermute | solution.py:472
  1613.5 96.5 %collective-permute-start.109 = (bf16[512,1024]{1,0:T(8,128)(2,1)}, bf16[512,1024]{1,0:T(8,128)(2,1)S(1)}, u32[]{:S(2)}, u32[]{:S(2)}) collective-permute-start(bf16[512,1024]{1,0:T(8,128)(2,1)} %get-tuple-element.294), channel_id=1, source_target_pairs={{0,1},{1,2},{2,3},{4,5},{5,6},{6,7},{8,9},{9,10},{10,11},{12,13},{... | collective-permute-start | bytes 3145736 | tf_op jit(solution)/shard_map/ppermute | solution.py:628
  1617.8 92.9 %collective-permute-start.110 = (bf16[512,1024]{1,0:T(8,128)(2,1)}, bf16[512,1024]{1,0:T(8,128)(2,1)}, u32[]{:S(2)}, u32[]{:S(2)}) collective-permute-start(bf16[512,1024]{1,0:T(8,128)(2,1)} %get-tuple-element.295), channel_id=1, source_target_pairs={{1,0},{2,1},{3,2},{5,4},{6,5},{7,6},{9,8},{10,9},{11,10},{13,12},{... | collective-permute-start | bytes 3145736 | tf_op jit(solution)/shard_map/ppermute | solution.py:629
  1619.2 48.0 %collective-permute-start.112 = (bf16[512,1024]{1,0:T(8,128)(2,1)S(1)}, bf16[512,1024]{1,0:T(8,128)(2,1)S(1)}, u32[]{:S(2)}, u32[]{:S(2)}) collective-permute-start(bf16[512,1024]{1,0:T(8,128)(2,1)S(1)} %copy-done.143), channel_id=1, source_target_pairs={{1,0},{2,1},{3,2},{5,4},{6,5},{7,6},{9,8},{10,9},{11,10},{13,12},{... | collective-permute-start | bytes 3145736 | tf_op jit(solution)/shard_map/ppermute | solution.py:629
  1679.3 79.4 %collective-permute-start.116 = (bf16[512,1024]{1,0:T(8,128)(2,1)}, bf16[512,1024]{1,0:T(8,128)(2,1)S(1)}, u32[]{:S(2)}, u32[]{:S(2)}) collective-permute-start(bf16[512,1024]{1,0:T(8,128)(2,1)} %get-tuple-element.304), channel_id=1, source_target_pairs={{0,1},{1,2},{2,3},{4,5},{5,6},{6,7},{8,9},{9,10},{10,11},{12,13},{... | collective-permute-start | bytes 3145736 | tf_op jit(solution)/shard_map/ppermute | solution.py:628
  1682.0 81.1 %collective-permute-start.117 = (bf16[512,1024]{1,0:T(8,128)(2,1)}, bf16[512,1024]{1,0:T(8,128)(2,1)}, u32[]{:S(2)}, u32[]{:S(2)}) collective-permute-start(bf16[512,1024]{1,0:T(8,128)(2,1)} %get-tuple-element.305), channel_id=1, source_target_pairs={{1,0},{2,1},{3,2},{5,4},{6,5},{7,6},{9,8},{10,9},{11,10},{13,12},{... | collective-permute-start | bytes 3145736 | tf_op jit(solution)/shard_map/ppermute | solution.py:629
  1710.0 106.5 %collective-permute-start.103 = (bf16[512,2048]{1,0:T(8,128)(2,1)}, bf16[512,2048]{1,0:T(8,128)(2,1)}, u32[]{:S(2)}, u32[]{:S(2)}) collective-permute-start(bf16[512,2048]{1,0:T(8,128)(2,1)} %shard_map.247), channel_id=1, source_target_pairs={{0,8},{8,0},{4,12},{12,4},{1,9},{9,1},{5,13},{13,5},{2,10},{10,2},... | collective-permute-start | bytes 6291464 | tf_op jit(solution)/shard_map/ppermute | solution.py:472
  1710.8 47.5 %collective-permute-start.86 = (f32[2,2048]{1,0:T(2,128)S(1)}, f32[2,2048]{1,0:T(2,128)S(1)}, u32[]{:S(2)}, u32[]{:S(2)}) collective-permute-start(f32[2,2048]{1,0:T(2,128)S(1)} %fusion.66), channel_id=1, source_target_pairs={{0,8},{8,0},{4,12},{12,4},{1,9},{9,1},{5,13},{13,5},{2,10},{10,2},... | collective-permute-start | bytes 49160 | tf_op jit(solution)/shard_map/ppermute | solution.py:472
  1781.2 41.1 %collective-permute-start.120 = (bf16[512,1024]{1,0:T(8,128)(2,1)}, bf16[512,1024]{1,0:T(8,128)(2,1)S(1)}, u32[]{:S(2)}, u32[]{:S(2)}) collective-permute-start(bf16[512,1024]{1,0:T(8,128)(2,1)} %get-tuple-element.309), channel_id=1, source_target_pairs={{0,1},{1,2},{2,3},{4,5},{5,6},{6,7},{8,9},{9,10},{10,11},{12,13},{... | collective-permute-start | bytes 3145736 | tf_op jit(solution)/shard_map/ppermute | solution.py:628
  1785.2 41.3 %collective-permute-start.121 = (bf16[512,1024]{1,0:T(8,128)(2,1)}, bf16[512,1024]{1,0:T(8,128)(2,1)}, u32[]{:S(2)}, u32[]{:S(2)}) collective-permute-start(bf16[512,1024]{1,0:T(8,128)(2,1)} %get-tuple-element.310), channel_id=1, source_target_pairs={{1,0},{2,1},{3,2},{5,4},{6,5},{7,6},{9,8},{10,9},{11,10},{13,12},{... | collective-permute-start | bytes 3145736 | tf_op jit(solution)/shard_map/ppermute | solution.py:629
  1810.8 70.7 %collective-permute-start.131 = (bf16[512,2048]{1,0:T(8,128)(2,1)}, bf16[512,2048]{1,0:T(8,128)(2,1)}, u32[]{:S(2)}, u32[]{:S(2)}) collective-permute-start(bf16[512,2048]{1,0:T(8,128)(2,1)} %shard_map.268), channel_id=1, source_target_pairs={{0,8},{8,0},{4,12},{12,4},{1,9},{9,1},{5,13},{13,5},{2,10},{10,2},... | collective-permute-start | bytes 6291464 | tf_op jit(solution)/shard_map/ppermute | solution.py:472
  1813.1 41.6 %collective-permute-start.118 = (bf16[512,1024]{1,0:T(8,128)(2,1)}, bf16[512,1024]{1,0:T(8,128)(2,1)S(1)}, u32[]{:S(2)}, u32[]{:S(2)}) collective-permute-start(bf16[512,1024]{1,0:T(8,128)(2,1)} %get-tuple-element.306), channel_id=1, source_target_pairs={{0,1},{1,2},{2,3},{4,5},{5,6},{6,7},{8,9},{9,10},{10,11},{12,13},{... | collective-permute-start | bytes 3145736 | tf_op jit(solution)/shard_map/ppermute | solution.py:628
  1816.5 42.8 %collective-permute-start.119 = (bf16[512,1024]{1,0:T(8,128)(2,1)}, bf16[512,1024]{1,0:T(8,128)(2,1)}, u32[]{:S(2)}, u32[]{:S(2)}) collective-permute-start(bf16[512,1024]{1,0:T(8,128)(2,1)} %get-tuple-element.307), channel_id=1, source_target_pairs={{1,0},{2,1},{3,2},{5,4},{6,5},{7,6},{9,8},{10,9},{11,10},{13,12},{... | collective-permute-start | bytes 3145736 | tf_op jit(solution)/shard_map/ppermute | solution.py:629
  1842.4 39.2 %collective-permute-start.133 = (bf16[512,1024]{1,0:T(8,128)(2,1)}, bf16[512,1024]{1,0:T(8,128)(2,1)}, u32[]{:S(2)}, u32[]{:S(2)}) collective-permute-start(bf16[512,1024]{1,0:T(8,128)(2,1)} %get-tuple-element.324), channel_id=1, source_target_pairs={{0,1},{1,2},{2,3},{4,5},{5,6},{6,7},{8,9},{9,10},{10,11},{12,13},{... | collective-permute-start | bytes 3145736 | tf_op jit(solution)/shard_map/ppermute | solution.py:628
  1881.5 43.0 %collective-permute-start.98 = (bf16[256,3072]{1,0:T(8,128)(2,1)S(1)}, bf16[256,3072]{1,0:T(8,128)(2,1)S(1)}, u32[]{:S(2)}, u32[]{:S(2)}) collective-permute-start(bf16[256,3072]{1,0:T(8,128)(2,1)S(1)} %pad_maximum_fusion.refs_5_), channel_id=1, source_target_pairs={{0,4},{4,0},{8,12},{12,8},{1,5},{5,1},{9,13},{13,9},{2,6},{6,2},{1... | collective-permute-start | bytes 4718600 | tf_op jit(solution)/shard_map/ppermute | solution.py:468
  1881.6 54.4 %collective-permute-start.97 = (bf16[256,3072]{1,0:T(8,128)(2,1)S(1)}, bf16[256,3072]{1,0:T(8,128)(2,1)S(1)}, u32[]{:S(2)}, u32[]{:S(2)}) collective-permute-start(bf16[256,3072]{1,0:T(8,128)(2,1)S(1)} %pad_maximum_fusion.1.refs_4_), channel_id=1, source_target_pairs={{0,4},{4,0},{8,12},{12,8},{1,5},{5,1},{9,13},{13,9},{2,6},{6,2},{1... | collective-permute-start | bytes 4718600 | tf_op jit(solution)/shard_map/ppermute | solution.py:468
  1882.1 62.2 %collective-permute-start.130 = (bf16[512,2048]{1,0:T(8,128)(2,1)}, bf16[512,2048]{1,0:T(8,128)(2,1)}, u32[]{:S(2)}, u32[]{:S(2)}) collective-permute-start(bf16[512,2048]{1,0:T(8,128)(2,1)} %shard_map.266), channel_id=1, source_target_pairs={{0,8},{8,0},{4,12},{12,4},{1,9},{9,1},{5,13},{13,5},{2,10},{10,2},... | collective-permute-start | bytes 6291464 | tf_op jit(solution)/shard_map/ppermute | solution.py:472
  1924.5 54.4 %collective-permute-start.135 = (bf16[512,1024]{1,0:T(8,128)(2,1)}, bf16[512,1024]{1,0:T(8,128)(2,1)S(1)}, u32[]{:S(2)}, u32[]{:S(2)}) collective-permute-start(bf16[512,1024]{1,0:T(8,128)(2,1)} %get-tuple-element.326), channel_id=1, source_target_pairs={{0,1},{1,2},{2,3},{4,5},{5,6},{6,7},{8,9},{9,10},{10,11},{12,13},{... | collective-permute-start | bytes 3145736 | tf_op jit(solution)/shard_map/ppermute | solution.py:628
  1929.1 53.2 %collective-permute-start.136 = (bf16[512,1024]{1,0:T(8,128)(2,1)}, bf16[512,1024]{1,0:T(8,128)(2,1)}, u32[]{:S(2)}, u32[]{:S(2)}) collective-permute-start(bf16[512,1024]{1,0:T(8,128)(2,1)} %get-tuple-element.327), channel_id=1, source_target_pairs={{1,0},{2,1},{3,2},{5,4},{6,5},{7,6},{9,8},{10,9},{11,10},{13,12},{... | collective-permute-start | bytes 3145736 | tf_op jit(solution)/shard_map/ppermute | solution.py:629
  1930.4 39.9 %collective-permute-start.137 = (bf16[512,1024]{1,0:T(8,128)(2,1)}, bf16[512,1024]{1,0:T(8,128)(2,1)}, u32[]{:S(2)}, u32[]{:S(2)}) collective-permute-start(bf16[512,1024]{1,0:T(8,128)(2,1)} %get-tuple-element.329), channel_id=1, source_target_pairs={{0,1},{1,2},{2,3},{4,5},{5,6},{6,7},{8,9},{9,10},{10,11},{12,13},{... | collective-permute-start | bytes 3145736 | tf_op jit(solution)/shard_map/ppermute | solution.py:628
  1944.2 60.1 %collective-permute-start.140 = (bf16[512,2048]{1,0:T(8,128)(2,1)}, bf16[512,2048]{1,0:T(8,128)(2,1)}, u32[]{:S(2)}, u32[]{:S(2)}) collective-permute-start(bf16[512,2048]{1,0:T(8,128)(2,1)} %shard_map.275), channel_id=1, source_target_pairs={{0,8},{8,0},{4,12},{12,4},{1,9},{9,1},{5,13},{13,5},{2,10},{10,2},... | collective-permute-start | bytes 6291464 | tf_op jit(solution)/shard_map/ppermute | solution.py:472
  1988.7 39.8 %collective-permute-start.139 = (bf16[512,1024]{1,0:T(8,128)(2,1)}, bf16[512,1024]{1,0:T(8,128)(2,1)S(1)}, u32[]{:S(2)}, u32[]{:S(2)}) collective-permute-start(bf16[512,1024]{1,0:T(8,128)(2,1)} %get-tuple-element.331), channel_id=1, source_target_pairs={{0,1},{1,2},{2,3},{4,5},{5,6},{6,7},{8,9},{9,10},{10,11},{12,13},{... | collective-permute-start | bytes 3145736 | tf_op jit(solution)/shard_map/ppermute | solution.py:628
  1993.4 39.6 %collective-permute-start.145 = (bf16[512,1024]{1,0:T(8,128)(2,1)}, bf16[512,1024]{1,0:T(8,128)(2,1)S(1)}, u32[]{:S(2)}, u32[]{:S(2)}) collective-permute-start(bf16[512,1024]{1,0:T(8,128)(2,1)} %get-tuple-element.338), channel_id=1, source_target_pairs={{1,0},{2,1},{3,2},{5,4},{6,5},{7,6},{9,8},{10,9},{11,10},{13,12},{... | collective-permute-start | bytes 3145736 | tf_op jit(solution)/shard_map/ppermute | solution.py:629
  2004.4 45.5 %collective-permute-start.123 = (bf16[512,1024]{1,0:T(8,128)(2,1)}, bf16[512,1024]{1,0:T(8,128)(2,1)}, u32[]{:S(2)}, u32[]{:S(2)}) collective-permute-start(bf16[512,1024]{1,0:T(8,128)(2,1)} %shard_map.263), channel_id=1, source_target_pairs={{0,8},{8,0},{4,12},{12,4},{1,9},{9,1},{5,13},{13,5},{2,10},{10,2},... | collective-permute-start | bytes 3145736 | tf_op jit(solution)/shard_map/ppermute | solution.py:472
  2104.4 46.7 %collective-permute-start.150 = (bf16[512,1024]{1,0:T(8,128)(2,1)}, bf16[512,1024]{1,0:T(8,128)(2,1)S(1)}, u32[]{:S(2)}, u32[]{:S(2)}) collective-permute-start(bf16[512,1024]{1,0:T(8,128)(2,1)} %get-tuple-element.344), channel_id=1, source_target_pairs={{0,1},{1,2},{2,3},{4,5},{5,6},{6,7},{8,9},{9,10},{10,11},{12,13},{... | collective-permute-start | bytes 3145736 | tf_op jit(solution)/shard_map/ppermute | solution.py:628
  2108.0 43.1 %collective-permute-start.151 = (bf16[512,1024]{1,0:T(8,128)(2,1)}, bf16[512,1024]{1,0:T(8,128)(2,1)}, u32[]{:S(2)}, u32[]{:S(2)}) collective-permute-start(bf16[512,1024]{1,0:T(8,128)(2,1)} %get-tuple-element.345), channel_id=1, source_target_pairs={{1,0},{2,1},{3,2},{5,4},{6,5},{7,6},{9,8},{10,9},{11,10},{13,12},{... | collective-permute-start | bytes 3145736 | tf_op jit(solution)/shard_map/ppermute | solution.py:629
  (315 other events, 6397.0 us)
Sparse Core Ops, SparseCore 0:
  56.5 82.2 all-gather.7
  140.9 79.2 all-gather.9
  222.4 44.4 all-gather.5
  268.3 148.3 all-gather.11

commit v3 on v2

--- a/solution.py
+++ b/solution.py
@@ -15,9 +15,9 @@
 CHUNK_COLS = 1024
 STREAMS = 2
 LEAD = 3
-AHEAD = 2
 ATTEND_AT = 4
-LOWER_AT = 14
+LOWER_AT = 15
+FAR_WITH = 7
 VMEM = 56 * 1024 * 1024
 BF = jnp.bfloat16
 F32 = jnp.float32
@@ -306,60 +306,43 @@
 
 
 def narrow_kernel(shard_ref, z_ref, m_ref, *refs):
-    lows, highs, y_ref = refs[:4], refs[4:8], refs[8]
-    step = pl.program_id(0)
-    depth = lows[0].shape[0]
-
-    def one(downs):
-        total = m_ref[...]
-        for k in range(4):
-            at = pl.multiple_of((shard_ref[0] ^ k) * depth, depth)
-            total = total + mm(z_ref[:, pl.ds(at, depth)], downs[k][...])
-        y_ref[...] = total
-
-    @pl.when(step < pl.num_programs(0) // 2)
-    def _():
-        one(lows)
-
-    @pl.when(step >= pl.num_programs(0) // 2)
-    def _():
-        one(highs)
-
-
-def narrow(shard, z, m, lows, highs, tile=256):
+    downs, y_ref = refs[:4], refs[4]
+    depth = downs[0].shape[0]
+    total = m_ref[...]
+    for k in range(4):
+        at = pl.multiple_of((shard_ref[0] ^ k) * depth, depth)
+        total = total + mm(z_ref[:, pl.ds(at, depth)], downs[k][...])
+    y_ref[...] = total
+
+
+def narrow(shard, z, m, downs, tile=256):
     rows, hidden = z.shape
-    depth, half = lows[0].shape
-    width = 2 * half
-    per = half // tile
+    depth, width = downs[0].shape
     block = pl.BlockSpec((rows, tile), lambda t, s: (0, t))
-    low = pl.BlockSpec((depth, tile), lambda t, s: (0, jnp.minimum(t, per - 1)))
-    high = pl.BlockSpec((depth, tile), lambda t, s: (0, jnp.maximum(t - per, 0)))
     return pl.pallas_call(
         narrow_kernel,
         grid_spec=pltpu.PrefetchScalarGridSpec(
             num_scalar_prefetch=1,
-            grid=(2 * per,),
+            grid=(width // tile,),
             in_specs=[pl.BlockSpec((rows, hidden), lambda t, s: (0, 0)), block]
-            + [low] * 4
-            + [high] * 4,
+            + [pl.BlockSpec((depth, tile), lambda t, s: (0, t))] * 4,
             out_specs=block,
         ),
         out_shape=jax.ShapeDtypeStruct((rows, width), F32),
         compiler_params=pltpu.CompilerParams(vmem_limit_bytes=VMEM),
         cost_estimate=pl.CostEstimate(flops=1, bytes_accessed=1, transcendentals=0),
-    )(shard, z, m, *lows, *highs)
+    )(shard, z, m, *downs)
 
 
 def hidden_back_kernel(shard_ref, dy_ref, g_ref, u_ref, *refs):
-    lows, highs, gates, ups = refs[:4], refs[4:8], refs[8:12], refs[12:16]
-    dg_ref, du_ref, db_ref, total = refs[16:]
-    middle = lows[0].shape[1]
+    downs, gates, ups = refs[:4], refs[4:8], refs[8:12]
+    dg_ref, du_ref, db_ref, total = refs[12:]
     step = pl.program_id(0)
     per = pl.num_programs(0) // 4
     depth = gates[0].shape[0]
 
-    def one(low, high):
-        dz = mm_nt(dy_ref[:, :middle], low[...]) + mm_nt(dy_ref[:, middle:], high[...])
+    def one(down):
+        dz = mm_nt(dy_ref[...], down[...])
         gate = g_ref[...].astype(F32)
         up = u_ref[...].astype(F32)
         slope = jax.nn.sigmoid(gate)
@@ -383,14 +366,14 @@
 
         @pl.when(step // per == k)
         def _():
-            one(lows[k], highs[k])
+            one(downs[k])
 
     @pl.when(step == pl.num_programs(0) - 1)
     def _():
         db_ref[...] = total[...]
 
 
-def hidden_back(shard, dy, g, u, lows, highs, gates, ups, tile=512):
+def hidden_back(shard, dy, g, u, downs, gates, ups, tile=512):
     rows, width = dy.shape
     hidden = g.shape[1]
     depth = gates[0].shape[0]
@@ -410,7 +393,7 @@
             num_scalar_prefetch=1,
             grid=(hidden // tile,),
             in_specs=[whole, cols, cols]
-            + [pl.BlockSpec((tile, width // 2), piece(k)) for k in (0, 1, 2, 3, 0, 1, 2, 3)]
+            + [pl.BlockSpec((tile, width), piece(k)) for k in range(4)]
             + [pl.BlockSpec((depth, tile), natural)] * 8,
             out_specs=[cols, cols, whole],
             scratch_shapes=[pltpu.VMEM((rows, width), F32)],
@@ -422,16 +405,16 @@
         ],
         compiler_params=pltpu.CompilerParams(vmem_limit_bytes=VMEM),
         cost_estimate=pl.CostEstimate(flops=1, bytes_accessed=1, transcendentals=0),
-    )(shard, dy, g, u, *lows, *highs, *gates, *ups)
-
-
-def outer(x, row, parts, column, width, added=None, earlier=None, tile=512):
-    per = (CHUNK_COLS if added is not None else width) // tile
+    )(shard, dy, g, u, *downs, *gates, *ups)
+
+
+def outer(x, row, parts, column, width, added=None, earlier=(), span=0, tile=512):
+    per = (span or width) // tile
     count = width // tile // per
     first = column // tile
     at = row // CHUNK_ROWS
     held = [] if added is None else [added]
-    extra = [] if earlier is None else [earlier]
+    extra = list(earlier)
 
     def kernel(*refs):
         step = pl.program_id(0)
@@ -585,8 +568,6 @@
     place_vector = place.astype(jnp.int32).reshape(1)
     root = (peers - 1) // 2
     delay = max(root, peers - 1 - root)
-    up_pairs = [(i, i + 1) for i in range(peers - 1)]
-    down_pairs = [(i + 1, i) for i in range(peers - 1)]
     counts = [len(range(q, count, stream_count)) for q in range(stream_count)]
     streams = [[] for _ in counts]
     ups = [[] for _ in streams]
@@ -601,6 +582,11 @@
     def nth(items, index):
         return items[index] if 0 <= index < len(items) else None
 
+    def going(position, direction, step):
+        if (root - position) * direction > 0:
+            return step - lags[position]
+        return step - delay - abs(position - root)
+
     for step in range(max(counts) + 2 * delay):
         for q in range(stream_count):
             if step >= counts[q] + 2 * delay:
@@ -608,7 +594,7 @@
             if wanted is not None and order:
                 wanted(len(order), order[-1][0])
             if step < counts[q]:
-                before = order[-LEAD][0] if len(order) >= LEAD else None
+                before = (order[-LEAD][0],) if len(order) >= LEAD else ()
                 streams[q].append(make(q + step * stream_count, before))
             places, operands = [], {}
             for lag in sorted(set(lags)):
@@ -625,6 +611,8 @@
             up, down = relay(place_vector, root, places, operands, earlier, shape, kind)
             sent[q].append((up, down))
             if step < counts[q] + 2 * delay - 1:
+                up_pairs = [(i, i + 1) for i in range(peers - 1) if 0 <= going(i, 1, step) < counts[q]]
+                down_pairs = [(i, i - 1) for i in range(1, peers) if 0 <= going(i, -1, step) < counts[q]]
                 ups[q].append(lax.ppermute(up, "dp", up_pairs))
                 downs[q].append(lax.ppermute(down, "dp", down_pairs))
                 order.append((ups[q][-1], downs[q][-1]))
@@ -694,19 +682,17 @@
     own_qkv = jnp.concatenate(pieces, axis=1)
     own_out, own_gate, own_up, own_down = w_out[0], w_gate[0], w_up[0], w_down[0]
     middle = own_gate.shape[1] // 2
-    sends = [part(own_gate[:, :middle]), part(own_gate[:, middle:])]
-    sends += [part(own_out), own_qkv, part(own_up)]
+    sends = [part(own_gate[:, :middle]), own_qkv, part(own_gate[:, middle:])]
+    sends += [part(own_out), part(own_up)]
     got = []
     spreads = []
     for index, send in enumerate(sends):
-        send = after(send, (start, *got)[(0, 1, 2, 2, 3)[index]])
+        send = after(send, got[-1] if got else start)
         if index == 4:
             send = after(send, spreads[0])
         got.append(chip_swap(send))
-        if index != 3:
+        if index != 1:
             spreads.append(spread(got[-1]))
-    half = own_down.shape[1] // 2
-    other_low = chip_swap(after(own_down[:, :half], got[3]))
 
     def shards(own, other):
         return (own, core_swap(own), other, core_swap(other))
@@ -719,7 +705,7 @@
         return whole
 
     gates = shards(own_gate, jnp.concatenate(spreads[:2], axis=1))
-    mat_qkv = natural(shards(own_qkv, got[3]))
+    mat_qkv = natural(shards(own_qkv, got[1]))
     mat_out = natural(shards(own_out, spreads[2]))
 
     def all_rows(x):
@@ -749,11 +735,12 @@
         normed_mlp = (residual_mid * inverse_two * gain_mlp).astype(BF)
         return attended, log_totals, residual_mid, inverse_two, normed_mlp
 
-    def leave(layer_input, entered, halfway):
+    def leave(layer_input, entered, halfway, widened=None):
         inverse_one, normed_attn, queries, pairs_all = entered
         attended, log_totals, residual_mid, inverse_two, normed_mlp = halfway
-        hidden_act, gate_pre, up_proj = widen(shard_vector, normed_mlp, gates, ups)
-        output = narrow(shard_vector, hidden_act, residual_mid, lows, highs)
+        widened = widened or widen(shard_vector, normed_mlp, gates, ups)
+        hidden_act, gate_pre, up_proj = widened
+        output = narrow(shard_vector, hidden_act, residual_mid, downs)
         return output, {
             "input": layer_input,
             "inverse_one": inverse_one,
@@ -772,7 +759,7 @@
 
     def back_upper(grad_top, saved):
         grad_gate_pre, grad_up_proj, grad_normed = hidden_back(
-            shard_vector, grad_top, saved["gate"], saved["up"], lows, highs, gates, ups
+            shard_vector, grad_top, saved["gate"], saved["up"], downs, gates, ups
         )
         inverse_two = saved["inverse_two"]
         base_mid = saved["mid"] * inverse_two
@@ -797,14 +784,13 @@
             return lax.dynamic_slice_in_dim(grad_pairs, index * tok_rows, tok_rows, 0)
 
         far = rows_of(shard ^ 2).astype(F32) + core_swap(rows_of(shard ^ 3)).astype(F32)
-        far = chip_swap(far.astype(BF))
+        far = far.astype(BF)
         near = rows_of(shard).astype(F32) + core_swap(rows_of(shard ^ 1)).astype(F32)
         return grad_queries, near, far
 
-    def back_lower(upper, attention, saved, *waits):
-        grad_queries, near, far = attention
-        if waits:
-            far = hold(far, *waits)
+    def back_lower(upper, attention, saved, far=None):
+        grad_queries, near, sent = attention
+        far = chip_swap(sent) if far is None else far
         grad_qkv = jnp.concatenate([grad_queries, (near + far.astype(F32)).astype(BF)], axis=1)
         grad_normed = mm_nt(grad_qkv, mat_qkv)
         base_in = saved["input"] * saved["inverse_one"]
@@ -826,11 +812,10 @@
 
     layer_input = ends_local[0].astype(F32)
     entered = enter(layer_input, table_b)
-    other_high = chip_swap(after(own_down[:, half:], entered[3]))
+    other_down = chip_swap(after(after(own_down, got[-1]), entered[3]))
     halfway = middle_part(layer_input, entered)
-    lows = shards(own_down[:, :half], hold(other_low, halfway[4]))
-    ups = shards(own_up, hold(spreads[3], halfway[4], lows[2]))
-    highs = shards(own_down[:, half:], hold(other_high, ups[2]))
+    ups = shards(own_up, hold(spreads[3], halfway[4]))
+    downs = shards(own_down, hold(other_down, halfway[4]))
     output, _ = leave(layer_input, entered, halfway)
     received = ahead(output)
     layer_input = choose(ends_local[1], received).astype(F32)
@@ -863,26 +848,36 @@
     top_b = choose(received, ends_local[1])
     upper_b = back_upper(top_b, saved_b)
     attention = back_attention(upper_b, saved_b, table_b)
-    grad_one, grad_qkv_b, gains_b = back_lower(upper_b, attention, saved_b, turned_b[0])
+    grad_one, grad_qkv_b, gains_b = back_lower(upper_b, attention, saved_b)
     received = back(grad_one)
+    shared = {name: shares_of(name) for name in ("b", "o", "a")}
+    received = hold(received, output_two, *[shared[name][1][0] for name in ("b", "o", "a")])
     top_a = choose(received, ends_local[0])
 
     late = {"down": (shares(turned_a, turned_b), chip_rows(top_a, top_b))}
     work = {}
+    crossed = []
 
     def begin_last(begun):
         work["upper"] = upper_a = back_upper(after(top_a, begun), saved_a)
-        normed = shares_of("b")
-        late["gate"] = (normed, chip_rows(upper_a[0], upper_b[0]))
-        late["up"] = (normed, chip_rows(upper_a[1], upper_b[1]))
-        late["out"] = (shares_of("o"), chip_rows(upper_a[2], upper_b[2]))
+        late["gate"] = (shared["b"], chip_rows(upper_a[0], upper_b[0]))
+        late["up"] = (shared["b"], chip_rows(upper_a[1], upper_b[1]))
+        late["out"] = (shared["o"], chip_rows(upper_a[2], upper_b[2]))
 
     def wanted(sends, last):
         if sends == ATTEND_AT:
             work["attention"] = back_attention(work["upper"], saved_a, table_a, last)
         if sends == LOWER_AT:
-            work["done"] = back_lower(work["upper"], work["attention"], saved_a, last)
-            late["attn"] = (shares_of("a"), chip_rows(work["done"][1], grad_qkv_b))
+            far = crossed[FAR_WITH][CHUNK_ROWS:, : work["attention"][2].shape[1]]
+            work["done"] = back_lower(work["upper"], work["attention"], saved_a, far)
+            late["attn"] = (shared["a"], chip_rows(work["done"][1], grad_qkv_b))
+            gains = work["done"][2] + gains_b
+            gains = (gains + core_swap(gains)).astype(BF)
+            block = model_width // 4
+            own, other = column_block(gains, shard, block), column_block(gains, shard ^ 2, block)
+            gains = own.astype(F32) + chip_swap(other).astype(F32)
+            spare = ((0, CHUNK_ROWS - gains.shape[0]), (0, CHUNK_COLS - block))
+            work["gains"] = jnp.pad(gains, spare).astype(BF)
 
     pair = 2 * CHUNK_COLS
     hidden_width = w_gate.shape[2]
@@ -893,39 +888,40 @@
     for name, width in (("gate", hidden_width), ("up", hidden_width), ("out", model_width)):
         plan += [(name, 0, col, pair) for col in range(0, width, pair)]
     plan += [("attn", 0, col, min(pair, qkv_width - col)) for col in range(0, qkv_width, pair)]
-    crossed = []
     made = []
 
     def cross(earlier):
         name, row, col, width = plan[len(crossed)]
         (own, other), parts = late[name]
         (result,) = outer(other, row, parts, col, width, None, earlier)
+        if len(crossed) == FAR_WITH:
+            far = work["attention"][2]
+            far = jnp.pad(far, ((0, 0), (0, result.shape[1] - far.shape[1])))
+            result = jnp.concatenate([result, far], axis=0)
         crossed.append(chip_swap(result))
         return result
 
     def make(index, earlier):
+        if index == count - 1:
+            return work["gains"]
         if index == len(made):
             at = index // 2
-            ahead_to = min(at + (AHEAD if at > 0 else 1), len(plan) - 1)
-            while len(crossed) <= ahead_to and plan[len(crossed)][0] in late:
-                result = cross(earlier)
             if index == 0:
-                begin_last(result)
-                earlier = work["upper"][0]
+                cross(())
+                begin_last(cross(()))
+                earlier = (work["upper"][0],)
             name, row, col, width = plan[at]
             (own, other), parts = late[name]
-            made.extend(outer(own, row, parts, col, width, crossed[at], earlier))
+            made.extend(outer(own, row, parts, col, width, crossed[at], earlier, CHUNK_COLS))
+        elif len(crossed) < len(plan):
+            cross(earlier)
         return made[index]
 
-    count = sum(width // CHUNK_COLS for _, _, _, width in plan)
+    count = sum(width // CHUNK_COLS for _, _, _, width in plan) + 1
     totals = replica_chain(count, make, (CHUNK_ROWS, CHUNK_COLS), BF, wanted=wanted)
-    grad_two, _, gains_a = work["done"]
-
-    gains = gains_a + gains_b
-    gains = gains + core_swap(gains)
-    gains = gains + chip_swap(gains)
-    gains = column_block(gains, shard, model_width // 4)
-    (gains,) = replica_chain(1, lambda index, earlier: gains, gains.shape, F32, 1)
+    grad_two = work["done"][0]
+
+    gains = totals.pop()[: gains_b.shape[0], : model_width // 4].astype(F32)
 
     def assembled(rows, cols):
         count = (rows // CHUNK_ROWS) * (cols // CHUNK_COLS)
@@ -940,7 +936,7 @@
     grad_gate = assembled(w_gate.shape[1], w_gate.shape[2])
     grad_up = assembled(w_up.shape[1], w_up.shape[2])
     grad_out = assembled(w_out.shape[1], w_out.shape[2])
-    grad_qkv = assembled(w_query.shape[1], mat_qkv.shape[1])
+    grad_qkv = assembled(w_query.shape[1], qkv_width)
     grad_pairs = [
         grad_qkv[:, at : at + LANES] for at in range(query_width, grad_qkv.shape[1], LANES)
     ]

time: 2260 us -> 2180 us (0.965); the launches traced: 2250 us -> 2150 us
  waiting for transfers between devices: 736 us -> 617 us
    ppermute x29 -> x27, waiting for transfers between devices: 454 us -> 220 us  [chip_swap(): return lax.ppermute(x, 'fsdp', [(0, 2), (2, 0), (1, 3), (3, 1)])]
    all_gather x4, waiting for transfers between devices: 31.8 us -> 111 us  [spread(): return lax.all_gather(x, 'dp', axis=0, tiled=True)]
    ppermute x39 -> x36, waiting for transfers between devices: 63.7 us -> 108 us  [replica_chain(): ups[q].append(lax.ppermute(up, 'dp', up_pairs))]
    ppermute x29 -> x27, starting transfers between devices: 64.3 us -> 106 us  [chip_swap(): return lax.ppermute(x, 'fsdp', [(0, 2), (2, 0), (1, 3), (3, 1)])]
    ppermute x2, waiting for transfers between devices: 34.4 us -> 0.01 us  [back(): return lax.ppermute(x.astype(BF), 'section', [(1, 0)])]
    ppermute x39 -> x36, starting transfers between devices: 157 us -> 130 us  [replica_chain(): ups[q].append(lax.ppermute(up, 'dp', up_pairs))]
    ppermute x39 -> x36, waiting for transfers between devices: 109 us -> 120 us  [replica_chain(): downs[q].append(lax.ppermute(down, 'dp', down_pairs))]
    unnamed x445 -> x414, local copies, waits for them, and re-layouts: 43.6 us -> 54 us
  transfers between devices with their start and end apart: 166 -> 156, of which waited for: 65 -> 52; matrix products, arithmetic and copies ran while one was open for 12% -> 13% of each run, Pallas kernels for 24% -> 26%
where the time goes in v3:
time: 2180 us; the launch traced here: 2150 us
  Pallas kernels  785 us (36%)
  waiting for transfers between devices  617 us (28%)
  starting transfers between devices  329 us (15%)
  other arithmetic  199 us (9%)
  local copies, waits for them, and re-layouts  122 us (6%)
  matrix products  63.7 us (3%)
    ppermute x27, waiting for transfers between devices, chip_swap(): return lax.ppermute(x, 'fsdp', [(0, 2), (2, 0), (1, 3), (3, 1)])  220 us
    pallas_call x30, Pallas kernels, outer(): pl.pallas_call(kernel, grid=(count * per,), in_specs=[pl.BlockSpec((CHUNK...  193 us
    pallas_call x3, Pallas kernels, hidden_back(): pl.pallas_call(hidden_back_kernel, grid_spec=pltpu.PrefetchScalarGridSpec...  170 us
    pallas_call x38, Pallas kernels, relay(): pl.pallas_call(kernel, grid_spec=pltpu.PrefetchScalarGridSpec(num_scalar_...  152 us
    ppermute x36, starting transfers between devices, replica_chain(): ups[q].append(lax.ppermute(up, 'dp', up_pairs))  130 us
    ppermute x36, waiting for transfers between devices, replica_chain(): downs[q].append(lax.ppermute(down, 'dp', down_pairs))  120 us
    all_gather x4, waiting for transfers between devices, spread(): return lax.all_gather(x, 'dp', axis=0, tiled=True)  111 us
    ppermute x36, waiting for transfers between devices, replica_chain(): ups[q].append(lax.ppermute(up, 'dp', up_pairs))  108 us
  transfers between devices with their start and end apart: 156, of which 52 were waited for; matrix products, arithmetic and copies ran while one was open for 13% of the time, Pallas kernels for 26%

profile of v3, /device:TPU:0, one launch (start us, length us, event | category | flops | bytes accessed | tf_op | source)
XLA Modules:
  0.0 2147.5 jit_solution(10076898163769057173)
XLA Ops:
  39.8 15.0 collective-permute-done.1
  69.3 67.7 %collective-permute-done.2 = bf16[512,3072]{1,0:T(8,128)(2,1)} collective-permute-done((bf16[512,3072]{1,0:T(8,128)(2,1)S(1)}, bf16[512,3072]{1,0:T(8,128)(2,1)}, u32[]{:S(2)}, u32[]{:S(2)}) %collective-permute-start.2) | collective-permute-done | bytes 3145760 | tf_op jit(solution)/shard_map/ppermute | solution.py:455
  144.0 21.7 %collective-permute-done.8 = bf16[128,4096]{1,0:T(8,128)(2,1)S(1)} collective-permute-done((bf16[128,4096]{1,0:T(8,128)(2,1)S(1)}, bf16[128,4096]{1,0:T(8,128)(2,1)S(1)}, u32[]{:S(2)}, u32[]{:S(2)}) %collective-permute-start.8) | collective-permute-done | bytes 1048608 | tf_op jit(solution)/shard_map/ppermute | solution.py:455
  170.2 9.5 collective-permute-done.9
  204.5 36.0 %collective-permute-done.14 = bf16[128,8192]{1,0:T(8,128)(2,1)} collective-permute-done((bf16[128,8192]{1,0:T(8,128)(2,1)}, bf16[128,8192]{1,0:T(8,128)(2,1)}, u32[]{:S(2)}, u32[]{:S(2)}) %collective-permute-start.14) | collective-permute-done | bytes 2097184 | tf_op jit(solution)/shard_map/ppermute | solution.py:455
  253.1 10.5 shard_map.186
  265.4 12.1 collective-permute-done.5
  285.2 8.7 select_select_fusion
  299.6 15.5 collective-permute-done.7
  322.6 7.3 shard_map.187
  348.9 110.7 %all-gather.12.cloned.1.call-done.refs_0_ = bf16[512,8192]{1,0:T(8,128)(2,1)} async-done(((bf16[128,8192]{1,0:T(8,128)(2,1)}), bf16[512,8192]{1,0:T(8,128)(2,1)}) %all-gather.12.cloned.1.call-update) | async-done | bytes 8388624 | tf_op jit(solution)/shard_map/all_gather | solution.py:677
  459.7 17.1 collective-permute-done.17.refs_0_
  477.3 34.3 %shard_map.189 = (bf16[256,8192]{1,0:T(8,128)(2,1)}, bf16[256,8192]{1,0:T(8,128)(2,1)}, bf16[256,8192]{1,0:T(8,128)(2,1)}) custom-call(s32[1]{0:T(128)} %bitcast.2.shard_ref, bf16[256,2048]{1,0:T(8,128)(2,1)} %multiply_convert_fusion.2.refs_1_.b_ref, bf16[512,8192]{1,0:T(8,128)(2,1)} %bitcast.176, bf16[512,8192]{1,0:T(8,128)(2,1)} %collective-permute-done.11.refs_1_.refs_5_, ...), custom_call_target="tpu_custom_call" | custom-call | flops 1 | bytes 1 | tf_op jit(solution)/shard_map/pallas_call | solution.py:293
  511.6 19.5 shard_map.191
  539.4 20.9 collective-permute-done.19
  562.1 10.5 shard_map.192
  574.1 11.7 collective-permute-done.21
  604.7 34.7 %shard_map.194 = (bf16[256,8192]{1,0:T(8,128)(2,1)}, bf16[256,8192]{1,0:T(8,128)(2,1)}, bf16[256,8192]{1,0:T(8,128)(2,1)}) custom-call(s32[1]{0:T(128)} %bitcast.2.shard_ref, bf16[256,2048]{1,0:T(8,128)(2,1)} %multiply_convert_fusion.1.b_ref.refs_0_.refs_1_.refs_2_.refs_3_, bf16[512,8192]{1,0:T(8,128)(2,1)} %bitcast.177, ...), custom_call_target="tpu_custom_call" | custom-call | flops 1 | bytes 1 | tf_op jit(solution)/shard_map/pallas_call | solution.py:293
  639.3 56.5 %shard_map.195 = (bf16[256,8192]{1,0:T(8,128)(2,1)}, bf16[256,8192]{1,0:T(8,128)(2,1)}, f32[256,2048]{1,0:T(8,128)}) custom-call(s32[1]{0:T(128)} %bitcast.2.shard_ref, bf16[256,2048]{1,0:T(8,128)(2,1)} %slice_bitcast_fusion.1.dy_ref, bf16[256,8192]{1,0:T(8,128)(2,1)} %get-tuple-element.184.g_ref, bf16[256,8192]{1,0:T(8,128)(2,1)} %get-tuple-element.185.u_ref, ...), custom_call_target="tpu_custom_call" | custom-call | flops 1 | bytes 1 | tf_op jit(solution)/shard_map/pallas_call | solution.py:390
  704.9 10.3 shard_map.196
  717.4 8.3 collective-permute-start.24
  729.0 17.4 collective-permute-start.25
  746.4 19.3 shard_map.197
  776.2 7.2 fusion.13
  783.5 13.5 collective-permute-done.27
  802.9 10.5 shard_map.199
  813.7 13.0 collective-permute-done.29
  854.2 34.3 %shard_map.201 = (bf16[256,8192]{1,0:T(8,128)(2,1)}, bf16[256,8192]{1,0:T(8,128)(2,1)}, bf16[256,8192]{1,0:T(8,128)(2,1)}) custom-call(s32[1]{0:T(128)} %bitcast.2.shard_ref, bf16[256,2048]{1,0:T(8,128)(2,1)} %multiply_convert_fusion.b_ref.refs_0_.refs_1_.refs_2_.refs_3_, bf16[512,8192]{1,0:T(8,128)(2,1)} %bitcast.179, ...), custom_call_target="tpu_custom_call" | custom-call | flops 1 | bytes 1 | tf_op jit(solution)/shard_map/pallas_call | solution.py:293
  890.8 56.5 %shard_map.202 = (bf16[256,8192]{1,0:T(8,128)(2,1)}, bf16[256,8192]{1,0:T(8,128)(2,1)}, f32[256,2048]{1,0:T(8,128)}) custom-call(s32[1]{0:T(128)} %bitcast.2.shard_ref, bf16[256,2048]{1,0:T(8,128)(2,1)} %bitcast_select_fusion.dy_ref.refs_5_, bf16[256,8192]{1,0:T(8,128)(2,1)} %get-tuple-element.195.g_ref, bf16[256,8192]{1,0:T(8,128)(2,1)} %get-tuple-element.196.u_ref, ...), custom_call_target="tpu_custom_call" | custom-call | flops 1 | bytes 1 | tf_op jit(solution)/shard_map/pallas_call | solution.py:390
  951.8 7.1 convolution_convert_fusion.1.do_ref
  958.8 12.0 shard_map.203
  972.3 7.3 collective-permute-start.32
  981.4 16.5 collective-permute-start.33
  997.9 12.4 collective-permute-done.33
  1010.6 7.6 fusion.30
  1034.8 19.3 shard_map.204.refs_1_
  1081.2 57.0 %shard_map.211 = (bf16[256,8192]{1,0:T(8,128)(2,1)}, bf16[256,8192]{1,0:T(8,128)(2,1)}, f32[256,2048]{1,0:T(8,128)}) custom-call(s32[1]{0:T(128)} %bitcast.2.shard_ref, bf16[256,2048]{1,0:T(8,128)(2,1)} %broadcast_select_fusion.31.dy_ref, bf16[256,8192]{1,0:T(8,128)(2,1)} %get-tuple-element.184.g_ref, bf16[256,8192]{1,0:T(8,128)(2,1)} %get-tuple-element.185.u_ref, ...), custom_call_target="tpu_custom_call" | custom-call | flops 1 | bytes 1 | tf_op jit(solution)/shard_map/pallas_call | solution.py:390
  1165.7 20.0 collective-permute-done.45.refs_4_.refs_2_.refs_8_.refs_5_
  1224.7 10.5 collective-permute-done.55.refs_8_.refs_6_.refs_3_.refs_5_
  1268.5 7.1 collective-permute-start.60
  1291.5 7.6 collective-permute-start.64
  1321.6 7.5 collective-permute-start.81
  1355.9 10.4 shard_map.218
  1388.1 11.7 collective-permute-start.87
  1418.8 14.7 collective-permute-done.85.refs_7_.refs_4_
  1433.5 11.6 collective-permute-start.69
  1465.9 14.0 collective-permute-done.88.refs_3_.refs_5_.refs_8_.refs_6_
  1507.7 11.6 collective-permute-start.95
  1537.1 12.6 collective-permute-start.102
  1587.2 7.2 shard_map.247
  1681.0 19.7 collective-permute-done.111.refs_9_.refs_3_.refs_5_.refs_6_
  1701.2 12.1 collective-permute-done.106.refs_4_.refs_7_
  1713.6 9.7 fusion.23
  1771.6 13.9 collective-permute-done.108.refs_8_.refs_6_.refs_3_.refs_5_
  1791.4 21.8 %collective-permute-done.114.refs_4_.refs_7_ = bf16[512,1024]{1,0:T(8,128)(2,1)} collective-permute-done((bf16[512,1024]{1,0:T(8,128)(2,1)}, bf16[512,1024]{1,0:T(8,128)(2,1)}, u32[]{:S(2)}, u32[]{:S(2)}) %collective-permute-start.114) | collective-permute-done | bytes 1048608 | tf_op jit(solution)/shard_map/ppermute | solution.py:617
  1815.0 7.1 shard_map.259
  1847.5 9.1 maximum_convert_fusion
  1975.0 8.0 collective-permute-done.132.refs_4_.refs_6_
  1997.4 8.0 collective-permute-done.139.refs_6_.refs_3_
  2015.9 11.7 convert_element_type.286
  2040.7 9.7 collective-permute-done.143.refs_5_.refs_2_
  2060.0 12.8 collective-permute-done.141.refs_2_.refs_4_
  2081.6 12.1 convert_element_type.287
  2106.8 8.0 collective-permute-done.145.refs_1_.refs_4_
  (932 shorter events, 968.1 us)
Async XLA Ops:
  7.2 176.2 %all-gather.8.cloned.1.call-start = ((), (), s32[]{:S(2)}) async-start(), calls=%async_computation.1 | async-start | bytes 5242880 | tf_op jit(solution)/shard_map/all_gather | solution.py:677
  55.7 240.4 %all-gather.6.cloned.1.call-start = ((), (), s32[]{:S(2)}) async-start(), calls=%async_computation | async-start | bytes 2621440 | tf_op jit(solution)/shard_map/all_gather | solution.py:677
  67.5 69.4 %collective-permute-start.2 = (bf16[512,3072]{1,0:T(8,128)(2,1)S(1)}, bf16[512,3072]{1,0:T(8,128)(2,1)}, u32[]{:S(2)}, u32[]{:S(2)}) collective-permute-start(bf16[512,3072]{1,0:T(8,128)(2,1)S(1)} %get-tuple-element.420), channel_id=1, source_target_pairs={{0,8},{8,0},{4,12},{12,4},{1,9},{9,1},{5,13},{13,5},{2,10},{10,2},... | collective-permute-start | bytes 9437192 | tf_op jit(solution)/shard_map/ppermute | solution.py:455
  180.5 161.0 %all-gather.10.cloned.1.call-start = ((), (), s32[]{:S(2)}) async-start(), calls=%async_computation.2 | async-start | bytes 5242880 | tf_op jit(solution)/shard_map/all_gather | solution.py:677
  181.3 278.4 %all-gather.12.cloned.1.call-start = ((), (), s32[]{:S(2)}) async-start(), calls=%async_computation.3 | async-start | bytes 10485760 | tf_op jit(solution)/shard_map/all_gather | solution.py:677
  181.6 60.2 %collective-permute-start = (bf16[512,3072]{1,0:T(8,128)(2,1)}, bf16[512,3072]{1,0:T(8,128)(2,1)}, u32[]{:S(2)}, u32[]{:S(2)}) collective-permute-start(bf16[512,3072]{1,0:T(8,128)(2,1)} %bitcast_dynamic-update-slice_fusion.17), channel_id=1, source_target_pairs={{0,4},{4,0},{8,12},{12,8},{1,5},{5,1},{9,13},{13,9},{2,6},{6,2},{1... | collective-permute-start | bytes 9437192 | tf_op jit(solution)/shard_map/ppermute | solution.py:451
  192.2 48.4 %collective-permute-start.14 = (bf16[128,8192]{1,0:T(8,128)(2,1)}, bf16[128,8192]{1,0:T(8,128)(2,1)}, u32[]{:S(2)}, u32[]{:S(2)}) collective-permute-start(bf16[128,8192]{1,0:T(8,128)(2,1)} %select_bitcast_fusion), channel_id=1, source_target_pairs={{0,8},{8,0},{4,12},{12,4},{1,9},{9,1},{5,13},{13,5},{2,10},{10,2},... | collective-permute-start | bytes 6291464 | tf_op jit(solution)/shard_map/ppermute | solution.py:455
  193.9 55.4 %collective-permute-start.3 = (bf16[512,3072]{1,0:T(8,128)(2,1)}, bf16[512,3072]{1,0:T(8,128)(2,1)}, u32[]{:S(2)}, u32[]{:S(2)}) collective-permute-start(bf16[512,3072]{1,0:T(8,128)(2,1)} %collective-permute-done.2), channel_id=1, source_target_pairs={{0,4},{4,0},{8,12},{12,8},{1,5},{5,1},{9,13},{13,9},{2,6},{6,2},{1... | collective-permute-start | bytes 9437192 | tf_op jit(solution)/shard_map/ppermute | solution.py:451
  293.9 182.8 %collective-permute-start.17 = (bf16[2048,2048]{1,0:T(8,128)(2,1)}, bf16[2048,2048]{1,0:T(8,128)(2,1)}, u32[]{:S(2)}, u32[]{:S(2)}) collective-permute-start(bf16[2048,2048]{1,0:T(8,128)(2,1)} %select_select_fusion), channel_id=1, source_target_pairs={{0,8},{8,0},{4,12},{12,4},{1,9},{9,1},{5,13},{13,5},{2,10},{10,2},... | collective-permute-start | bytes 25165832 | tf_op jit(solution)/shard_map/ppermute | solution.py:455
  295.6 181.2 %collective-permute-start.11 = (bf16[512,8192]{1,0:T(8,128)(2,1)}, bf16[512,8192]{1,0:T(8,128)(2,1)}, u32[]{:S(2)}, u32[]{:S(2)}) collective-permute-start(bf16[512,8192]{1,0:T(8,128)(2,1)} %bitcast.175), channel_id=1, source_target_pairs={{0,4},{4,0},{8,12},{12,8},{1,5},{5,1},{9,13},{13,9},{2,6},{6,2},{1... | collective-permute-start | bytes 25165832 | tf_op jit(solution)/shard_map/ppermute | solution.py:451
  296.1 181.1 %collective-permute-start.13 = (bf16[512,8192]{1,0:T(8,128)(2,1)}, bf16[512,8192]{1,0:T(8,128)(2,1)}, u32[]{:S(2)}, u32[]{:S(2)}) collective-permute-start(bf16[512,8192]{1,0:T(8,128)(2,1)} %bitcast.189), channel_id=1, source_target_pairs={{0,4},{4,0},{8,12},{12,8},{1,5},{5,1},{9,13},{13,9},{2,6},{6,2},{1... | collective-permute-start | bytes 25165832 | tf_op jit(solution)/shard_map/ppermute | solution.py:451
  346.3 131.0 %collective-permute-start.12 = (bf16[512,8192]{1,0:T(8,128)(2,1)}, bf16[512,8192]{1,0:T(8,128)(2,1)}, u32[]{:S(2)}, u32[]{:S(2)}) collective-permute-start(bf16[512,8192]{1,0:T(8,128)(2,1)} %constant_dynamic-update-slice_fusion.refs_2_.refs_6_), channel_id=1, source_target_pairs={{0,4},{4,0},{8,12},{12,8},{1,5},{5,1},{9,13},{13,9},{2,6},{6,2},{1... | collective-permute-start | bytes 25165832 | tf_op jit(solution)/shard_map/ppermute | solution.py:451
  725.8 48.3 %collective-permute-start.23 = (bf16[256,1024]{1,0:T(8,128)(2,1)}, bf16[256,1024]{1,0:T(8,128)(2,1)S(1)}, u32[]{:S(2)}, u32[]{:S(2)}) collective-permute-start(bf16[256,1024]{1,0:T(8,128)(2,1)} %get-tuple-element.427), channel_id=1, source_target_pairs={{0,4},{4,0},{8,12},{12,8},{1,5},{5,1},{9,13},{13,9},{2,6},{6,2},{1... | collective-permute-start | bytes 1572872 | tf_op jit(solution)/shard_map/ppermute | solution.py:451
  729.0 45.1 %collective-permute-start.25 = (bf16[256,1024]{1,0:T(8,128)(2,1)}, bf16[256,1024]{1,0:T(8,128)(2,1)}, u32[]{:S(2)}, u32[]{:S(2)}) collective-permute-start(bf16[256,1024]{1,0:T(8,128)(2,1)} %add_convert_fusion.5), channel_id=1, source_target_pairs={{0,8},{8,0},{4,12},{12,4},{1,9},{9,1},{5,13},{13,5},{2,10},{10,2},... | collective-permute-start | bytes 1572872 | tf_op jit(solution)/shard_map/ppermute | solution.py:455
  835.1 53.3 %collective-permute-start.26 = (bf16[256,2048]{1,0:T(8,128)(2,1)}, bf16[256,2048]{1,0:T(8,128)(2,1)}, u32[]{:S(2)}, u32[]{:S(2)}) collective-permute-start(bf16[256,2048]{1,0:T(8,128)(2,1)} %get-tuple-element.426), channel_id=1, source_target_pairs={{16,0},{17,1},{18,2},{19,3},{20,4},{21,5},{22,6},{23,7},{24,8},{25... | collective-permute-start | bytes 3145736 | tf_op jit(solution)/shard_map/ppermute | solution.py:808
  1068.0 81.5 %collective-permute-start.42 = (bf16[512,2048]{1,0:T(8,128)(2,1)}, bf16[512,2048]{1,0:T(8,128)(2,1)}, u32[]{:S(2)}, u32[]{:S(2)}) collective-permute-start(bf16[512,2048]{1,0:T(8,128)(2,1)} %shard_map.213), channel_id=1, source_target_pairs={{0,8},{8,0},{4,12},{12,4},{1,9},{9,1},{5,13},{13,5},{2,10},{10,2},... | collective-permute-start | bytes 6291464 | tf_op jit(solution)/shard_map/ppermute | solution.py:455
  1076.0 86.5 %collective-permute-start.41 = (bf16[512,2048]{1,0:T(8,128)(2,1)}, bf16[512,2048]{1,0:T(8,128)(2,1)}, u32[]{:S(2)}, u32[]{:S(2)}) collective-permute-start(bf16[512,2048]{1,0:T(8,128)(2,1)} %shard_map.210), channel_id=1, source_target_pairs={{0,8},{8,0},{4,12},{12,4},{1,9},{9,1},{5,13},{13,5},{2,10},{10,2},... | collective-permute-start | bytes 6291464 | tf_op jit(solution)/shard_map/ppermute | solution.py:455
  1076.2 62.5 %collective-permute-start.39 = (bf16[2048,256]{1,0:T(8,128)(2,1)}, bf16[2048,256]{1,0:T(8,128)(2,1)S(1)}, u32[]{:S(2)}, u32[]{:S(2)}) collective-permute-start(bf16[2048,256]{1,0:T(8,128)(2,1)} %get-tuple-element.211), channel_id=1, source_target_pairs={{0,4},{4,0},{8,12},{12,8},{1,5},{5,1},{9,13},{13,9},{2,6},{6,2},{1... | collective-permute-start | bytes 3145736 | tf_op jit(solution)/shard_map/ppermute | solution.py:451
  1076.3 69.1 %collective-permute-start.40 = (bf16[2048,256]{1,0:T(8,128)(2,1)}, bf16[2048,256]{1,0:T(8,128)(2,1)S(1)}, u32[]{:S(2)}, u32[]{:S(2)}) collective-permute-start(bf16[2048,256]{1,0:T(8,128)(2,1)} %get-tuple-element.212), channel_id=1, source_target_pairs={{0,4},{4,0},{8,12},{12,8},{1,5},{5,1},{9,13},{13,9},{2,6},{6,2},{1... | collective-permute-start | bytes 3145736 | tf_op jit(solution)/shard_map/ppermute | solution.py:451
  1076.8 61.4 %collective-permute-start.49 = (bf16[512,256]{1,0:T(8,128)(2,1)S(1)}, bf16[512,256]{1,0:T(8,128)(2,1)S(1)}, u32[]{:S(2)}, u32[]{:S(2)}) collective-permute-start(bf16[512,256]{1,0:T(8,128)(2,1)S(1)} %copy-done.196), channel_id=1, source_target_pairs={{0,4},{4,0},{8,12},{12,8},{1,5},{5,1},{9,13},{13,9},{2,6},{6,2},{1... | collective-permute-start | bytes 786440 | tf_op jit(solution)/shard_map/ppermute | solution.py:451
  1138.2 114.2 %collective-permute-start.52 = (bf16[256,8192]{1,0:T(8,128)(2,1)S(1)}, bf16[256,8192]{1,0:T(8,128)(2,1)}, u32[]{:S(2)}, u32[]{:S(2)}) collective-permute-start(bf16[256,8192]{1,0:T(8,128)(2,1)S(1)} %copy-done.1), channel_id=1, source_target_pairs={{0,4},{4,0},{8,12},{12,8},{1,5},{5,1},{9,13},{13,9},{2,6},{6,2},{1... | collective-permute-start | bytes 12582920 | tf_op jit(solution)/shard_map/ppermute | solution.py:451
  1138.8 116.9 %collective-permute-start.51 = (bf16[256,8192]{1,0:T(8,128)(2,1)}, bf16[256,8192]{1,0:T(8,128)(2,1)}, u32[]{:S(2)}, u32[]{:S(2)}) collective-permute-start(bf16[256,8192]{1,0:T(8,128)(2,1)} %get-tuple-element.214.refs_9_.refs_4_), channel_id=1, source_target_pairs={{0,4},{4,0},{8,12},{12,8},{1,5},{5,1},{9,13},{13,9},{2,6},{6,2},{1... | collective-permute-start | bytes 12582920 | tf_op jit(solution)/shard_map/ppermute | solution.py:451
  1145.4 60.7 %collective-permute-start.57 = (bf16[512,2048]{1,0:T(8,128)(2,1)}, bf16[512,2048]{1,0:T(8,128)(2,1)}, u32[]{:S(2)}, u32[]{:S(2)}) collective-permute-start(bf16[512,2048]{1,0:T(8,128)(2,1)} %shard_map.222), channel_id=1, source_target_pairs={{0,8},{8,0},{4,12},{12,4},{1,9},{9,1},{5,13},{13,5},{2,10},{10,2},... | collective-permute-start | bytes 6291464 | tf_op jit(solution)/shard_map/ppermute | solution.py:455
  1220.8 54.8 %collective-permute-start.61 = (bf16[512,2048]{1,0:T(8,128)(2,1)}, bf16[512,2048]{1,0:T(8,128)(2,1)}, u32[]{:S(2)}, u32[]{:S(2)}) collective-permute-start(bf16[512,2048]{1,0:T(8,128)(2,1)} %shard_map.226), channel_id=1, source_target_pairs={{0,8},{8,0},{4,12},{12,4},{1,9},{9,1},{5,13},{13,5},{2,10},{10,2},... | collective-permute-start | bytes 6291464 | tf_op jit(solution)/shard_map/ppermute | solution.py:455
  1263.3 67.1 %collective-permute-start.56 = (bf16[512,2048]{1,0:T(8,128)(2,1)}, bf16[512,2048]{1,0:T(8,128)(2,1)}, u32[]{:S(2)}, u32[]{:S(2)}) collective-permute-start(bf16[512,2048]{1,0:T(8,128)(2,1)} %shard_map.221), channel_id=1, source_target_pairs={{0,8},{8,0},{4,12},{12,4},{1,9},{9,1},{5,13},{13,5},{2,10},{10,2},... | collective-permute-start | bytes 6291464 | tf_op jit(solution)/shard_map/ppermute | solution.py:455
  1268.5 39.8 %collective-permute-start.60 = (bf16[512,1024]{1,0:T(8,128)(2,1)}, bf16[512,1024]{1,0:T(8,128)(2,1)S(1)}, u32[]{:S(2)}, u32[]{:S(2)}) collective-permute-start(bf16[512,1024]{1,0:T(8,128)(2,1)} %get-tuple-element.237), channel_id=1, source_target_pairs={{0,1},{1,2},{4,5},{5,6},{8,9},{9,10},{12,13},{13,14},{16,17},{17,1... | collective-permute-start | bytes 3145736 | tf_op jit(solution)/shard_map/ppermute | solution.py:616
  1291.5 45.9 %collective-permute-start.64 = (bf16[512,1024]{1,0:T(8,128)(2,1)}, bf16[512,1024]{1,0:T(8,128)(2,1)S(1)}, u32[]{:S(2)}, u32[]{:S(2)}) collective-permute-start(bf16[512,1024]{1,0:T(8,128)(2,1)} %get-tuple-element.243), channel_id=1, source_target_pairs={{0,1},{1,2},{2,3},{4,5},{5,6},{6,7},{8,9},{9,10},{10,11},{12,13},{... | collective-permute-start | bytes 3145736 | tf_op jit(solution)/shard_map/ppermute | solution.py:616
  1321.6 52.4 %collective-permute-start.81 = (bf16[512,1024]{1,0:T(8,128)(2,1)}, bf16[512,1024]{1,0:T(8,128)(2,1)S(1)}, u32[]{:S(2)}, u32[]{:S(2)}) collective-permute-start(bf16[512,1024]{1,0:T(8,128)(2,1)} %get-tuple-element.257), channel_id=1, source_target_pairs={{0,1},{1,2},{2,3},{4,5},{5,6},{6,7},{8,9},{9,10},{10,11},{12,13},{... | collective-permute-start | bytes 3145736 | tf_op jit(solution)/shard_map/ppermute | solution.py:616
  1329.2 44.9 %collective-permute-start.82 = (bf16[512,1024]{1,0:T(8,128)(2,1)}, bf16[512,1024]{1,0:T(8,128)(2,1)S(1)}, u32[]{:S(2)}, u32[]{:S(2)}) collective-permute-start(bf16[512,1024]{1,0:T(8,128)(2,1)} %get-tuple-element.260), channel_id=1, source_target_pairs={{1,0},{2,1},{3,2},{5,4},{6,5},{7,6},{9,8},{10,9},{11,10},{13,12},{... | collective-permute-start | bytes 3145736 | tf_op jit(solution)/shard_map/ppermute | solution.py:617
  1330.5 75.7 %collective-permute-start.80 = (bf16[512,2048]{1,0:T(8,128)(2,1)}, bf16[512,2048]{1,0:T(8,128)(2,1)}, u32[]{:S(2)}, u32[]{:S(2)}) collective-permute-start(bf16[512,2048]{1,0:T(8,128)(2,1)} %shard_map.233), channel_id=1, source_target_pairs={{0,8},{8,0},{4,12},{12,4},{1,9},{9,1},{5,13},{13,5},{2,10},{10,2},... | collective-permute-start | bytes 6291464 | tf_op jit(solution)/shard_map/ppermute | solution.py:455
  1342.7 45.4 %collective-permute-start.67 = (bf16[512,1024]{1,0:T(8,128)(2,1)}, bf16[512,1024]{1,0:T(8,128)(2,1)S(1)}, u32[]{:S(2)}, u32[]{:S(2)}) collective-permute-start(bf16[512,1024]{1,0:T(8,128)(2,1)} %get-tuple-element.246), channel_id=1, source_target_pairs={{0,1},{1,2},{2,3},{4,5},{5,6},{6,7},{8,9},{9,10},{10,11},{12,13},{... | collective-permute-start | bytes 3145736 | tf_op jit(solution)/shard_map/ppermute | solution.py:616
  1374.0 122.7 %collective-permute-start.79 = (bf16[256,8192]{1,0:T(8,128)(2,1)S(1)}, bf16[256,8192]{1,0:T(8,128)(2,1)}, u32[]{:S(2)}, u32[]{:S(2)}) collective-permute-start(bf16[256,8192]{1,0:T(8,128)(2,1)S(1)} %copy-done), channel_id=1, source_target_pairs={{0,4},{4,0},{8,12},{12,8},{1,5},{5,1},{9,13},{13,9},{2,6},{6,2},{1... | collective-permute-start | bytes 12582920 | tf_op jit(solution)/shard_map/ppermute | solution.py:451
  1374.1 127.4 %collective-permute-start.78 = (bf16[256,8192]{1,0:T(8,128)(2,1)}, bf16[256,8192]{1,0:T(8,128)(2,1)}, u32[]{:S(2)}, u32[]{:S(2)}) collective-permute-start(bf16[256,8192]{1,0:T(8,128)(2,1)} %get-tuple-element.254.refs_4_), channel_id=1, source_target_pairs={{0,4},{4,0},{8,12},{12,8},{1,5},{5,1},{9,13},{13,9},{2,6},{6,2},{1... | collective-permute-start | bytes 12582920 | tf_op jit(solution)/shard_map/ppermute | solution.py:451
  1388.1 72.1 %collective-permute-start.87 = (bf16[512,2048]{1,0:T(8,128)(2,1)}, bf16[512,2048]{1,0:T(8,128)(2,1)}, u32[]{:S(2)}, u32[]{:S(2)}) collective-permute-start(bf16[512,2048]{1,0:T(8,128)(2,1)} %shard_map.239), channel_id=1, source_target_pairs={{0,8},{8,0},{4,12},{12,4},{1,9},{9,1},{5,13},{13,5},{2,10},{10,2},... | collective-permute-start | bytes 6291464 | tf_op jit(solution)/shard_map/ppermute | solution.py:455
  1406.1 50.0 %collective-permute-start.84 = (bf16[512,1024]{1,0:T(8,128)(2,1)}, bf16[512,1024]{1,0:T(8,128)(2,1)S(1)}, u32[]{:S(2)}, u32[]{:S(2)}) collective-permute-start(bf16[512,1024]{1,0:T(8,128)(2,1)} %get-tuple-element.262), channel_id=1, source_target_pairs={{1,0},{2,1},{3,2},{5,4},{6,5},{7,6},{9,8},{10,9},{11,10},{13,12},{... | collective-permute-start | bytes 3145736 | tf_op jit(solution)/shard_map/ppermute | solution.py:617
  1433.5 103.6 %collective-permute-start.69 = (bf16[768,2048]{1,0:T(8,128)(2,1)}, bf16[768,2048]{1,0:T(8,128)(2,1)}, u32[]{:S(2)}, u32[]{:S(2)}) collective-permute-start(bf16[768,2048]{1,0:T(8,128)(2,1)} %fusion.1), channel_id=1, source_target_pairs={{0,8},{8,0},{4,12},{12,4},{1,9},{9,1},{5,13},{13,5},{2,10},{10,2},... | collective-permute-start | bytes 9437192 | tf_op jit(solution)/shard_map/ppermute | solution.py:455
  1479.8 39.5 %collective-permute-start.86 = (bf16[512,1024]{1,0:T(8,128)(2,1)}, bf16[512,1024]{1,0:T(8,128)(2,1)S(1)}, u32[]{:S(2)}, u32[]{:S(2)}) collective-permute-start(bf16[512,1024]{1,0:T(8,128)(2,1)} %get-tuple-element.264), channel_id=1, source_target_pairs={{0,1},{1,2},{2,3},{4,5},{5,6},{6,7},{8,9},{9,10},{10,11},{12,13},{... | collective-permute-start | bytes 3145736 | tf_op jit(solution)/shard_map/ppermute | solution.py:616
  1507.7 75.1 %collective-permute-start.95 = (bf16[512,2048]{1,0:T(8,128)(2,1)}, bf16[512,2048]{1,0:T(8,128)(2,1)}, u32[]{:S(2)}, u32[]{:S(2)}) collective-permute-start(bf16[512,2048]{1,0:T(8,128)(2,1)} %shard_map.245), channel_id=1, source_target_pairs={{0,8},{8,0},{4,12},{12,4},{1,9},{9,1},{5,13},{13,5},{2,10},{10,2},... | collective-permute-start | bytes 6291464 | tf_op jit(solution)/shard_map/ppermute | solution.py:455
  1524.9 41.9 %collective-permute-start.96 = (bf16[512,1024]{1,0:T(8,128)(2,1)}, bf16[512,1024]{1,0:T(8,128)(2,1)S(1)}, u32[]{:S(2)}, u32[]{:S(2)}) collective-permute-start(bf16[512,1024]{1,0:T(8,128)(2,1)} %get-tuple-element.275), channel_id=1, source_target_pairs={{0,1},{1,2},{2,3},{4,5},{5,6},{6,7},{8,9},{9,10},{10,11},{12,13},{... | collective-permute-start | bytes 3145736 | tf_op jit(solution)/shard_map/ppermute | solution.py:616
  1529.5 43.5 %collective-permute-start.97 = (bf16[512,1024]{1,0:T(8,128)(2,1)}, bf16[512,1024]{1,0:T(8,128)(2,1)}, u32[]{:S(2)}, u32[]{:S(2)}) collective-permute-start(bf16[512,1024]{1,0:T(8,128)(2,1)} %get-tuple-element.278), channel_id=1, source_target_pairs={{1,0},{2,1},{3,2},{5,4},{6,5},{7,6},{9,8},{10,9},{11,10},{13,12},{... | collective-permute-start | bytes 3145736 | tf_op jit(solution)/shard_map/ppermute | solution.py:617
  1537.1 88.7 %collective-permute-start.102 = (bf16[512,2048]{1,0:T(8,128)(2,1)}, bf16[512,2048]{1,0:T(8,128)(2,1)}, u32[]{:S(2)}, u32[]{:S(2)}) collective-permute-start(bf16[512,2048]{1,0:T(8,128)(2,1)} %shard_map.251), channel_id=1, source_target_pairs={{0,8},{8,0},{4,12},{12,4},{1,9},{9,1},{5,13},{13,5},{2,10},{10,2},... | collective-permute-start | bytes 6291464 | tf_op jit(solution)/shard_map/ppermute | solution.py:455
  1615.7 64.8 %collective-permute-start.94 = (bf16[512,2048]{1,0:T(8,128)(2,1)}, bf16[512,2048]{1,0:T(8,128)(2,1)}, u32[]{:S(2)}, u32[]{:S(2)}) collective-permute-start(bf16[512,2048]{1,0:T(8,128)(2,1)} %shard_map.244), channel_id=1, source_target_pairs={{0,8},{8,0},{4,12},{12,4},{1,9},{9,1},{5,13},{13,5},{2,10},{10,2},... | collective-permute-start | bytes 6291464 | tf_op jit(solution)/shard_map/ppermute | solution.py:455
  1660.7 40.0 %collective-permute-start.111 = (bf16[512,1024]{1,0:T(8,128)(2,1)}, bf16[512,1024]{1,0:T(8,128)(2,1)S(1)}, u32[]{:S(2)}, u32[]{:S(2)}) collective-permute-start(bf16[512,1024]{1,0:T(8,128)(2,1)} %get-tuple-element.293), channel_id=1, source_target_pairs={{0,1},{1,2},{2,3},{4,5},{5,6},{6,7},{8,9},{9,10},{10,11},{12,13},{... | collective-permute-start | bytes 3145736 | tf_op jit(solution)/shard_map/ppermute | solution.py:616
  1665.3 48.0 %collective-permute-start.106 = (bf16[512,1024]{1,0:T(8,128)(2,1)}, bf16[512,1024]{1,0:T(8,128)(2,1)}, u32[]{:S(2)}, u32[]{:S(2)}) collective-permute-start(bf16[512,1024]{1,0:T(8,128)(2,1)} %get-tuple-element.289), channel_id=1, source_target_pairs={{1,0},{2,1},{3,2},{5,4},{6,5},{7,6},{9,8},{10,9},{11,10},{13,12},{... | collective-permute-start | bytes 3145736 | tf_op jit(solution)/shard_map/ppermute | solution.py:617
  1680.4 63.0 %collective-permute-start.120 = (bf16[256,2048]{1,0:T(8,128)(2,1)}, bf16[256,2048]{1,0:T(8,128)(2,1)}, u32[]{:S(2)}, u32[]{:S(2)}) collective-permute-start(bf16[256,2048]{1,0:T(8,128)(2,1)} %fusion.47.refs_5_), channel_id=1, source_target_pairs={{0,4},{4,0},{8,12},{12,8},{1,5},{5,1},{9,13},{13,9},{2,6},{6,2},{1... | collective-permute-start | bytes 3145736 | tf_op jit(solution)/shard_map/ppermute | solution.py:451
  1680.5 54.2 %collective-permute-start.122 = (bf16[512,256]{1,0:T(8,128)(2,1)}, bf16[512,256]{1,0:T(8,128)(2,1)S(1)}, u32[]{:S(2)}, u32[]{:S(2)}) collective-permute-start(bf16[512,256]{1,0:T(8,128)(2,1)} %get-tuple-element.308), channel_id=1, source_target_pairs={{0,4},{4,0},{8,12},{12,8},{1,5},{5,1},{9,13},{13,9},{2,6},{6,2},{1... | collective-permute-start | bytes 786440 | tf_op jit(solution)/shard_map/ppermute | solution.py:451
  1700.7 52.1 %collective-permute-start.75 = (bf16[256,3072]{1,0:T(8,128)(2,1)S(1)}, bf16[256,3072]{1,0:T(8,128)(2,1)S(1)}, u32[]{:S(2)}, u32[]{:S(2)}) collective-permute-start(bf16[256,3072]{1,0:T(8,128)(2,1)S(1)} %pad_maximum_fusion.refs_5_), channel_id=1, source_target_pairs={{0,4},{4,0},{8,12},{12,8},{1,5},{5,1},{9,13},{13,9},{2,6},{6,2},{1... | collective-permute-start | bytes 4718600 | tf_op jit(solution)/shard_map/ppermute | solution.py:451
  1700.7 42.7 %collective-permute-start.119 = (bf16[256,2048]{1,0:T(8,128)(2,1)}, bf16[256,2048]{1,0:T(8,128)(2,1)}, u32[]{:S(2)}, u32[]{:S(2)}) collective-permute-start(bf16[256,2048]{1,0:T(8,128)(2,1)} %fusion.48.refs_4_), channel_id=1, source_target_pairs={{0,4},{4,0},{8,12},{12,8},{1,5},{5,1},{9,13},{13,9},{2,6},{6,2},{1... | collective-permute-start | bytes 3145736 | tf_op jit(solution)/shard_map/ppermute | solution.py:451
  1713.3 51.2 %collective-permute-start.110 = (bf16[512,2048]{1,0:T(8,128)(2,1)}, bf16[512,2048]{1,0:T(8,128)(2,1)}, u32[]{:S(2)}, u32[]{:S(2)}) collective-permute-start(bf16[512,2048]{1,0:T(8,128)(2,1)} %shard_map.257), channel_id=1, source_target_pairs={{0,8},{8,0},{4,12},{12,4},{1,9},{9,1},{5,13},{13,5},{2,10},{10,2},... | collective-permute-start | bytes 6291464 | tf_op jit(solution)/shard_map/ppermute | solution.py:455
  1750.9 94.9 %collective-permute-start.123 = (bf16[512,2048]{1,0:T(8,128)(2,1)}, bf16[512,2048]{1,0:T(8,128)(2,1)}, u32[]{:S(2)}, u32[]{:S(2)}) collective-permute-start(bf16[512,2048]{1,0:T(8,128)(2,1)} %shard_map.264), channel_id=1, source_target_pairs={{0,8},{8,0},{4,12},{12,4},{1,9},{9,1},{5,13},{13,5},{2,10},{10,2},... | collective-permute-start | bytes 6291464 | tf_op jit(solution)/shard_map/ppermute | solution.py:455
  1752.7 77.9 %collective-permute-start.74 = (bf16[256,3072]{1,0:T(8,128)(2,1)S(1)}, bf16[256,3072]{1,0:T(8,128)(2,1)S(1)}, u32[]{:S(2)}, u32[]{:S(2)}) collective-permute-start(bf16[256,3072]{1,0:T(8,128)(2,1)S(1)} %pad_maximum_fusion.1.refs_4_), channel_id=1, source_target_pairs={{0,4},{4,0},{8,12},{12,8},{1,5},{5,1},{9,13},{13,9},{2,6},{6,2},{1... | collective-permute-start | bytes 4718600 | tf_op jit(solution)/shard_map/ppermute | solution.py:451
  1764.5 48.7 %collective-permute-start.114 = (bf16[512,1024]{1,0:T(8,128)(2,1)}, bf16[512,1024]{1,0:T(8,128)(2,1)}, u32[]{:S(2)}, u32[]{:S(2)}) collective-permute-start(bf16[512,1024]{1,0:T(8,128)(2,1)} %get-tuple-element.298), channel_id=1, source_target_pairs={{1,0},{2,1},{3,2},{5,4},{6,5},{7,6},{9,8},{10,9},{11,10},{13,12},{... | collective-permute-start | bytes 3145736 | tf_op jit(solution)/shard_map/ppermute | solution.py:617
  1785.6 52.9 %collective-permute-start.117 = (bf16[512,256]{1,0:T(8,128)(2,1)}, bf16[512,256]{1,0:T(8,128)(2,1)S(1)}, u32[]{:S(2)}, u32[]{:S(2)}) collective-permute-start(bf16[512,256]{1,0:T(8,128)(2,1)} %get-tuple-element.304), channel_id=1, source_target_pairs={{0,4},{4,0},{8,12},{12,8},{1,5},{5,1},{9,13},{13,9},{2,6},{6,2},{1... | collective-permute-start | bytes 786440 | tf_op jit(solution)/shard_map/ppermute | solution.py:451
  1791.4 48.4 %collective-permute-start.118 = (bf16[512,256]{1,0:T(8,128)(2,1)}, bf16[512,256]{1,0:T(8,128)(2,1)S(1)}, u32[]{:S(2)}, u32[]{:S(2)}) collective-permute-start(bf16[512,256]{1,0:T(8,128)(2,1)} %get-tuple-element.305), channel_id=1, source_target_pairs={{0,4},{4,0},{8,12},{12,8},{1,5},{5,1},{9,13},{13,9},{2,6},{6,2},{1... | collective-permute-start | bytes 786440 | tf_op jit(solution)/shard_map/ppermute | solution.py:451
  1844.4 42.8 %collective-permute-start.124 = (bf16[512,1024]{1,0:T(8,128)(2,1)}, bf16[512,1024]{1,0:T(8,128)(2,1)}, u32[]{:S(2)}, u32[]{:S(2)}) collective-permute-start(bf16[512,1024]{1,0:T(8,128)(2,1)} %get-tuple-element.310), channel_id=1, source_target_pairs={{1,0},{2,1},{3,2},{5,4},{6,5},{7,6},{9,8},{10,9},{11,10},{13,12},{... | collective-permute-start | bytes 3145736 | tf_op jit(solution)/shard_map/ppermute | solution.py:617
  1845.8 64.5 %collective-permute-start.109 = (bf16[512,2048]{1,0:T(8,128)(2,1)}, bf16[512,2048]{1,0:T(8,128)(2,1)}, u32[]{:S(2)}, u32[]{:S(2)}) collective-permute-start(bf16[512,2048]{1,0:T(8,128)(2,1)} %shard_map.256), channel_id=1, source_target_pairs={{0,8},{8,0},{4,12},{12,4},{1,9},{9,1},{5,13},{13,5},{2,10},{10,2},... | collective-permute-start | bytes 6291464 | tf_op jit(solution)/shard_map/ppermute | solution.py:455
  1876.7 42.1 %collective-permute-start.129 = (bf16[512,1024]{1,0:T(8,128)(2,1)}, bf16[512,1024]{1,0:T(8,128)(2,1)S(1)}, u32[]{:S(2)}, u32[]{:S(2)}) collective-permute-start(bf16[512,1024]{1,0:T(8,128)(2,1)} %get-tuple-element.317), channel_id=1, source_target_pairs={{0,1},{1,2},{2,3},{4,5},{5,6},{6,7},{8,9},{9,10},{10,11},{12,13},{... | collective-permute-start | bytes 3145736 | tf_op jit(solution)/shard_map/ppermute | solution.py:616
  1910.3 44.8 %collective-permute-start.137 = (bf16[512,1024]{1,0:T(8,128)(2,1)}, bf16[512,1024]{1,0:T(8,128)(2,1)}, u32[]{:S(2)}, u32[]{:S(2)}) collective-permute-start(bf16[512,1024]{1,0:T(8,128)(2,1)} %shard_map.272), channel_id=1, source_target_pairs={{0,8},{8,0},{4,12},{12,4},{1,9},{9,1},{5,13},{13,5},{2,10},{10,2},... | collective-permute-start | bytes 3145736 | tf_op jit(solution)/shard_map/ppermute | solution.py:455
  1987.2 40.5 %collective-permute-start.135 = (bf16[512,1024]{1,0:T(8,128)(2,1)}, bf16[512,1024]{1,0:T(8,128)(2,1)S(1)}, u32[]{:S(2)}, u32[]{:S(2)}) collective-permute-start(bf16[512,1024]{1,0:T(8,128)(2,1)} %get-tuple-element.324), channel_id=1, source_target_pairs={{0,1},{1,2},{2,3},{4,5},{5,6},{6,7},{8,9},{9,10},{10,11},{12,13},{... | collective-permute-start | bytes 3145736 | tf_op jit(solution)/shard_map/ppermute | solution.py:616
  1989.4 38.5 %collective-permute-start.136 = (bf16[512,1024]{1,0:T(8,128)(2,1)}, bf16[512,1024]{1,0:T(8,128)(2,1)}, u32[]{:S(2)}, u32[]{:S(2)}) collective-permute-start(bf16[512,1024]{1,0:T(8,128)(2,1)} %get-tuple-element.325), channel_id=1, source_target_pairs={{1,0},{2,1},{3,2},{5,4},{6,5},{7,6},{9,8},{10,9},{11,10},{13,12},{... | collective-permute-start | bytes 3145736 | tf_op jit(solution)/shard_map/ppermute | solution.py:617
  2010.0 40.4 %collective-permute-start.143 = (bf16[512,1024]{1,0:T(8,128)(2,1)}, bf16[512,1024]{1,0:T(8,128)(2,1)}, u32[]{:S(2)}, u32[]{:S(2)}) collective-permute-start(bf16[512,1024]{1,0:T(8,128)(2,1)} %get-tuple-element.331), channel_id=1, source_target_pairs={{1,0},{2,1},{5,4},{6,5},{9,8},{10,9},{13,12},{14,13},{17,16},{18,1... | collective-permute-start | bytes 3145736 | tf_op jit(solution)/shard_map/ppermute | solution.py:617
  2033.2 39.6 %collective-permute-start.141 = (bf16[512,1024]{1,0:T(8,128)(2,1)}, bf16[512,1024]{1,0:T(8,128)(2,1)}, u32[]{:S(2)}, u32[]{:S(2)}) collective-permute-start(bf16[512,1024]{1,0:T(8,128)(2,1)} %get-tuple-element.329), channel_id=1, source_target_pairs={{1,0},{2,1},{5,4},{6,5},{9,8},{10,9},{13,12},{14,13},{17,16},{18,1... | collective-permute-start | bytes 3145736 | tf_op jit(solution)/shard_map/ppermute | solution.py:617
  2053.9 42.4 %collective-permute-start.146 = (bf16[512,1024]{1,0:T(8,128)(2,1)}, bf16[512,1024]{1,0:T(8,128)(2,1)}, u32[]{:S(2)}, u32[]{:S(2)}) collective-permute-start(bf16[512,1024]{1,0:T(8,128)(2,1)} %get-tuple-element.334), channel_id=1, source_target_pairs={{1,2},{2,3},{5,6},{6,7},{9,10},{10,11},{13,14},{14,15},{17,18},{18... | collective-permute-start | bytes 3145736 | tf_op jit(solution)/shard_map/ppermute | solution.py:616
  2055.5 40.8 %collective-permute-start.147 = (bf16[512,1024]{1,0:T(8,128)(2,1)}, bf16[512,1024]{1,0:T(8,128)(2,1)}, u32[]{:S(2)}, u32[]{:S(2)}) collective-permute-start(bf16[512,1024]{1,0:T(8,128)(2,1)} %get-tuple-element.335), channel_id=1, source_target_pairs={{1,0},{5,4},{9,8},{13,12},{17,16},{21,20},{25,24},{29,28}} | collective-permute-start | bytes 3145736 | tf_op jit(solution)/shard_map/ppermute | solution.py:617
  (289 other events, 6983.0 us)
Sparse Core Ops, SparseCore 0:
  55.9 82.2 all-gather.7
  180.7 47.6 all-gather.5
  230.5 79.4 all-gather.9
  311.4 148.1 all-gather.11

commit v4 on v3

--- a/solution.py
+++ b/solution.py
@@ -616,17 +616,42 @@
                 ups[q].append(lax.ppermute(up, "dp", up_pairs))
                 downs[q].append(lax.ppermute(down, "dp", down_pairs))
                 order.append((ups[q][-1], downs[q][-1]))
-    distance = jnp.abs(place - root)
-    totals = [None] * count
-    for q in range(stream_count):
-        for index in range(counts[q]):
-            total = None
-            for hops in range(delay + 1):
-                up, down = sent[q][index + delay + hops]
-                value = jnp.where(place >= root, up, down)
-                total = value if total is None else jnp.where(distance == hops, value, total)
-            totals[q + index * stream_count] = total
-    return totals
+    choice = 2 * jnp.abs(place - root) + (place < root).astype(jnp.int32)
+    found = []
+    for index in range(count):
+        at, q = divmod(index, stream_count)
+        found.append([x for hops in range(delay + 1) for x in sent[q][at + delay + hops]])
+    return choice.astype(jnp.int32).reshape(1), found
+
+
+def place_chunk(choice, found, whole, shape, row, column, tile=128):
+    per = CHUNK_ROWS // tile
+    kept = [] if whole is None else [whole]
+
+    def kernel(choice_ref, *refs):
+        for index in range(len(found)):
+
+            @pl.when(choice_ref[0] == index)
+            def _():
+                refs[-1][...] = refs[index][...].astype(F32)
+
+    def chosen(index):
+        return lambda t, s: (jnp.where(s[0] == index, t, 0), 0)
+
+    return pl.pallas_call(
+        kernel,
+        grid_spec=pltpu.PrefetchScalarGridSpec(
+            num_scalar_prefetch=1,
+            grid=(per,),
+            in_specs=[pl.BlockSpec((tile, CHUNK_COLS), chosen(k)) for k in range(len(found))]
+            + [pl.BlockSpec(memory_space=pl.ANY)] * len(kept),
+            out_specs=pl.BlockSpec((tile, CHUNK_COLS), lambda t, s: (row * per + t, column)),
+        ),
+        out_shape=jax.ShapeDtypeStruct(shape, F32),
+        input_output_aliases={1 + len(found): 0} if kept else {},
+        compiler_params=pltpu.CompilerParams(vmem_limit_bytes=VMEM),
+        cost_estimate=pl.CostEstimate(flops=1, bytes_accessed=1, transcendentals=0),
+    )(choice, *found, *kept)
 
 
 def body(
@@ -918,33 +943,35 @@
         return made[index]
 
     count = sum(width // CHUNK_COLS for _, _, _, width in plan) + 1
-    totals = replica_chain(count, make, (CHUNK_ROWS, CHUNK_COLS), BF, wanted=wanted)
+    choice, found = replica_chain(count, make, (CHUNK_ROWS, CHUNK_COLS), BF, wanted=wanted)
     grad_two = work["done"][0]
 
-    gains = totals.pop()[: gains_b.shape[0], : model_width // 4].astype(F32)
+    last = [x[: gains_b.shape[0], : model_width // 4] for x in found.pop()]
+    gains = last[0]
+    for index, x in enumerate(last):
+        gains = jnp.where(choice[0] == index, x, gains)
+    gains = gains.astype(F32)
 
     def assembled(rows, cols):
-        count = (rows // CHUNK_ROWS) * (cols // CHUNK_COLS)
-        taken, totals[:] = totals[:count], totals[count:]
+        whole = None
         across = cols // CHUNK_COLS
-        lines = [
-            jnp.concatenate(taken[at : at + across], axis=1) for at in range(0, count, across)
-        ]
-        return jnp.concatenate(lines, axis=0).astype(F32)
+        for index in range(rows // CHUNK_ROWS * across):
+            row, column = divmod(index, across)
+            whole = place_chunk(choice, found.pop(0), whole, (rows, cols), row, column)
+        return whole
 
     grad_down = assembled(w_down.shape[1], w_down.shape[2])
     grad_gate = assembled(w_gate.shape[1], w_gate.shape[2])
     grad_up = assembled(w_up.shape[1], w_up.shape[2])
     grad_out = assembled(w_out.shape[1], w_out.shape[2])
-    grad_qkv = assembled(w_query.shape[1], qkv_width)
-    grad_pairs = [
-        grad_qkv[:, at : at + LANES] for at in range(query_width, grad_qkv.shape[1], LANES)
-    ]
+    grad_query = assembled(w_query.shape[1], query_width)
+    grad_both = assembled(w_query.shape[1], 2 * key_width)
+    grad_pairs = [grad_both[:, at : at + LANES] for at in range(0, 2 * key_width, LANES)]
     boundary = choose(jnp.stack([grad_one, grad_two]), jnp.stack([output_one, output_two]))
     return (
         boundary[None, :, None],
         gains[0][None],
-        grad_qkv[:, :query_width][None],
+        grad_query[None],
         jnp.concatenate(grad_pairs[::2], axis=1)[None],
         jnp.concatenate(grad_pairs[1::2], axis=1)[None],
         grad_out[None],

time: 2180 us -> 2230 us (1.023)
  Pallas kernels: 785 us -> 901 us
  other arithmetic: 199 us -> 85 us
  waiting for transfers between devices: 617 us -> 714 us
  starting transfers between devices: 329 us -> 290 us
    pallas_call x0 -> x29, Pallas kernels: none -> 118 us  [place_chunk(): pl.pallas_call(kernel, grid_spec=pltpu.PrefetchScalarGridSpec(num_scalar_...]
    ppermute x36, waiting for transfers between devices: 108 us -> 190 us  [replica_chain(): ups[q].append(lax.ppermute(up, 'dp', up_pairs))]
    unnamed x13 -> x0, other arithmetic: 40.8 us -> none
    convert_element_type x6 -> x1, other arithmetic: 37.1 us -> 0.79 us  [body(): gains = gains.astype(F32)]
    ppermute x27, starting transfers between devices: 106 us -> 71.9 us  [chip_swap(): return lax.ppermute(x, 'fsdp', [(0, 2), (2, 0), (1, 3), (3, 1)])]
    unnamed x414 -> x348, local copies, waits for them, and re-layouts: 54 us -> 57.5 us
  transfers between devices with their start and end apart: 156 -> 156, of which waited for: 52 -> 59; matrix products, arithmetic and copies ran while one was open for 13% -> 8% of each run, Pallas kernels for 26% -> 30%
where the time goes in v4:
time: 2230 us; the launch traced here: 2210 us
  Pallas kernels  901 us (40%)
  waiting for transfers between devices  714 us (32%)
  starting transfers between devices  290 us (13%)
  local copies, waits for them, and re-layouts  125 us (6%)
  other arithmetic  85 us (4%)
  matrix products  64.7 us (3%)
    ppermute x27, waiting for transfers between devices, chip_swap(): return lax.ppermute(x, 'fsdp', [(0, 2), (2, 0), (1, 3), (3, 1)])  221 us
    pallas_call x30, Pallas kernels, outer(): pl.pallas_call(kernel, grid=(count * per,), in_specs=[pl.BlockSpec((CHUNK...  192 us
    ppermute x36, waiting for transfers between devices, replica_chain(): ups[q].append(lax.ppermute(up, 'dp', up_pairs))  190 us
    pallas_call x3, Pallas kernels, hidden_back(): pl.pallas_call(hidden_back_kernel, grid_spec=pltpu.PrefetchScalarGridSpec...  170 us
    pallas_call x38, Pallas kernels, relay(): pl.pallas_call(kernel, grid_spec=pltpu.PrefetchScalarGridSpec(num_scalar_...  151 us
    ppermute x36, waiting for transfers between devices, replica_chain(): downs[q].append(lax.ppermute(down, 'dp', down_pairs))  133 us
    ppermute x36, starting transfers between devices, replica_chain(): ups[q].append(lax.ppermute(up, 'dp', up_pairs))  125 us
    pallas_call x29, Pallas kernels, place_chunk(): pl.pallas_call(kernel, grid_spec=pltpu.PrefetchScalarGridSpec(num_scalar_...  118 us
  transfers between devices with their start and end apart: 156, of which 59 were waited for; matrix products, arithmetic and copies ran while one was open for 8% of the time, Pallas kernels for 30%

profile of v4, /device:TPU:0, one launch (start us, length us, event | category | flops | bytes accessed | tf_op | source)
XLA Modules:
  0.0 2210.4 jit_solution(3527578954955827129)
XLA Ops:
  39.8 15.0 collective-permute-done.1
  69.3 67.7 %collective-permute-done.2 = bf16[512,3072]{1,0:T(8,128)(2,1)} collective-permute-done((bf16[512,3072]{1,0:T(8,128)(2,1)S(1)}, bf16[512,3072]{1,0:T(8,128)(2,1)}, u32[]{:S(2)}, u32[]{:S(2)}) %collective-permute-start.2) | collective-permute-done | bytes 3145760 | tf_op jit(solution)/shard_map/ppermute | solution.py:455
  144.0 21.7 collective-permute-done.8
  170.2 9.5 collective-permute-done.9
  204.4 36.0 %collective-permute-done.14 = bf16[128,8192]{1,0:T(8,128)(2,1)} collective-permute-done((bf16[128,8192]{1,0:T(8,128)(2,1)}, bf16[128,8192]{1,0:T(8,128)(2,1)}, u32[]{:S(2)}, u32[]{:S(2)}) %collective-permute-start.14) | collective-permute-done | bytes 2097184 | tf_op jit(solution)/shard_map/ppermute | solution.py:455
  253.0 10.5 shard_map.186
  265.2 12.1 collective-permute-done.5
  285.1 8.7 select_select_fusion
  299.4 15.5 collective-permute-done.7
  322.4 7.0 shard_map.187
  348.3 111.3 %all-gather.12.cloned.1.call-done.refs_0_ = bf16[512,8192]{1,0:T(8,128)(2,1)} async-done(((bf16[128,8192]{1,0:T(8,128)(2,1)}), bf16[512,8192]{1,0:T(8,128)(2,1)}) %all-gather.12.cloned.1.call-update) | async-done | bytes 8388624 | tf_op jit(solution)/shard_map/all_gather | solution.py:702
  459.6 17.0 collective-permute-done.17.refs_0_
  477.1 34.3 %shard_map.189 = (bf16[256,8192]{1,0:T(8,128)(2,1)}, bf16[256,8192]{1,0:T(8,128)(2,1)}, bf16[256,8192]{1,0:T(8,128)(2,1)}) custom-call(s32[1]{0:T(128)} %bitcast.2.shard_ref, bf16[256,2048]{1,0:T(8,128)(2,1)} %multiply_convert_fusion.2.refs_1_.b_ref, bf16[512,8192]{1,0:T(8,128)(2,1)} %bitcast.139, bf16[512,8192]{1,0:T(8,128)(2,1)} %collective-permute-done.11.refs_1_.refs_5_, ...), custom_call_target="tpu_custom_call" | custom-call | flops 1 | bytes 1 | tf_op jit(solution)/shard_map/pallas_call | solution.py:293
  511.4 19.8 shard_map.191
  539.5 20.9 collective-permute-done.19
  562.2 10.5 shard_map.192
  574.3 11.7 collective-permute-done.21
  605.0 34.4 %shard_map.194 = (bf16[256,8192]{1,0:T(8,128)(2,1)}, bf16[256,8192]{1,0:T(8,128)(2,1)}, bf16[256,8192]{1,0:T(8,128)(2,1)}) custom-call(s32[1]{0:T(128)} %bitcast.2.shard_ref, bf16[256,2048]{1,0:T(8,128)(2,1)} %multiply_convert_fusion.1.b_ref.refs_0_.refs_1_.refs_2_.refs_3_, bf16[512,8192]{1,0:T(8,128)(2,1)} %bitcast.140, ...), custom_call_target="tpu_custom_call" | custom-call | flops 1 | bytes 1 | tf_op jit(solution)/shard_map/pallas_call | solution.py:293
  639.4 56.4 %shard_map.195 = (bf16[256,8192]{1,0:T(8,128)(2,1)}, bf16[256,8192]{1,0:T(8,128)(2,1)}, f32[256,2048]{1,0:T(8,128)}) custom-call(s32[1]{0:T(128)} %bitcast.2.shard_ref, bf16[256,2048]{1,0:T(8,128)(2,1)} %slice_bitcast_fusion.dy_ref, bf16[256,8192]{1,0:T(8,128)(2,1)} %get-tuple-element.184.g_ref, bf16[256,8192]{1,0:T(8,128)(2,1)} %get-tuple-element.185.u_ref, ...), custom_call_target="tpu_custom_call" | custom-call | flops 1 | bytes 1 | tf_op jit(solution)/shard_map/pallas_call | solution.py:390
  704.8 10.5 shard_map.196
  717.6 8.4 collective-permute-start.24
  729.3 17.4 collective-permute-start.25
  746.7 19.3 shard_map.197
  776.5 7.2 fusion.13
  783.8 13.5 collective-permute-done.27
  803.1 10.5 shard_map.199
  813.9 13.0 collective-permute-done.29
  854.3 34.3 %shard_map.201 = (bf16[256,8192]{1,0:T(8,128)(2,1)}, bf16[256,8192]{1,0:T(8,128)(2,1)}, bf16[256,8192]{1,0:T(8,128)(2,1)}) custom-call(s32[1]{0:T(128)} %bitcast.2.shard_ref, bf16[256,2048]{1,0:T(8,128)(2,1)} %multiply_convert_fusion.b_ref.refs_0_.refs_1_.refs_2_.refs_3_, bf16[512,8192]{1,0:T(8,128)(2,1)} %bitcast.142, ...), custom_call_target="tpu_custom_call" | custom-call | flops 1 | bytes 1 | tf_op jit(solution)/shard_map/pallas_call | solution.py:293
  890.8 56.8 %shard_map.202 = (bf16[256,8192]{1,0:T(8,128)(2,1)}, bf16[256,8192]{1,0:T(8,128)(2,1)}, f32[256,2048]{1,0:T(8,128)}) custom-call(s32[1]{0:T(128)} %bitcast.2.shard_ref, bf16[256,2048]{1,0:T(8,128)(2,1)} %bitcast_select_fusion.dy_ref.refs_5_, bf16[256,8192]{1,0:T(8,128)(2,1)} %get-tuple-element.195.g_ref, bf16[256,8192]{1,0:T(8,128)(2,1)} %get-tuple-element.196.u_ref, ...), custom_call_target="tpu_custom_call" | custom-call | flops 1 | bytes 1 | tf_op jit(solution)/shard_map/pallas_call | solution.py:390
  951.2 7.1 convolution_convert_fusion.1.do_ref
  958.3 12.1 shard_map.203
  971.8 7.3 collective-permute-start.32
  980.9 16.5 collective-permute-start.33
  997.4 12.4 collective-permute-done.33
  1010.1 7.7 fusion.30
  1034.3 19.3 shard_map.204.refs_1_
  1082.3 56.5 %shard_map.211 = (bf16[256,8192]{1,0:T(8,128)(2,1)}, bf16[256,8192]{1,0:T(8,128)(2,1)}, f32[256,2048]{1,0:T(8,128)}) custom-call(s32[1]{0:T(128)} %bitcast.2.shard_ref, bf16[256,2048]{1,0:T(8,128)(2,1)} %broadcast_select_fusion.1.dy_ref, bf16[256,8192]{1,0:T(8,128)(2,1)} %get-tuple-element.184.g_ref, bf16[256,8192]{1,0:T(8,128)(2,1)} %get-tuple-element.185.u_ref, ...), custom_call_target="tpu_custom_call" | custom-call | flops 1 | bytes 1 | tf_op jit(solution)/shard_map/pallas_call | solution.py:390
  1166.8 19.0 collective-permute-done.45.refs_4_.refs_2_.refs_8_.refs_5_
  1225.7 9.6 collective-permute-done.55.refs_8_.refs_6_.refs_3_.refs_5_
  1269.1 7.7 collective-permute-start.60
  1278.1 7.8 collective-permute-done.62.refs_3_.refs_5_.refs_8_.refs_6_
  1285.9 7.2 shard_map.227
  1341.7 7.1 convolution_convert_fusion.do_ref
  1350.2 10.7 shard_map.218
  1382.4 11.7 collective-permute-start.87
  1408.0 14.1 collective-permute-done.85.refs_7_.refs_4_
  1433.2 9.9 collective-permute-done.84.refs_4_.refs_7_
  1451.0 16.2 collective-permute-done.88.refs_3_.refs_5_.refs_8_.refs_6_
  1551.7 11.0 collective-permute-done.93.refs_8_.refs_6_.refs_3_.refs_5_
  1626.9 7.6 collective-permute-done.101.refs_9_.refs_6_.refs_3_.refs_5_
  1703.3 17.2 collective-permute-done.113.refs_3_.refs_9_.refs_5_.refs_6_
  1723.4 17.3 collective-permute-done.115.refs_7_.refs_4_
  1767.1 9.7 collective-permute-done.116.refs_9_.refs_3_.refs_5_.refs_6_
  1783.3 10.5 fusion.23
  1793.9 10.0 collective-permute-done.125.refs_6_.refs_3_.refs_5_.refs_8_
  1803.9 7.2 shard_map.265
  1845.9 7.2 collective-permute-done.128.refs_4_.refs_7_
  1853.1 13.1 collective-permute-done.129.refs_6_.refs_3_.refs_5_
  1866.2 8.3 collective-permute-done.130.refs_7_.refs_4_
  1910.1 16.1 collective-permute-done.133.refs_6_.refs_3_.refs_4_
  1949.3 12.3 collective-permute-done.135.refs_2_.refs_3_.refs_4_
  1966.0 14.9 collective-permute-done.138.refs_5_.refs_2_.refs_3_
  1997.9 21.0 collective-permute-done.141.refs_2_.refs_4_
  2018.9 18.6 collective-permute-done.143.refs_5_.refs_2_
  (858 shorter events, 1018.2 us)
Async XLA Ops:
  7.2 176.1 %all-gather.8.cloned.1.call-start = ((), (), s32[]{:S(2)}) async-start(), calls=%async_computation.1 | async-start | bytes 5242880 | tf_op jit(solution)/shard_map/all_gather | solution.py:702
  55.7 240.2 %all-gather.6.cloned.1.call-start = ((), (), s32[]{:S(2)}) async-start(), calls=%async_computation | async-start | bytes 2621440 | tf_op jit(solution)/shard_map/all_gather | solution.py:702
  67.5 69.4 %collective-permute-start.2 = (bf16[512,3072]{1,0:T(8,128)(2,1)S(1)}, bf16[512,3072]{1,0:T(8,128)(2,1)}, u32[]{:S(2)}, u32[]{:S(2)}) collective-permute-start(bf16[512,3072]{1,0:T(8,128)(2,1)S(1)} %get-tuple-element.360), channel_id=1, source_target_pairs={{0,8},{8,0},{4,12},{12,4},{1,9},{9,1},{5,13},{13,5},{2,10},{10,2},... | collective-permute-start | bytes 9437192 | tf_op jit(solution)/shard_map/ppermute | solution.py:455
  180.5 160.5 %all-gather.10.cloned.1.call-start = ((), (), s32[]{:S(2)}) async-start(), calls=%async_computation.2 | async-start | bytes 5242880 | tf_op jit(solution)/shard_map/all_gather | solution.py:702
  181.3 278.3 %all-gather.12.cloned.1.call-start = ((), (), s32[]{:S(2)}) async-start(), calls=%async_computation.3 | async-start | bytes 10485760 | tf_op jit(solution)/shard_map/all_gather | solution.py:702
  181.5 60.2 %collective-permute-start = (bf16[512,3072]{1,0:T(8,128)(2,1)}, bf16[512,3072]{1,0:T(8,128)(2,1)}, u32[]{:S(2)}, u32[]{:S(2)}) collective-permute-start(bf16[512,3072]{1,0:T(8,128)(2,1)} %bitcast_dynamic-update-slice_fusion.1), channel_id=1, source_target_pairs={{0,4},{4,0},{8,12},{12,8},{1,5},{5,1},{9,13},{13,9},{2,6},{6,2},{1... | collective-permute-start | bytes 9437192 | tf_op jit(solution)/shard_map/ppermute | solution.py:451
  192.0 48.4 %collective-permute-start.14 = (bf16[128,8192]{1,0:T(8,128)(2,1)}, bf16[128,8192]{1,0:T(8,128)(2,1)}, u32[]{:S(2)}, u32[]{:S(2)}) collective-permute-start(bf16[128,8192]{1,0:T(8,128)(2,1)} %select_bitcast_fusion), channel_id=1, source_target_pairs={{0,8},{8,0},{4,12},{12,4},{1,9},{9,1},{5,13},{13,5},{2,10},{10,2},... | collective-permute-start | bytes 6291464 | tf_op jit(solution)/shard_map/ppermute | solution.py:455
  193.8 55.4 %collective-permute-start.3 = (bf16[512,3072]{1,0:T(8,128)(2,1)}, bf16[512,3072]{1,0:T(8,128)(2,1)}, u32[]{:S(2)}, u32[]{:S(2)}) collective-permute-start(bf16[512,3072]{1,0:T(8,128)(2,1)} %collective-permute-done.2), channel_id=1, source_target_pairs={{0,4},{4,0},{8,12},{12,8},{1,5},{5,1},{9,13},{13,9},{2,6},{6,2},{1... | collective-permute-start | bytes 9437192 | tf_op jit(solution)/shard_map/ppermute | solution.py:451
  293.8 182.8 %collective-permute-start.17 = (bf16[2048,2048]{1,0:T(8,128)(2,1)}, bf16[2048,2048]{1,0:T(8,128)(2,1)}, u32[]{:S(2)}, u32[]{:S(2)}) collective-permute-start(bf16[2048,2048]{1,0:T(8,128)(2,1)} %select_select_fusion), channel_id=1, source_target_pairs={{0,8},{8,0},{4,12},{12,4},{1,9},{9,1},{5,13},{13,5},{2,10},{10,2},... | collective-permute-start | bytes 25165832 | tf_op jit(solution)/shard_map/ppermute | solution.py:455
  295.5 181.2 %collective-permute-start.11 = (bf16[512,8192]{1,0:T(8,128)(2,1)}, bf16[512,8192]{1,0:T(8,128)(2,1)}, u32[]{:S(2)}, u32[]{:S(2)}) collective-permute-start(bf16[512,8192]{1,0:T(8,128)(2,1)} %bitcast.138), channel_id=1, source_target_pairs={{0,4},{4,0},{8,12},{12,8},{1,5},{5,1},{9,13},{13,9},{2,6},{6,2},{1... | collective-permute-start | bytes 25165832 | tf_op jit(solution)/shard_map/ppermute | solution.py:451
  296.0 181.1 %collective-permute-start.13 = (bf16[512,8192]{1,0:T(8,128)(2,1)}, bf16[512,8192]{1,0:T(8,128)(2,1)}, u32[]{:S(2)}, u32[]{:S(2)}) collective-permute-start(bf16[512,8192]{1,0:T(8,128)(2,1)} %bitcast.152), channel_id=1, source_target_pairs={{0,4},{4,0},{8,12},{12,8},{1,5},{5,1},{9,13},{13,9},{2,6},{6,2},{1... | collective-permute-start | bytes 25165832 | tf_op jit(solution)/shard_map/ppermute | solution.py:451
  345.7 131.4 %collective-permute-start.12 = (bf16[512,8192]{1,0:T(8,128)(2,1)}, bf16[512,8192]{1,0:T(8,128)(2,1)}, u32[]{:S(2)}, u32[]{:S(2)}) collective-permute-start(bf16[512,8192]{1,0:T(8,128)(2,1)} %constant_dynamic-update-slice_fusion.refs_2_.refs_6_), channel_id=1, source_target_pairs={{0,4},{4,0},{8,12},{12,8},{1,5},{5,1},{9,13},{13,9},{2,6},{6,2},{1... | collective-permute-start | bytes 25165832 | tf_op jit(solution)/shard_map/ppermute | solution.py:451
  726.0 48.4 %collective-permute-start.23 = (bf16[256,1024]{1,0:T(8,128)(2,1)}, bf16[256,1024]{1,0:T(8,128)(2,1)S(1)}, u32[]{:S(2)}, u32[]{:S(2)}) collective-permute-start(bf16[256,1024]{1,0:T(8,128)(2,1)} %get-tuple-element.375), channel_id=1, source_target_pairs={{0,4},{4,0},{8,12},{12,8},{1,5},{5,1},{9,13},{13,9},{2,6},{6,2},{1... | collective-permute-start | bytes 1572872 | tf_op jit(solution)/shard_map/ppermute | solution.py:451
  729.3 45.1 %collective-permute-start.25 = (bf16[256,1024]{1,0:T(8,128)(2,1)}, bf16[256,1024]{1,0:T(8,128)(2,1)}, u32[]{:S(2)}, u32[]{:S(2)}) collective-permute-start(bf16[256,1024]{1,0:T(8,128)(2,1)} %add_convert_fusion.5), channel_id=1, source_target_pairs={{0,8},{8,0},{4,12},{12,4},{1,9},{9,1},{5,13},{13,5},{2,10},{10,2},... | collective-permute-start | bytes 1572872 | tf_op jit(solution)/shard_map/ppermute | solution.py:455
  835.3 53.2 %collective-permute-start.26 = (bf16[256,2048]{1,0:T(8,128)(2,1)}, bf16[256,2048]{1,0:T(8,128)(2,1)}, u32[]{:S(2)}, u32[]{:S(2)}) collective-permute-start(bf16[256,2048]{1,0:T(8,128)(2,1)} %get-tuple-element.374), channel_id=1, source_target_pairs={{16,0},{17,1},{18,2},{19,3},{20,4},{21,5},{22,6},{23,7},{24,8},{25... | collective-permute-start | bytes 3145736 | tf_op jit(solution)/shard_map/ppermute | solution.py:833
  1067.5 82.0 %collective-permute-start.42 = (bf16[512,2048]{1,0:T(8,128)(2,1)}, bf16[512,2048]{1,0:T(8,128)(2,1)}, u32[]{:S(2)}, u32[]{:S(2)}) collective-permute-start(bf16[512,2048]{1,0:T(8,128)(2,1)} %shard_map.213), channel_id=1, source_target_pairs={{0,8},{8,0},{4,12},{12,4},{1,9},{9,1},{5,13},{13,5},{2,10},{10,2},... | collective-permute-start | bytes 6291464 | tf_op jit(solution)/shard_map/ppermute | solution.py:455
  1075.6 87.0 %collective-permute-start.41 = (bf16[512,2048]{1,0:T(8,128)(2,1)}, bf16[512,2048]{1,0:T(8,128)(2,1)}, u32[]{:S(2)}, u32[]{:S(2)}) collective-permute-start(bf16[512,2048]{1,0:T(8,128)(2,1)} %shard_map.210), channel_id=1, source_target_pairs={{0,8},{8,0},{4,12},{12,4},{1,9},{9,1},{5,13},{13,5},{2,10},{10,2},... | collective-permute-start | bytes 6291464 | tf_op jit(solution)/shard_map/ppermute | solution.py:455
  1075.9 62.9 %collective-permute-start.39 = (bf16[2048,256]{1,0:T(8,128)(2,1)}, bf16[2048,256]{1,0:T(8,128)(2,1)S(1)}, u32[]{:S(2)}, u32[]{:S(2)}) collective-permute-start(bf16[2048,256]{1,0:T(8,128)(2,1)} %get-tuple-element.211), channel_id=1, source_target_pairs={{0,4},{4,0},{8,12},{12,8},{1,5},{5,1},{9,13},{13,9},{2,6},{6,2},{1... | collective-permute-start | bytes 3145736 | tf_op jit(solution)/shard_map/ppermute | solution.py:451
  1075.9 69.6 %collective-permute-start.40 = (bf16[2048,256]{1,0:T(8,128)(2,1)}, bf16[2048,256]{1,0:T(8,128)(2,1)}, u32[]{:S(2)}, u32[]{:S(2)}) collective-permute-start(bf16[2048,256]{1,0:T(8,128)(2,1)} %get-tuple-element.212), channel_id=1, source_target_pairs={{0,4},{4,0},{8,12},{12,8},{1,5},{5,1},{9,13},{13,9},{2,6},{6,2},{1... | collective-permute-start | bytes 3145736 | tf_op jit(solution)/shard_map/ppermute | solution.py:451
  1080.4 171.0 %collective-permute-start.52 = (bf16[256,8192]{1,0:T(8,128)(2,1)S(1)}, bf16[256,8192]{1,0:T(8,128)(2,1)}, u32[]{:S(2)}, u32[]{:S(2)}) collective-permute-start(bf16[256,8192]{1,0:T(8,128)(2,1)S(1)} %copy-done.1), channel_id=1, source_target_pairs={{0,4},{4,0},{8,12},{12,8},{1,5},{5,1},{9,13},{13,9},{2,6},{6,2},{1... | collective-permute-start | bytes 12582920 | tf_op jit(solution)/shard_map/ppermute | solution.py:451
  1138.8 116.9 %collective-permute-start.51 = (bf16[256,8192]{1,0:T(8,128)(2,1)}, bf16[256,8192]{1,0:T(8,128)(2,1)}, u32[]{:S(2)}, u32[]{:S(2)}) collective-permute-start(bf16[256,8192]{1,0:T(8,128)(2,1)} %get-tuple-element.214.refs_9_.refs_4_), channel_id=1, source_target_pairs={{0,4},{4,0},{8,12},{12,8},{1,5},{5,1},{9,13},{13,9},{2,6},{6,2},{1... | collective-permute-start | bytes 12582920 | tf_op jit(solution)/shard_map/ppermute | solution.py:451
  1145.4 60.2 %collective-permute-start.57 = (bf16[512,2048]{1,0:T(8,128)(2,1)}, bf16[512,2048]{1,0:T(8,128)(2,1)}, u32[]{:S(2)}, u32[]{:S(2)}) collective-permute-start(bf16[512,2048]{1,0:T(8,128)(2,1)} %shard_map.222), channel_id=1, source_target_pairs={{0,8},{8,0},{4,12},{12,4},{1,9},{9,1},{5,13},{13,5},{2,10},{10,2},... | collective-permute-start | bytes 6291464 | tf_op jit(solution)/shard_map/ppermute | solution.py:455
  1221.9 54.9 %collective-permute-start.61 = (bf16[512,2048]{1,0:T(8,128)(2,1)}, bf16[512,2048]{1,0:T(8,128)(2,1)}, u32[]{:S(2)}, u32[]{:S(2)}) collective-permute-start(bf16[512,2048]{1,0:T(8,128)(2,1)} %shard_map.226), channel_id=1, source_target_pairs={{0,8},{8,0},{4,12},{12,4},{1,9},{9,1},{5,13},{13,5},{2,10},{10,2},... | collective-permute-start | bytes 6291464 | tf_op jit(solution)/shard_map/ppermute | solution.py:455
  1263.5 60.0 %collective-permute-start.56 = (bf16[512,2048]{1,0:T(8,128)(2,1)}, bf16[512,2048]{1,0:T(8,128)(2,1)}, u32[]{:S(2)}, u32[]{:S(2)}) collective-permute-start(bf16[512,2048]{1,0:T(8,128)(2,1)} %shard_map.221), channel_id=1, source_target_pairs={{0,8},{8,0},{4,12},{12,4},{1,9},{9,1},{5,13},{13,5},{2,10},{10,2},... | collective-permute-start | bytes 6291464 | tf_op jit(solution)/shard_map/ppermute | solution.py:455
  1269.1 42.7 %collective-permute-start.60 = (bf16[512,1024]{1,0:T(8,128)(2,1)}, bf16[512,1024]{1,0:T(8,128)(2,1)S(1)}, u32[]{:S(2)}, u32[]{:S(2)}) collective-permute-start(bf16[512,1024]{1,0:T(8,128)(2,1)} %get-tuple-element.237.refs_0_), channel_id=1, source_target_pairs={{0,1},{1,2},{4,5},{5,6},{8,9},{9,10},{12,13},{13,14},{16,17},{17,1... | collective-permute-start | bytes 3145736 | tf_op jit(solution)/shard_map/ppermute | solution.py:616
  1311.9 82.2 %collective-permute-start.80 = (bf16[512,2048]{1,0:T(8,128)(2,1)}, bf16[512,2048]{1,0:T(8,128)(2,1)}, u32[]{:S(2)}, u32[]{:S(2)}) collective-permute-start(bf16[512,2048]{1,0:T(8,128)(2,1)} %shard_map.233), channel_id=1, source_target_pairs={{0,8},{8,0},{4,12},{12,4},{1,9},{9,1},{5,13},{13,5},{2,10},{10,2},... | collective-permute-start | bytes 6291464 | tf_op jit(solution)/shard_map/ppermute | solution.py:455
  1318.9 49.3 %collective-permute-start.81 = (bf16[512,1024]{1,0:T(8,128)(2,1)}, bf16[512,1024]{1,0:T(8,128)(2,1)S(1)}, u32[]{:S(2)}, u32[]{:S(2)}) collective-permute-start(bf16[512,1024]{1,0:T(8,128)(2,1)} %get-tuple-element.257.refs_2_.refs_0_), channel_id=1, source_target_pairs={{0,1},{1,2},{2,3},{4,5},{5,6},{6,7},{8,9},{9,10},{10,11},{12,13},{... | collective-permute-start | bytes 3145736 | tf_op jit(solution)/shard_map/ppermute | solution.py:616
  1323.5 44.8 %collective-permute-start.82 = (bf16[512,1024]{1,0:T(8,128)(2,1)}, bf16[512,1024]{1,0:T(8,128)(2,1)S(1)}, u32[]{:S(2)}, u32[]{:S(2)}) collective-permute-start(bf16[512,1024]{1,0:T(8,128)(2,1)} %get-tuple-element.260.refs_3_.refs_1_), channel_id=1, source_target_pairs={{1,0},{2,1},{3,2},{5,4},{6,5},{7,6},{9,8},{10,9},{11,10},{13,12},{... | collective-permute-start | bytes 3145736 | tf_op jit(solution)/shard_map/ppermute | solution.py:617
  1336.9 45.4 %collective-permute-start.67 = (bf16[512,1024]{1,0:T(8,128)(2,1)}, bf16[512,1024]{1,0:T(8,128)(2,1)S(1)}, u32[]{:S(2)}, u32[]{:S(2)}) collective-permute-start(bf16[512,1024]{1,0:T(8,128)(2,1)} %get-tuple-element.246.refs_4_.refs_2_.refs_0_), channel_id=1, source_target_pairs={{0,1},{1,2},{2,3},{4,5},{5,6},{6,7},{8,9},{9,10},{10,11},{12,13},{... | collective-permute-start | bytes 3145736 | tf_op jit(solution)/shard_map/ppermute | solution.py:616
  1368.2 115.8 %collective-permute-start.79 = (bf16[256,8192]{1,0:T(8,128)(2,1)S(1)}, bf16[256,8192]{1,0:T(8,128)(2,1)}, u32[]{:S(2)}, u32[]{:S(2)}) collective-permute-start(bf16[256,8192]{1,0:T(8,128)(2,1)S(1)} %copy-done), channel_id=1, source_target_pairs={{0,4},{4,0},{8,12},{12,8},{1,5},{5,1},{9,13},{13,9},{2,6},{6,2},{1... | collective-permute-start | bytes 12582920 | tf_op jit(solution)/shard_map/ppermute | solution.py:451
  1368.3 120.3 %collective-permute-start.78 = (bf16[256,8192]{1,0:T(8,128)(2,1)}, bf16[256,8192]{1,0:T(8,128)(2,1)}, u32[]{:S(2)}, u32[]{:S(2)}) collective-permute-start(bf16[256,8192]{1,0:T(8,128)(2,1)} %get-tuple-element.254.refs_4_), channel_id=1, source_target_pairs={{0,4},{4,0},{8,12},{12,8},{1,5},{5,1},{9,13},{13,9},{2,6},{6,2},{1... | collective-permute-start | bytes 12582920 | tf_op jit(solution)/shard_map/ppermute | solution.py:451
  1382.4 63.0 %collective-permute-start.87 = (bf16[512,2048]{1,0:T(8,128)(2,1)}, bf16[512,2048]{1,0:T(8,128)(2,1)}, u32[]{:S(2)}, u32[]{:S(2)}) collective-permute-start(bf16[512,2048]{1,0:T(8,128)(2,1)} %shard_map.239), channel_id=1, source_target_pairs={{0,8},{8,0},{4,12},{12,4},{1,9},{9,1},{5,13},{13,5},{2,10},{10,2},... | collective-permute-start | bytes 6291464 | tf_op jit(solution)/shard_map/ppermute | solution.py:455
  1403.0 40.1 %collective-permute-start.84 = (bf16[512,1024]{1,0:T(8,128)(2,1)}, bf16[512,1024]{1,0:T(8,128)(2,1)S(1)}, u32[]{:S(2)}, u32[]{:S(2)}) collective-permute-start(bf16[512,1024]{1,0:T(8,128)(2,1)} %get-tuple-element.262.refs_5_.refs_3_.refs_1_), channel_id=1, source_target_pairs={{1,0},{2,1},{3,2},{5,4},{6,5},{7,6},{9,8},{10,9},{11,10},{13,12},{... | collective-permute-start | bytes 3145736 | tf_op jit(solution)/shard_map/ppermute | solution.py:617
  1422.1 86.1 %collective-permute-start.69 = (bf16[768,2048]{1,0:T(8,128)(2,1)}, bf16[768,2048]{1,0:T(8,128)(2,1)}, u32[]{:S(2)}, u32[]{:S(2)}) collective-permute-start(bf16[768,2048]{1,0:T(8,128)(2,1)} %fusion.1), channel_id=1, source_target_pairs={{0,8},{8,0},{4,12},{12,4},{1,9},{9,1},{5,13},{13,5},{2,10},{10,2},... | collective-permute-start | bytes 9437192 | tf_op jit(solution)/shard_map/ppermute | solution.py:455
  1496.1 74.4 %collective-permute-start.95 = (bf16[512,2048]{1,0:T(8,128)(2,1)}, bf16[512,2048]{1,0:T(8,128)(2,1)}, u32[]{:S(2)}, u32[]{:S(2)}) collective-permute-start(bf16[512,2048]{1,0:T(8,128)(2,1)} %shard_map.245), channel_id=1, source_target_pairs={{0,8},{8,0},{4,12},{12,4},{1,9},{9,1},{5,13},{13,5},{2,10},{10,2},... | collective-permute-start | bytes 6291464 | tf_op jit(solution)/shard_map/ppermute | solution.py:455
  1536.1 63.3 %collective-permute-start.102 = (bf16[512,2048]{1,0:T(8,128)(2,1)}, bf16[512,2048]{1,0:T(8,128)(2,1)}, u32[]{:S(2)}, u32[]{:S(2)}) collective-permute-start(bf16[512,2048]{1,0:T(8,128)(2,1)} %shard_map.251), channel_id=1, source_target_pairs={{0,8},{8,0},{4,12},{12,4},{1,9},{9,1},{5,13},{13,5},{2,10},{10,2},... | collective-permute-start | bytes 6291464 | tf_op jit(solution)/shard_map/ppermute | solution.py:455
  1540.3 37.7 %collective-permute-start.100 = (bf16[512,1024]{1,0:T(8,128)(2,1)S(1)}, bf16[512,1024]{1,0:T(8,128)(2,1)S(1)}, u32[]{:S(2)}, u32[]{:S(2)}) collective-permute-start(bf16[512,1024]{1,0:T(8,128)(2,1)S(1)} %copy-done.76), channel_id=1, source_target_pairs={{1,0},{2,1},{3,2},{5,4},{6,5},{7,6},{9,8},{10,9},{11,10},{13,12},{... | collective-permute-start | bytes 3145736 | tf_op jit(solution)/shard_map/ppermute | solution.py:617
  1548.3 40.0 %collective-permute-start.98 = (bf16[512,1024]{1,0:T(8,128)(2,1)}, bf16[512,1024]{1,0:T(8,128)(2,1)S(1)}, u32[]{:S(2)}, u32[]{:S(2)}) collective-permute-start(bf16[512,1024]{1,0:T(8,128)(2,1)} %get-tuple-element.279.refs_2_.refs_0_.refs_4_), channel_id=1, source_target_pairs={{0,1},{1,2},{2,3},{4,5},{5,6},{6,7},{8,9},{9,10},{10,11},{12,13},{... | collective-permute-start | bytes 3145736 | tf_op jit(solution)/shard_map/ppermute | solution.py:616
  1570.5 85.5 %collective-permute-start.94 = (bf16[512,2048]{1,0:T(8,128)(2,1)}, bf16[512,2048]{1,0:T(8,128)(2,1)}, u32[]{:S(2)}, u32[]{:S(2)}) collective-permute-start(bf16[512,2048]{1,0:T(8,128)(2,1)} %shard_map.244), channel_id=1, source_target_pairs={{0,8},{8,0},{4,12},{12,4},{1,9},{9,1},{5,13},{13,5},{2,10},{10,2},... | collective-permute-start | bytes 6291464 | tf_op jit(solution)/shard_map/ppermute | solution.py:455
  1594.8 39.7 %collective-permute-start.101 = (bf16[512,1024]{1,0:T(8,128)(2,1)}, bf16[512,1024]{1,0:T(8,128)(2,1)S(1)}, u32[]{:S(2)}, u32[]{:S(2)}) collective-permute-start(bf16[512,1024]{1,0:T(8,128)(2,1)} %get-tuple-element.282.refs_4_.refs_2_.refs_0_), channel_id=1, source_target_pairs={{0,1},{1,2},{2,3},{4,5},{5,6},{6,7},{8,9},{9,10},{10,11},{12,13},{... | collective-permute-start | bytes 3145736 | tf_op jit(solution)/shard_map/ppermute | solution.py:616
  1599.4 39.5 %collective-permute-start.107 = (bf16[512,1024]{1,0:T(8,128)(2,1)}, bf16[512,1024]{1,0:T(8,128)(2,1)S(1)}, u32[]{:S(2)}, u32[]{:S(2)}) collective-permute-start(bf16[512,1024]{1,0:T(8,128)(2,1)} %get-tuple-element.290.refs_5_.refs_3_.refs_1_), channel_id=1, source_target_pairs={{1,0},{2,1},{3,2},{5,4},{6,5},{7,6},{9,8},{10,9},{11,10},{13,12},{... | collective-permute-start | bytes 3145736 | tf_op jit(solution)/shard_map/ppermute | solution.py:617
  1654.5 48.0 %collective-permute-start.110 = (bf16[512,2048]{1,0:T(8,128)(2,1)}, bf16[512,2048]{1,0:T(8,128)(2,1)}, u32[]{:S(2)}, u32[]{:S(2)}) collective-permute-start(bf16[512,2048]{1,0:T(8,128)(2,1)} %shard_map.257), channel_id=1, source_target_pairs={{0,8},{8,0},{4,12},{12,4},{1,9},{9,1},{5,13},{13,5},{2,10},{10,2},... | collective-permute-start | bytes 6291464 | tf_op jit(solution)/shard_map/ppermute | solution.py:455
  1692.9 47.7 %collective-permute-start.115 = (bf16[512,1024]{1,0:T(8,128)(2,1)}, bf16[512,1024]{1,0:T(8,128)(2,1)}, u32[]{:S(2)}, u32[]{:S(2)}) collective-permute-start(bf16[512,1024]{1,0:T(8,128)(2,1)} %get-tuple-element.299.refs_5_.refs_3_.refs_1_), channel_id=1, source_target_pairs={{1,0},{2,1},{3,2},{5,4},{6,5},{7,6},{9,8},{10,9},{11,10},{13,12},{... | collective-permute-start | bytes 3145736 | tf_op jit(solution)/shard_map/ppermute | solution.py:617
  1702.4 52.3 %collective-permute-start.75 = (bf16[256,3072]{1,0:T(8,128)(2,1)S(1)}, bf16[256,3072]{1,0:T(8,128)(2,1)S(1)}, u32[]{:S(2)}, u32[]{:S(2)}) collective-permute-start(bf16[256,3072]{1,0:T(8,128)(2,1)S(1)} %pad_maximum_fusion.refs_5_), channel_id=1, source_target_pairs={{0,4},{4,0},{8,12},{12,8},{1,5},{5,1},{9,13},{13,9},{2,6},{6,2},{1... | collective-permute-start | bytes 4718600 | tf_op jit(solution)/shard_map/ppermute | solution.py:451
  1702.5 74.9 %collective-permute-start.123 = (bf16[512,2048]{1,0:T(8,128)(2,1)}, bf16[512,2048]{1,0:T(8,128)(2,1)}, u32[]{:S(2)}, u32[]{:S(2)}) collective-permute-start(bf16[512,2048]{1,0:T(8,128)(2,1)} %shard_map.264), channel_id=1, source_target_pairs={{0,8},{8,0},{4,12},{12,4},{1,9},{9,1},{5,13},{13,5},{2,10},{10,2},... | collective-permute-start | bytes 6291464 | tf_op jit(solution)/shard_map/ppermute | solution.py:455
  1766.5 58.7 %collective-permute-start.72 = (bf16[512,256]{1,0:T(8,128)(2,1)S(1)}, bf16[512,256]{1,0:T(8,128)(2,1)S(1)}, u32[]{:S(2)}, u32[]{:S(2)}) collective-permute-start(bf16[512,256]{1,0:T(8,128)(2,1)S(1)} %copy-done.159), channel_id=1, source_target_pairs={{0,4},{4,0},{8,12},{12,8},{1,5},{5,1},{9,13},{13,9},{2,6},{6,2},{1... | collective-permute-start | bytes 786440 | tf_op jit(solution)/shard_map/ppermute | solution.py:451
  1766.8 59.6 %collective-permute-start.73 = (bf16[512,256]{1,0:T(8,128)(2,1)}, bf16[512,256]{1,0:T(8,128)(2,1)S(1)}, u32[]{:S(2)}, u32[]{:S(2)}) collective-permute-start(bf16[512,256]{1,0:T(8,128)(2,1)} %get-tuple-element.250), channel_id=1, source_target_pairs={{0,4},{4,0},{8,12},{12,8},{1,5},{5,1},{9,13},{13,9},{2,6},{6,2},{1... | collective-permute-start | bytes 786440 | tf_op jit(solution)/shard_map/ppermute | solution.py:451
  1776.7 55.9 %collective-permute-start.109 = (bf16[512,2048]{1,0:T(8,128)(2,1)}, bf16[512,2048]{1,0:T(8,128)(2,1)}, u32[]{:S(2)}, u32[]{:S(2)}) collective-permute-start(bf16[512,2048]{1,0:T(8,128)(2,1)} %shard_map.256), channel_id=1, source_target_pairs={{0,8},{8,0},{4,12},{12,4},{1,9},{9,1},{5,13},{13,5},{2,10},{10,2},... | collective-permute-start | bytes 6291464 | tf_op jit(solution)/shard_map/ppermute | solution.py:455
  1826.5 39.7 %collective-permute-start.129 = (bf16[512,1024]{1,0:T(8,128)(2,1)}, bf16[512,1024]{1,0:T(8,128)(2,1)S(1)}, u32[]{:S(2)}, u32[]{:S(2)}) collective-permute-start(bf16[512,1024]{1,0:T(8,128)(2,1)} %get-tuple-element.317.refs_4_.refs_2_.refs_0_), channel_id=1, source_target_pairs={{0,1},{1,2},{2,3},{4,5},{5,6},{6,7},{8,9},{9,10},{10,11},{12,13},{... | collective-permute-start | bytes 3145736 | tf_op jit(solution)/shard_map/ppermute | solution.py:616
  1831.1 43.3 %collective-permute-start.130 = (bf16[512,1024]{1,0:T(8,128)(2,1)}, bf16[512,1024]{1,0:T(8,128)(2,1)S(1)}, u32[]{:S(2)}, u32[]{:S(2)}) collective-permute-start(bf16[512,1024]{1,0:T(8,128)(2,1)} %get-tuple-element.318.refs_5_.refs_3_.refs_1_), channel_id=1, source_target_pairs={{1,0},{2,1},{3,2},{5,4},{6,5},{7,6},{9,8},{10,9},{11,10},{13,12},{... | collective-permute-start | bytes 3145736 | tf_op jit(solution)/shard_map/ppermute | solution.py:617
  1832.7 59.4 %collective-permute-start.71 = (bf16[2,512]{1,0:T(2,128)(2,1)S(1)}, bf16[2,512]{1,0:T(2,128)(2,1)S(1)}, u32[]{:S(2)}, u32[]{:S(2)}) collective-permute-start(bf16[2,512]{1,0:T(2,128)(2,1)S(1)} %constant_dynamic-slice_fusion), channel_id=1, source_target_pairs={{0,8},{8,0},{4,12},{12,4},{1,9},{9,1},{5,13},{13,5},{2,10},{10,2},... | collective-permute-start | bytes 6152 | tf_op jit(solution)/shard_map/ppermute | solution.py:455
  1845.0 49.5 %collective-permute-start.137 = (bf16[512,1024]{1,0:T(8,128)(2,1)S(1)}, bf16[512,1024]{1,0:T(8,128)(2,1)}, u32[]{:S(2)}, u32[]{:S(2)}) collective-permute-start(bf16[512,1024]{1,0:T(8,128)(2,1)S(1)} %copy-done.123), channel_id=1, source_target_pairs={{0,8},{8,0},{4,12},{12,4},{1,9},{9,1},{5,13},{13,5},{2,10},{10,2},... | collective-permute-start | bytes 3145736 | tf_op jit(solution)/shard_map/ppermute | solution.py:455
  1887.5 38.7 %collective-permute-start.133 = (bf16[512,1024]{1,0:T(8,128)(2,1)}, bf16[512,1024]{1,0:T(8,128)(2,1)S(1)}, u32[]{:S(2)}, u32[]{:S(2)}) collective-permute-start(bf16[512,1024]{1,0:T(8,128)(2,1)} %get-tuple-element.322.refs_4_.refs_2_.refs_0_), channel_id=1, source_target_pairs={{0,1},{1,2},{2,3},{4,5},{5,6},{6,7},{8,9},{9,10},{10,11},{12,13},{... | collective-permute-start | bytes 3145736 | tf_op jit(solution)/shard_map/ppermute | solution.py:616
  1892.1 38.1 %collective-permute-start.134 = (bf16[512,1024]{1,0:T(8,128)(2,1)}, bf16[512,1024]{1,0:T(8,128)(2,1)S(1)}, u32[]{:S(2)}, u32[]{:S(2)}) collective-permute-start(bf16[512,1024]{1,0:T(8,128)(2,1)} %get-tuple-element.323.refs_5_.refs_3_.refs_1_), channel_id=1, source_target_pairs={{1,0},{2,1},{3,2},{5,4},{6,5},{7,6},{9,8},{10,9},{11,10},{13,12},{... | collective-permute-start | bytes 3145736 | tf_op jit(solution)/shard_map/ppermute | solution.py:617
  1943.4 37.5 %collective-permute-start.138 = (bf16[512,1024]{1,0:T(8,128)(2,1)}, bf16[512,1024]{1,0:T(8,128)(2,1)S(1)}, u32[]{:S(2)}, u32[]{:S(2)}) collective-permute-start(bf16[512,1024]{1,0:T(8,128)(2,1)} %get-tuple-element.326.refs_0_.refs_4_.refs_2_), channel_id=1, source_target_pairs={{0,1},{1,2},{2,3},{4,5},{5,6},{6,7},{8,9},{9,10},{10,11},{12,13},{... | collective-permute-start | bytes 3145736 | tf_op jit(solution)/shard_map/ppermute | solution.py:616
  1996.6 41.0 %collective-permute-start.143 = (bf16[512,1024]{1,0:T(8,128)(2,1)}, bf16[512,1024]{1,0:T(8,128)(2,1)S(1)}, u32[]{:S(2)}, u32[]{:S(2)}) collective-permute-start(bf16[512,1024]{1,0:T(8,128)(2,1)} %get-tuple-element.331.refs_1_.refs_3_.refs_5_), channel_id=1, source_target_pairs={{1,0},{2,1},{5,4},{6,5},{9,8},{10,9},{13,12},{14,13},{17,16},{18,1... | collective-permute-start | bytes 3145736 | tf_op jit(solution)/shard_map/ppermute | solution.py:617
  2042.0 74.2 %collective-permute-start.144 = (bf16[512,1024]{1,0:T(8,128)(2,1)}, bf16[512,1024]{1,0:T(8,128)(2,1)}, u32[]{:S(2)}, u32[]{:S(2)}) collective-permute-start(bf16[512,1024]{1,0:T(8,128)(2,1)} %get-tuple-element.332.refs_2_.refs_4_), channel_id=1, source_target_pairs={{1,2},{2,3},{5,6},{6,7},{9,10},{10,11},{13,14},{14,15},{17,18},{18... | collective-permute-start | bytes 3145736 | tf_op jit(solution)/shard_map/ppermute | solution.py:616
  2043.7 72.5 %collective-permute-start.145 = (bf16[512,1024]{1,0:T(8,128)(2,1)}, bf16[512,1024]{1,0:T(8,128)(2,1)}, u32[]{:S(2)}, u32[]{:S(2)}) collective-permute-start(bf16[512,1024]{1,0:T(8,128)(2,1)} %get-tuple-element.333.refs_3_.refs_5_), channel_id=1, source_target_pairs={{1,0},{5,4},{9,8},{13,12},{17,16},{21,20},{25,24},{29,28}} | collective-permute-start | bytes 3145736 | tf_op jit(solution)/shard_map/ppermute | solution.py:617
  2048.5 67.7 %collective-permute-start.146 = (bf16[512,1024]{1,0:T(8,128)(2,1)}, bf16[512,1024]{1,0:T(8,128)(2,1)}, u32[]{:S(2)}, u32[]{:S(2)}) collective-permute-start(bf16[512,1024]{1,0:T(8,128)(2,1)} %get-tuple-element.334.refs_2_.refs_0_.refs_4_), channel_id=1, source_target_pairs={{1,2},{2,3},{5,6},{6,7},{9,10},{10,11},{13,14},{14,15},{17,18},{18... | collective-permute-start | bytes 3145736 | tf_op jit(solution)/shard_map/ppermute | solution.py:616
  2050.1 66.1 %collective-permute-start.147 = (bf16[512,1024]{1,0:T(8,128)(2,1)}, bf16[512,1024]{1,0:T(8,128)(2,1)}, u32[]{:S(2)}, u32[]{:S(2)}) collective-permute-start(bf16[512,1024]{1,0:T(8,128)(2,1)} %get-tuple-element.335.refs_3_.refs_1_.refs_5_), channel_id=1, source_target_pairs={{1,0},{5,4},{9,8},{13,12},{17,16},{21,20},{25,24},{29,28}} | collective-permute-start | bytes 3145736 | tf_op jit(solution)/shard_map/ppermute | solution.py:617
  2119.3 68.1 %collective-permute-start.148 = (bf16[512,1024]{1,0:T(8,128)(2,1)}, bf16[512,1024]{1,0:T(8,128)(2,1)}, u32[]{:S(2)}, u32[]{:S(2)}) collective-permute-start(bf16[512,1024]{1,0:T(8,128)(2,1)} %get-tuple-element.336.refs_4_), channel_id=1, source_target_pairs={{2,3},{6,7},{10,11},{14,15},{18,19},{22,23},{26,27},{30,31}} | collective-permute-start | bytes 3145736 | tf_op jit(solution)/shard_map/ppermute | solution.py:616
  2121.0 66.4 %collective-permute-start.149 = (bf16[512,1024]{1,0:T(8,128)(2,1)}, bf16[512,1024]{1,0:T(8,128)(2,1)}, u32[]{:S(2)}, u32[]{:S(2)}) collective-permute-start(bf16[512,1024]{1,0:T(8,128)(2,1)} %get-tuple-element.337.refs_5_), channel_id=1, source_target_pairs={} | collective-permute-start | bytes 3145736 | tf_op jit(solution)/shard_map/ppermute | solution.py:617
  2134.0 57.8 %collective-permute-start.150 = (bf16[512,1024]{1,0:T(8,128)(2,1)}, bf16[512,1024]{1,0:T(8,128)(2,1)S(1)}, u32[]{:S(2)}, u32[]{:S(2)}) collective-permute-start(bf16[512,1024]{1,0:T(8,128)(2,1)} %get-tuple-element.340.refs_4_.refs_2_), channel_id=1, source_target_pairs={{2,3},{6,7},{10,11},{14,15},{18,19},{22,23},{26,27},{30,31}} | collective-permute-start | bytes 3145736 | tf_op jit(solution)/shard_map/ppermute | solution.py:616
  2134.8 56.9 %collective-permute-start.151 = (bf16[512,1024]{1,0:T(8,128)(2,1)}, bf16[512,1024]{1,0:T(8,128)(2,1)}, u32[]{:S(2)}, u32[]{:S(2)}) collective-permute-start(bf16[512,1024]{1,0:T(8,128)(2,1)} %get-tuple-element.341.refs_5_.refs_3_), channel_id=1, source_target_pairs={} | collective-permute-start | bytes 3145736 | tf_op jit(solution)/shard_map/ppermute | solution.py:617
  (256 other events, 6479.7 us)
Sparse Core Ops, SparseCore 0:
  55.9 82.2 all-gather.7
  180.7 47.6 all-gather.5
  230.5 79.3 all-gather.9
  311.4 148.1 all-gather.11

commit v5 on v4

--- a/solution.py
+++ b/solution.py
@@ -562,7 +562,7 @@
     )(place, *unique, *earlier)
 
 
-def replica_chain(count, make, shape, kind, stream_count=STREAMS, wanted=None):
+def replica_chain(count, make, shape, kind, stream_count=STREAMS, wanted=None, done=None):
     peers = lax.axis_size("dp")
     place = lax.axis_index("dp")
     place_vector = place.astype(jnp.int32).reshape(1)
@@ -574,6 +574,10 @@
     downs = [[] for _ in streams]
     sent = [[] for _ in streams]
     order = []
+    tokens = []
+    choice = 2 * jnp.abs(place - root) + (place < root).astype(jnp.int32)
+    choice = choice.astype(jnp.int32).reshape(1)
+    found = []
     lags = [
         position if position < root else delay if position == root else peers - 1 - position
         for position in range(peers)
@@ -608,20 +612,22 @@
             earlier = ()
             if stream_count > 1 and len(order) > stream_count:
                 earlier = order[-(stream_count + 1)]
+            if len(tokens) >= 2:
+                earlier = (*earlier, tokens[-2])
             up, down = relay(place_vector, root, places, operands, earlier, shape, kind)
             sent[q].append((up, down))
+            at = step - 2 * delay
+            if at >= 0:
+                found = [x for hops in range(delay + 1) for x in sent[q][at + delay + hops]]
+                token = done(q + at * stream_count, choice, found)
+                if token is not None:
+                    tokens.append(token)
             if step < counts[q] + 2 * delay - 1:
                 up_pairs = [(i, i + 1) for i in range(peers - 1) if 0 <= going(i, 1, step) < counts[q]]
                 down_pairs = [(i, i - 1) for i in range(1, peers) if 0 <= going(i, -1, step) < counts[q]]
                 ups[q].append(lax.ppermute(up, "dp", up_pairs))
                 downs[q].append(lax.ppermute(down, "dp", down_pairs))
                 order.append((ups[q][-1], downs[q][-1]))
-    choice = 2 * jnp.abs(place - root) + (place < root).astype(jnp.int32)
-    found = []
-    for index in range(count):
-        at, q = divmod(index, stream_count)
-        found.append([x for hops in range(delay + 1) for x in sent[q][at + delay + hops]])
-    return choice.astype(jnp.int32).reshape(1), found
 
 
 def place_chunk(choice, found, whole, shape, row, column, tile=128):
@@ -633,7 +639,9 @@
 
             @pl.when(choice_ref[0] == index)
             def _():
-                refs[-1][...] = refs[index][...].astype(F32)
+                refs[-2][...] = refs[index][...].astype(F32)
+
+        refs[-1][...] = jnp.zeros(refs[-1].shape, F32)
 
     def chosen(index):
         return lambda t, s: (jnp.where(s[0] == index, t, 0), 0)
@@ -645,9 +653,15 @@
             grid=(per,),
             in_specs=[pl.BlockSpec((tile, CHUNK_COLS), chosen(k)) for k in range(len(found))]
             + [pl.BlockSpec(memory_space=pl.ANY)] * len(kept),
-            out_specs=pl.BlockSpec((tile, CHUNK_COLS), lambda t, s: (row * per + t, column)),
+            out_specs=[
+                pl.BlockSpec((tile, CHUNK_COLS), lambda t, s: (row * per + t, column)),
+                pl.BlockSpec((8, LANES), lambda t, s: (0, 0)),
+            ],
         ),
-        out_shape=jax.ShapeDtypeStruct(shape, F32),
+        out_shape=[
+            jax.ShapeDtypeStruct(shape, F32),
+            jax.ShapeDtypeStruct((8, LANES), F32),
+        ],
         input_output_aliases={1 + len(found): 0} if kept else {},
         compiler_params=pltpu.CompilerParams(vmem_limit_bytes=VMEM),
         cost_estimate=pl.CostEstimate(flops=1, bytes_accessed=1, transcendentals=0),
@@ -943,29 +957,38 @@
         return made[index]
 
     count = sum(width // CHUNK_COLS for _, _, _, width in plan) + 1
-    choice, found = replica_chain(count, make, (CHUNK_ROWS, CHUNK_COLS), BF, wanted=wanted)
+    results = {}
+    table = []
+    for name, rows, cols in (
+        ("down", w_down.shape[1], w_down.shape[2]),
+        ("gate", w_gate.shape[1], w_gate.shape[2]),
+        ("up", w_up.shape[1], w_up.shape[2]),
+        ("out", w_out.shape[1], w_out.shape[2]),
+        ("query", w_query.shape[1], query_width),
+        ("pairs", w_query.shape[1], 2 * key_width),
+    ):
+        for row in range(rows // CHUNK_ROWS):
+            for column in range(cols // CHUNK_COLS):
+                table.append((name, (rows, cols), row, column))
+
+    def done(index, choice, found):
+        if index == count - 1:
+            last = [x[: gains_b.shape[0], : model_width // 4] for x in found]
+            gains = last[0]
+            for at, x in enumerate(last):
+                gains = jnp.where(choice[0] == at, x, gains)
+            results["gains"] = gains.astype(F32)
+            return None
+        name, shape, row, column = table[index]
+        whole = results.get(name)
+        results[name], token = place_chunk(choice, found, whole, shape, row, column)
+        return token
+
+    replica_chain(count, make, (CHUNK_ROWS, CHUNK_COLS), BF, wanted=wanted, done=done)
     grad_two = work["done"][0]
-
-    last = [x[: gains_b.shape[0], : model_width // 4] for x in found.pop()]
-    gains = last[0]
-    for index, x in enumerate(last):
-        gains = jnp.where(choice[0] == index, x, gains)
-    gains = gains.astype(F32)
-
-    def assembled(rows, cols):
-        whole = None
-        across = cols // CHUNK_COLS
-        for index in range(rows // CHUNK_ROWS * across):
-            row, column = divmod(index, across)
-            whole = place_chunk(choice, found.pop(0), whole, (rows, cols), row, column)
-        return whole
-
-    grad_down = assembled(w_down.shape[1], w_down.shape[2])
-    grad_gate = assembled(w_gate.shape[1], w_gate.shape[2])
-    grad_up = assembled(w_up.shape[1], w_up.shape[2])
-    grad_out = assembled(w_out.shape[1], w_out.shape[2])
-    grad_query = assembled(w_query.shape[1], query_width)
-    grad_both = assembled(w_query.shape[1], 2 * key_width)
+    gains = results["gains"]
+    grad_down, grad_gate, grad_up = results["down"], results["gate"], results["up"]
+    grad_out, grad_query, grad_both = results["out"], results["query"], results["pairs"]
     grad_pairs = [grad_both[:, at : at + LANES] for at in range(0, 2 * key_width, LANES)]
     boundary = choose(jnp.stack([grad_one, grad_two]), jnp.stack([output_one, output_two]))
     return (

time: 2230 us -> 2190 us (0.982)
  waiting for transfers between devices: 714 us -> 667 us
    ppermute x36, waiting for transfers between devices: 190 us -> 146 us  [replica_chain(): ups[q].append(lax.ppermute(up, 'dp', up_pairs))]
    unnamed x348 -> x340, local copies, waits for them, and re-layouts: 57.5 us -> 58.5 us
  transfers between devices with their start and end apart: 156 -> 156, of which waited for: 59 -> 52; matrix products, arithmetic and copies ran while one was open for 8% -> 8% of each run, Pallas kernels for 30% -> 30%
where the time goes in v5:
time: 2190 us; the launch traced here: 2170 us
  Pallas kernels  901 us (41%)
  waiting for transfers between devices  667 us (30%)
  starting transfers between devices  296 us (14%)
  local copies, waits for them, and re-layouts  126 us (6%)
  other arithmetic  81.9 us (4%)
  matrix products  63.5 us (3%)
    ppermute x27, waiting for transfers between devices, chip_swap(): return lax.ppermute(x, 'fsdp', [(0, 2), (2, 0), (1, 3), (3, 1)])  220 us
    pallas_call x30, Pallas kernels, outer(): pl.pallas_call(kernel, grid=(count * per,), in_specs=[pl.BlockSpec((CHUNK...  192 us
    pallas_call x3, Pallas kernels, hidden_back(): pl.pallas_call(hidden_back_kernel, grid_spec=pltpu.PrefetchScalarGridSpec...  170 us
    pallas_call x38, Pallas kernels, relay(): pl.pallas_call(kernel, grid_spec=pltpu.PrefetchScalarGridSpec(num_scalar_...  151 us
    ppermute x36, waiting for transfers between devices, replica_chain(): ups[q].append(lax.ppermute(up, 'dp', up_pairs))  146 us
    ppermute x36, waiting for transfers between devices, replica_chain(): downs[q].append(lax.ppermute(down, 'dp', down_pairs))  131 us
    ppermute x36, starting transfers between devices, replica_chain(): ups[q].append(lax.ppermute(up, 'dp', up_pairs))  130 us
    pallas_call x29, Pallas kernels, place_chunk(): pl.pallas_call(kernel, grid_spec=pltpu.PrefetchScalarGridSpec(num_scalar_...  118 us
  transfers between devices with their start and end apart: 156, of which 52 were waited for; matrix products, arithmetic and copies ran while one was open for 8% of the time, Pallas kernels for 30%

profile of v5, /device:TPU:0, one launch (start us, length us, event | category | flops | bytes accessed | tf_op | source)
XLA Modules:
  0.0 2165.4 jit_solution(14861944119688088493)
XLA Ops:
  39.8 15.0 collective-permute-done.1
  69.3 67.7 %collective-permute-done.2 = bf16[512,3072]{1,0:T(8,128)(2,1)} collective-permute-done((bf16[512,3072]{1,0:T(8,128)(2,1)S(1)}, bf16[512,3072]{1,0:T(8,128)(2,1)}, u32[]{:S(2)}, u32[]{:S(2)}) %collective-permute-start.2) | collective-permute-done | bytes 3145760 | tf_op jit(solution)/shard_map/ppermute | solution.py:455
  144.0 21.7 %collective-permute-done.8 = bf16[128,4096]{1,0:T(8,128)(2,1)S(1)} collective-permute-done((bf16[128,4096]{1,0:T(8,128)(2,1)S(1)}, bf16[128,4096]{1,0:T(8,128)(2,1)S(1)}, u32[]{:S(2)}, u32[]{:S(2)}) %collective-permute-start.8) | collective-permute-done | bytes 1048608 | tf_op jit(solution)/shard_map/ppermute | solution.py:455
  170.2 9.5 collective-permute-done.9
  204.3 36.1 %collective-permute-done.14 = bf16[128,8192]{1,0:T(8,128)(2,1)} collective-permute-done((bf16[128,8192]{1,0:T(8,128)(2,1)}, bf16[128,8192]{1,0:T(8,128)(2,1)}, u32[]{:S(2)}, u32[]{:S(2)}) %collective-permute-start.14) | collective-permute-done | bytes 2097184 | tf_op jit(solution)/shard_map/ppermute | solution.py:455
  253.0 10.5 shard_map.186
  265.2 12.1 collective-permute-done.5
  285.1 8.7 select_select_fusion
  299.4 15.5 collective-permute-done.7
  322.5 7.0 shard_map.187
  348.4 111.2 %all-gather.12.cloned.1.call-done.refs_0_ = bf16[512,8192]{1,0:T(8,128)(2,1)} async-done(((bf16[128,8192]{1,0:T(8,128)(2,1)}), bf16[512,8192]{1,0:T(8,128)(2,1)}) %all-gather.12.cloned.1.call-update) | async-done | bytes 8388624 | tf_op jit(solution)/shard_map/all_gather | solution.py:716
  459.6 17.0 collective-permute-done.17.refs_0_
  477.2 34.3 %shard_map.189 = (bf16[256,8192]{1,0:T(8,128)(2,1)}, bf16[256,8192]{1,0:T(8,128)(2,1)}, bf16[256,8192]{1,0:T(8,128)(2,1)}) custom-call(s32[1]{0:T(128)} %bitcast.2.shard_ref, bf16[256,2048]{1,0:T(8,128)(2,1)} %multiply_convert_fusion.2.refs_1_.b_ref, bf16[512,8192]{1,0:T(8,128)(2,1)} %bitcast.139, bf16[512,8192]{1,0:T(8,128)(2,1)} %collective-permute-done.11.refs_1_.refs_5_, ...), custom_call_target="tpu_custom_call" | custom-call | flops 1 | bytes 1 | tf_op jit(solution)/shard_map/pallas_call | solution.py:293
  511.4 19.8 shard_map.191
  539.5 20.9 collective-permute-done.19
  562.2 10.5 shard_map.192
  574.3 11.7 collective-permute-done.21
  604.8 34.4 %shard_map.194 = (bf16[256,8192]{1,0:T(8,128)(2,1)}, bf16[256,8192]{1,0:T(8,128)(2,1)}, bf16[256,8192]{1,0:T(8,128)(2,1)}) custom-call(s32[1]{0:T(128)} %bitcast.2.shard_ref, bf16[256,2048]{1,0:T(8,128)(2,1)} %multiply_convert_fusion.1.b_ref.refs_0_.refs_1_.refs_2_.refs_3_, bf16[512,8192]{1,0:T(8,128)(2,1)} %bitcast.140, ...), custom_call_target="tpu_custom_call" | custom-call | flops 1 | bytes 1 | tf_op jit(solution)/shard_map/pallas_call | solution.py:293
  639.3 56.3 %shard_map.195 = (bf16[256,8192]{1,0:T(8,128)(2,1)}, bf16[256,8192]{1,0:T(8,128)(2,1)}, f32[256,2048]{1,0:T(8,128)}) custom-call(s32[1]{0:T(128)} %bitcast.2.shard_ref, bf16[256,2048]{1,0:T(8,128)(2,1)} %slice_bitcast_fusion.dy_ref, bf16[256,8192]{1,0:T(8,128)(2,1)} %get-tuple-element.241.g_ref, bf16[256,8192]{1,0:T(8,128)(2,1)} %get-tuple-element.242.u_ref, ...), custom_call_target="tpu_custom_call" | custom-call | flops 1 | bytes 1 | tf_op jit(solution)/shard_map/pallas_call | solution.py:390
  697.8 6.9 convolution_convert_fusion.2.do_ref
  704.7 10.5 shard_map.196
  717.5 8.4 collective-permute-start.24
  729.1 17.4 collective-permute-start.25
  746.6 19.3 shard_map.197
  776.4 7.2 fusion.13
  783.7 13.5 collective-permute-done.27
  803.0 10.5 shard_map.199
  813.8 13.0 collective-permute-done.29
  854.1 34.3 %shard_map.201 = (bf16[256,8192]{1,0:T(8,128)(2,1)}, bf16[256,8192]{1,0:T(8,128)(2,1)}, bf16[256,8192]{1,0:T(8,128)(2,1)}) custom-call(s32[1]{0:T(128)} %bitcast.2.shard_ref, bf16[256,2048]{1,0:T(8,128)(2,1)} %multiply_convert_fusion.b_ref.refs_0_.refs_1_.refs_2_.refs_3_, bf16[512,8192]{1,0:T(8,128)(2,1)} %bitcast.142, ...), custom_call_target="tpu_custom_call" | custom-call | flops 1 | bytes 1 | tf_op jit(solution)/shard_map/pallas_call | solution.py:293
  890.6 56.8 %shard_map.202 = (bf16[256,8192]{1,0:T(8,128)(2,1)}, bf16[256,8192]{1,0:T(8,128)(2,1)}, f32[256,2048]{1,0:T(8,128)}) custom-call(s32[1]{0:T(128)} %bitcast.2.shard_ref, bf16[256,2048]{1,0:T(8,128)(2,1)} %bitcast_select_fusion.dy_ref.refs_5_, bf16[256,8192]{1,0:T(8,128)(2,1)} %get-tuple-element.252.g_ref, bf16[256,8192]{1,0:T(8,128)(2,1)} %get-tuple-element.253.u_ref, ...), custom_call_target="tpu_custom_call" | custom-call | flops 1 | bytes 1 | tf_op jit(solution)/shard_map/pallas_call | solution.py:390
  951.0 7.1 convolution_convert_fusion.1.do_ref
  958.1 12.1 shard_map.203
  971.7 7.2 collective-permute-start.32
  980.7 16.6 collective-permute-start.33
  997.2 12.4 collective-permute-done.33
  1010.0 7.6 fusion.30
  1034.1 19.3 shard_map.204.refs_1_
  1082.1 56.5 %shard_map.211 = (bf16[256,8192]{1,0:T(8,128)(2,1)}, bf16[256,8192]{1,0:T(8,128)(2,1)}, f32[256,2048]{1,0:T(8,128)}) custom-call(s32[1]{0:T(128)} %bitcast.2.shard_ref, bf16[256,2048]{1,0:T(8,128)(2,1)} %broadcast_select_fusion.1.dy_ref, bf16[256,8192]{1,0:T(8,128)(2,1)} %get-tuple-element.241.g_ref, bf16[256,8192]{1,0:T(8,128)(2,1)} %get-tuple-element.242.u_ref, ...), custom_call_target="tpu_custom_call" | custom-call | flops 1 | bytes 1 | tf_op jit(solution)/shard_map/pallas_call | solution.py:390
  1166.5 19.1 collective-permute-done.45.refs_4_.refs_2_.refs_8_.refs_5_
  1225.5 9.5 collective-permute-done.55.refs_8_.refs_6_.refs_3_.refs_5_
  1268.5 7.2 collective-permute-start.60
  1277.0 8.7 collective-permute-done.62.refs_3_.refs_5_.refs_8_.refs_6_
  1285.7 7.1 shard_map.227
  1349.8 10.4 shard_map.218
  1381.3 11.7 collective-permute-start.87
  1406.8 14.2 collective-permute-done.85.refs_7_.refs_4_
  1453.8 12.0 collective-permute-done.88.refs_3_.refs_5_.refs_8_.refs_6_
  1475.6 6.9 shard_map.242
  1610.8 6.9 shard_map.260
  1629.3 7.2 collective-permute-done.101.refs_9_.refs_6_.refs_3_.refs_5_
  1667.2 6.9 shard_map.258
  1713.2 15.1 collective-permute-done.113.refs_3_.refs_9_.refs_5_.refs_6_
  1731.2 19.0 collective-permute-done.115.refs_7_.refs_4_
  1784.9 9.6 collective-permute-done.116.refs_9_.refs_3_.refs_5_.refs_6_
  1801.6 9.6 fusion.23
  1811.3 10.7 collective-permute-done.125.refs_6_.refs_3_.refs_5_.refs_8_
  1879.8 12.6 collective-permute-done.129.refs_6_.refs_3_.refs_5_
  1892.4 8.3 collective-permute-done.130.refs_7_.refs_4_
  1936.3 16.2 collective-permute-done.133.refs_6_.refs_3_.refs_4_
  1992.3 15.0 collective-permute-done.138.refs_5_.refs_2_.refs_3_
  2032.4 12.8 collective-permute-done.141.refs_2_.refs_4_
  2045.2 18.7 collective-permute-done.143.refs_5_.refs_2_
  2085.0 12.4 collective-permute-done.145.refs_1_.refs_4_
  2097.4 17.8 collective-permute-done.147.refs_4_.refs_1_
  (850 shorter events, 983.5 us)
Async XLA Ops:
  7.2 176.1 %all-gather.8.cloned.1.call-start = ((), (), s32[]{:S(2)}) async-start(), calls=%async_computation.1 | async-start | bytes 5242880 | tf_op jit(solution)/shard_map/all_gather | solution.py:716
  55.7 240.2 %all-gather.6.cloned.1.call-start = ((), (), s32[]{:S(2)}) async-start(), calls=%async_computation | async-start | bytes 2621440 | tf_op jit(solution)/shard_map/all_gather | solution.py:716
  67.5 69.4 %collective-permute-start.2 = (bf16[512,3072]{1,0:T(8,128)(2,1)S(1)}, bf16[512,3072]{1,0:T(8,128)(2,1)}, u32[]{:S(2)}, u32[]{:S(2)}) collective-permute-start(bf16[512,3072]{1,0:T(8,128)(2,1)S(1)} %get-tuple-element.474), channel_id=1, source_target_pairs={{0,8},{8,0},{4,12},{12,4},{1,9},{9,1},{5,13},{13,5},{2,10},{10,2},... | collective-permute-start | bytes 9437192 | tf_op jit(solution)/shard_map/ppermute | solution.py:455
  180.5 160.5 %all-gather.10.cloned.1.call-start = ((), (), s32[]{:S(2)}) async-start(), calls=%async_computation.2 | async-start | bytes 5242880 | tf_op jit(solution)/shard_map/all_gather | solution.py:716
  181.3 278.3 %all-gather.12.cloned.1.call-start = ((), (), s32[]{:S(2)}) async-start(), calls=%async_computation.3 | async-start | bytes 10485760 | tf_op jit(solution)/shard_map/all_gather | solution.py:716
  181.5 60.2 %collective-permute-start = (bf16[512,3072]{1,0:T(8,128)(2,1)}, bf16[512,3072]{1,0:T(8,128)(2,1)}, u32[]{:S(2)}, u32[]{:S(2)}) collective-permute-start(bf16[512,3072]{1,0:T(8,128)(2,1)} %bitcast_dynamic-update-slice_fusion.1), channel_id=1, source_target_pairs={{0,4},{4,0},{8,12},{12,8},{1,5},{5,1},{9,13},{13,9},{2,6},{6,2},{1... | collective-permute-start | bytes 9437192 | tf_op jit(solution)/shard_map/ppermute | solution.py:451
  192.0 48.4 %collective-permute-start.14 = (bf16[128,8192]{1,0:T(8,128)(2,1)}, bf16[128,8192]{1,0:T(8,128)(2,1)}, u32[]{:S(2)}, u32[]{:S(2)}) collective-permute-start(bf16[128,8192]{1,0:T(8,128)(2,1)} %select_bitcast_fusion), channel_id=1, source_target_pairs={{0,8},{8,0},{4,12},{12,4},{1,9},{9,1},{5,13},{13,5},{2,10},{10,2},... | collective-permute-start | bytes 6291464 | tf_op jit(solution)/shard_map/ppermute | solution.py:455
  193.8 55.4 %collective-permute-start.3 = (bf16[512,3072]{1,0:T(8,128)(2,1)}, bf16[512,3072]{1,0:T(8,128)(2,1)}, u32[]{:S(2)}, u32[]{:S(2)}) collective-permute-start(bf16[512,3072]{1,0:T(8,128)(2,1)} %collective-permute-done.2), channel_id=1, source_target_pairs={{0,4},{4,0},{8,12},{12,8},{1,5},{5,1},{9,13},{13,9},{2,6},{6,2},{1... | collective-permute-start | bytes 9437192 | tf_op jit(solution)/shard_map/ppermute | solution.py:451
  293.8 182.8 %collective-permute-start.17 = (bf16[2048,2048]{1,0:T(8,128)(2,1)}, bf16[2048,2048]{1,0:T(8,128)(2,1)}, u32[]{:S(2)}, u32[]{:S(2)}) collective-permute-start(bf16[2048,2048]{1,0:T(8,128)(2,1)} %select_select_fusion), channel_id=1, source_target_pairs={{0,8},{8,0},{4,12},{12,4},{1,9},{9,1},{5,13},{13,5},{2,10},{10,2},... | collective-permute-start | bytes 25165832 | tf_op jit(solution)/shard_map/ppermute | solution.py:455
  295.5 181.2 %collective-permute-start.11 = (bf16[512,8192]{1,0:T(8,128)(2,1)}, bf16[512,8192]{1,0:T(8,128)(2,1)}, u32[]{:S(2)}, u32[]{:S(2)}) collective-permute-start(bf16[512,8192]{1,0:T(8,128)(2,1)} %bitcast.138), channel_id=1, source_target_pairs={{0,4},{4,0},{8,12},{12,8},{1,5},{5,1},{9,13},{13,9},{2,6},{6,2},{1... | collective-permute-start | bytes 25165832 | tf_op jit(solution)/shard_map/ppermute | solution.py:451
  296.0 181.1 %collective-permute-start.13 = (bf16[512,8192]{1,0:T(8,128)(2,1)}, bf16[512,8192]{1,0:T(8,128)(2,1)}, u32[]{:S(2)}, u32[]{:S(2)}) collective-permute-start(bf16[512,8192]{1,0:T(8,128)(2,1)} %bitcast.152), channel_id=1, source_target_pairs={{0,4},{4,0},{8,12},{12,8},{1,5},{5,1},{9,13},{13,9},{2,6},{6,2},{1... | collective-permute-start | bytes 25165832 | tf_op jit(solution)/shard_map/ppermute | solution.py:451
  345.8 131.3 %collective-permute-start.12 = (bf16[512,8192]{1,0:T(8,128)(2,1)}, bf16[512,8192]{1,0:T(8,128)(2,1)}, u32[]{:S(2)}, u32[]{:S(2)}) collective-permute-start(bf16[512,8192]{1,0:T(8,128)(2,1)} %constant_dynamic-update-slice_fusion.refs_2_.refs_6_), channel_id=1, source_target_pairs={{0,4},{4,0},{8,12},{12,8},{1,5},{5,1},{9,13},{13,9},{2,6},{6,2},{1... | collective-permute-start | bytes 25165832 | tf_op jit(solution)/shard_map/ppermute | solution.py:451
  725.8 48.5 %collective-permute-start.23 = (bf16[256,1024]{1,0:T(8,128)(2,1)}, bf16[256,1024]{1,0:T(8,128)(2,1)S(1)}, u32[]{:S(2)}, u32[]{:S(2)}) collective-permute-start(bf16[256,1024]{1,0:T(8,128)(2,1)} %get-tuple-element.489), channel_id=1, source_target_pairs={{0,4},{4,0},{8,12},{12,8},{1,5},{5,1},{9,13},{13,9},{2,6},{6,2},{1... | collective-permute-start | bytes 1572872 | tf_op jit(solution)/shard_map/ppermute | solution.py:451
  729.1 45.2 %collective-permute-start.25 = (bf16[256,1024]{1,0:T(8,128)(2,1)}, bf16[256,1024]{1,0:T(8,128)(2,1)}, u32[]{:S(2)}, u32[]{:S(2)}) collective-permute-start(bf16[256,1024]{1,0:T(8,128)(2,1)} %add_convert_fusion.5), channel_id=1, source_target_pairs={{0,8},{8,0},{4,12},{12,4},{1,9},{9,1},{5,13},{13,5},{2,10},{10,2},... | collective-permute-start | bytes 1572872 | tf_op jit(solution)/shard_map/ppermute | solution.py:455
  835.2 53.1 %collective-permute-start.26 = (bf16[256,2048]{1,0:T(8,128)(2,1)}, bf16[256,2048]{1,0:T(8,128)(2,1)}, u32[]{:S(2)}, u32[]{:S(2)}) collective-permute-start(bf16[256,2048]{1,0:T(8,128)(2,1)} %get-tuple-element.488), channel_id=1, source_target_pairs={{16,0},{17,1},{18,2},{19,3},{20,4},{21,5},{22,6},{23,7},{24,8},{25... | collective-permute-start | bytes 3145736 | tf_op jit(solution)/shard_map/ppermute | solution.py:847
  1067.4 81.9 %collective-permute-start.42 = (bf16[512,2048]{1,0:T(8,128)(2,1)}, bf16[512,2048]{1,0:T(8,128)(2,1)}, u32[]{:S(2)}, u32[]{:S(2)}) collective-permute-start(bf16[512,2048]{1,0:T(8,128)(2,1)} %shard_map.213), channel_id=1, source_target_pairs={{0,8},{8,0},{4,12},{12,4},{1,9},{9,1},{5,13},{13,5},{2,10},{10,2},... | collective-permute-start | bytes 6291464 | tf_op jit(solution)/shard_map/ppermute | solution.py:455
  1075.5 86.8 %collective-permute-start.41 = (bf16[512,2048]{1,0:T(8,128)(2,1)}, bf16[512,2048]{1,0:T(8,128)(2,1)}, u32[]{:S(2)}, u32[]{:S(2)}) collective-permute-start(bf16[512,2048]{1,0:T(8,128)(2,1)} %shard_map.210), channel_id=1, source_target_pairs={{0,8},{8,0},{4,12},{12,4},{1,9},{9,1},{5,13},{13,5},{2,10},{10,2},... | collective-permute-start | bytes 6291464 | tf_op jit(solution)/shard_map/ppermute | solution.py:455
  1075.8 62.8 %collective-permute-start.39 = (bf16[2048,256]{1,0:T(8,128)(2,1)}, bf16[2048,256]{1,0:T(8,128)(2,1)S(1)}, u32[]{:S(2)}, u32[]{:S(2)}) collective-permute-start(bf16[2048,256]{1,0:T(8,128)(2,1)} %get-tuple-element.268), channel_id=1, source_target_pairs={{0,4},{4,0},{8,12},{12,8},{1,5},{5,1},{9,13},{13,9},{2,6},{6,2},{1... | collective-permute-start | bytes 3145736 | tf_op jit(solution)/shard_map/ppermute | solution.py:451
  1075.8 69.5 %collective-permute-start.40 = (bf16[2048,256]{1,0:T(8,128)(2,1)}, bf16[2048,256]{1,0:T(8,128)(2,1)}, u32[]{:S(2)}, u32[]{:S(2)}) collective-permute-start(bf16[2048,256]{1,0:T(8,128)(2,1)} %get-tuple-element.269), channel_id=1, source_target_pairs={{0,4},{4,0},{8,12},{12,8},{1,5},{5,1},{9,13},{13,9},{2,6},{6,2},{1... | collective-permute-start | bytes 3145736 | tf_op jit(solution)/shard_map/ppermute | solution.py:451
  1080.3 171.8 %collective-permute-start.52 = (bf16[256,8192]{1,0:T(8,128)(2,1)S(1)}, bf16[256,8192]{1,0:T(8,128)(2,1)}, u32[]{:S(2)}, u32[]{:S(2)}) collective-permute-start(bf16[256,8192]{1,0:T(8,128)(2,1)S(1)} %copy-done), channel_id=1, source_target_pairs={{0,4},{4,0},{8,12},{12,8},{1,5},{5,1},{9,13},{13,9},{2,6},{6,2},{1... | collective-permute-start | bytes 12582920 | tf_op jit(solution)/shard_map/ppermute | solution.py:451
  1138.6 116.9 %collective-permute-start.51 = (bf16[256,8192]{1,0:T(8,128)(2,1)}, bf16[256,8192]{1,0:T(8,128)(2,1)}, u32[]{:S(2)}, u32[]{:S(2)}) collective-permute-start(bf16[256,8192]{1,0:T(8,128)(2,1)} %get-tuple-element.271.refs_9_.refs_4_), channel_id=1, source_target_pairs={{0,4},{4,0},{8,12},{12,8},{1,5},{5,1},{9,13},{13,9},{2,6},{6,2},{1... | collective-permute-start | bytes 12582920 | tf_op jit(solution)/shard_map/ppermute | solution.py:451
  1145.2 60.3 %collective-permute-start.57 = (bf16[512,2048]{1,0:T(8,128)(2,1)}, bf16[512,2048]{1,0:T(8,128)(2,1)}, u32[]{:S(2)}, u32[]{:S(2)}) collective-permute-start(bf16[512,2048]{1,0:T(8,128)(2,1)} %shard_map.222), channel_id=1, source_target_pairs={{0,8},{8,0},{4,12},{12,4},{1,9},{9,1},{5,13},{13,5},{2,10},{10,2},... | collective-permute-start | bytes 6291464 | tf_op jit(solution)/shard_map/ppermute | solution.py:455
  1221.6 54.0 %collective-permute-start.61 = (bf16[512,2048]{1,0:T(8,128)(2,1)}, bf16[512,2048]{1,0:T(8,128)(2,1)}, u32[]{:S(2)}, u32[]{:S(2)}) collective-permute-start(bf16[512,2048]{1,0:T(8,128)(2,1)} %shard_map.226), channel_id=1, source_target_pairs={{0,8},{8,0},{4,12},{12,4},{1,9},{9,1},{5,13},{13,5},{2,10},{10,2},... | collective-permute-start | bytes 6291464 | tf_op jit(solution)/shard_map/ppermute | solution.py:455
  1255.5 37.3 %collective-permute-start.63 = (bf16[512,1024]{1,0:T(8,128)(2,1)}, bf16[512,1024]{1,0:T(8,128)(2,1)S(1)}, u32[]{:S(2)}, u32[]{:S(2)}) collective-permute-start(bf16[512,1024]{1,0:T(8,128)(2,1)} %get-tuple-element.299.refs_1_), channel_id=1, source_target_pairs={{1,0},{2,1},{3,2},{5,4},{6,5},{7,6},{9,8},{10,9},{11,10},{13,12},{... | collective-permute-start | bytes 3145736 | tf_op jit(solution)/shard_map/ppermute | solution.py:629
  1263.2 59.7 %collective-permute-start.56 = (bf16[512,2048]{1,0:T(8,128)(2,1)}, bf16[512,2048]{1,0:T(8,128)(2,1)}, u32[]{:S(2)}, u32[]{:S(2)}) collective-permute-start(bf16[512,2048]{1,0:T(8,128)(2,1)} %shard_map.221), channel_id=1, source_target_pairs={{0,8},{8,0},{4,12},{12,4},{1,9},{9,1},{5,13},{13,5},{2,10},{10,2},... | collective-permute-start | bytes 6291464 | tf_op jit(solution)/shard_map/ppermute | solution.py:455
  1268.5 42.9 %collective-permute-start.60 = (bf16[512,1024]{1,0:T(8,128)(2,1)}, bf16[512,1024]{1,0:T(8,128)(2,1)S(1)}, u32[]{:S(2)}, u32[]{:S(2)}) collective-permute-start(bf16[512,1024]{1,0:T(8,128)(2,1)} %get-tuple-element.294.refs_0_), channel_id=1, source_target_pairs={{0,1},{1,2},{4,5},{5,6},{8,9},{9,10},{12,13},{13,14},{16,17},{17,1... | collective-permute-start | bytes 3145736 | tf_op jit(solution)/shard_map/ppermute | solution.py:628
  1275.7 35.8 %collective-permute-start.66 = (bf16[512,1024]{1,0:T(8,128)(2,1)}, bf16[512,1024]{1,0:T(8,128)(2,1)}, u32[]{:S(2)}, u32[]{:S(2)}) collective-permute-start(bf16[512,1024]{1,0:T(8,128)(2,1)} %get-tuple-element.302.refs_1_), channel_id=1, source_target_pairs={{1,0},{2,1},{3,2},{5,4},{6,5},{7,6},{9,8},{10,9},{11,10},{13,12},{... | collective-permute-start | bytes 3145736 | tf_op jit(solution)/shard_map/ppermute | solution.py:629
  1311.5 81.5 %collective-permute-start.80 = (bf16[512,2048]{1,0:T(8,128)(2,1)}, bf16[512,2048]{1,0:T(8,128)(2,1)}, u32[]{:S(2)}, u32[]{:S(2)}) collective-permute-start(bf16[512,2048]{1,0:T(8,128)(2,1)} %shard_map.233), channel_id=1, source_target_pairs={{0,8},{8,0},{4,12},{12,4},{1,9},{9,1},{5,13},{13,5},{2,10},{10,2},... | collective-permute-start | bytes 6291464 | tf_op jit(solution)/shard_map/ppermute | solution.py:455
  1318.3 48.7 %collective-permute-start.81 = (bf16[512,1024]{1,0:T(8,128)(2,1)}, bf16[512,1024]{1,0:T(8,128)(2,1)S(1)}, u32[]{:S(2)}, u32[]{:S(2)}) collective-permute-start(bf16[512,1024]{1,0:T(8,128)(2,1)} %get-tuple-element.314.refs_2_.refs_0_), channel_id=1, source_target_pairs={{0,1},{1,2},{2,3},{4,5},{5,6},{6,7},{8,9},{9,10},{10,11},{12,13},{... | collective-permute-start | bytes 3145736 | tf_op jit(solution)/shard_map/ppermute | solution.py:628
  1322.9 44.1 %collective-permute-start.82 = (bf16[512,1024]{1,0:T(8,128)(2,1)}, bf16[512,1024]{1,0:T(8,128)(2,1)S(1)}, u32[]{:S(2)}, u32[]{:S(2)}) collective-permute-start(bf16[512,1024]{1,0:T(8,128)(2,1)} %get-tuple-element.317.refs_3_.refs_1_), channel_id=1, source_target_pairs={{1,0},{2,1},{3,2},{5,4},{6,5},{7,6},{9,8},{10,9},{11,10},{13,12},{... | collective-permute-start | bytes 3145736 | tf_op jit(solution)/shard_map/ppermute | solution.py:629
  1336.4 44.9 %collective-permute-start.67 = (bf16[512,1024]{1,0:T(8,128)(2,1)}, bf16[512,1024]{1,0:T(8,128)(2,1)S(1)}, u32[]{:S(2)}, u32[]{:S(2)}) collective-permute-start(bf16[512,1024]{1,0:T(8,128)(2,1)} %get-tuple-element.303.refs_4_.refs_2_.refs_0_), channel_id=1, source_target_pairs={{0,1},{1,2},{2,3},{4,5},{5,6},{6,7},{8,9},{9,10},{10,11},{12,13},{... | collective-permute-start | bytes 3145736 | tf_op jit(solution)/shard_map/ppermute | solution.py:628
  1366.9 119.8 %collective-permute-start.79 = (bf16[256,8192]{1,0:T(8,128)(2,1)}, bf16[256,8192]{1,0:T(8,128)(2,1)}, u32[]{:S(2)}, u32[]{:S(2)}) collective-permute-start(bf16[256,8192]{1,0:T(8,128)(2,1)} %get-tuple-element.312.refs_5_), channel_id=1, source_target_pairs={{0,4},{4,0},{8,12},{12,8},{1,5},{5,1},{9,13},{13,9},{2,6},{6,2},{1... | collective-permute-start | bytes 12582920 | tf_op jit(solution)/shard_map/ppermute | solution.py:451
  1367.0 124.4 %collective-permute-start.78 = (bf16[256,8192]{1,0:T(8,128)(2,1)}, bf16[256,8192]{1,0:T(8,128)(2,1)}, u32[]{:S(2)}, u32[]{:S(2)}) collective-permute-start(bf16[256,8192]{1,0:T(8,128)(2,1)} %get-tuple-element.311.refs_4_), channel_id=1, source_target_pairs={{0,4},{4,0},{8,12},{12,8},{1,5},{5,1},{9,13},{13,9},{2,6},{6,2},{1... | collective-permute-start | bytes 12582920 | tf_op jit(solution)/shard_map/ppermute | solution.py:451
  1381.3 62.9 %collective-permute-start.87 = (bf16[512,2048]{1,0:T(8,128)(2,1)}, bf16[512,2048]{1,0:T(8,128)(2,1)}, u32[]{:S(2)}, u32[]{:S(2)}) collective-permute-start(bf16[512,2048]{1,0:T(8,128)(2,1)} %shard_map.241), channel_id=1, source_target_pairs={{0,8},{8,0},{4,12},{12,4},{1,9},{9,1},{5,13},{13,5},{2,10},{10,2},... | collective-permute-start | bytes 6291464 | tf_op jit(solution)/shard_map/ppermute | solution.py:455
  1401.8 40.2 %collective-permute-start.84 = (bf16[512,1024]{1,0:T(8,128)(2,1)}, bf16[512,1024]{1,0:T(8,128)(2,1)S(1)}, u32[]{:S(2)}, u32[]{:S(2)}) collective-permute-start(bf16[512,1024]{1,0:T(8,128)(2,1)} %get-tuple-element.319.refs_5_.refs_3_.refs_1_), channel_id=1, source_target_pairs={{1,0},{2,1},{3,2},{5,4},{6,5},{7,6},{9,8},{10,9},{11,10},{13,12},{... | collective-permute-start | bytes 3145736 | tf_op jit(solution)/shard_map/ppermute | solution.py:629
  1422.0 91.6 %collective-permute-start.69 = (bf16[768,2048]{1,0:T(8,128)(2,1)}, bf16[768,2048]{1,0:T(8,128)(2,1)}, u32[]{:S(2)}, u32[]{:S(2)}) collective-permute-start(bf16[768,2048]{1,0:T(8,128)(2,1)} %fusion.1), channel_id=1, source_target_pairs={{0,8},{8,0},{4,12},{12,4},{1,9},{9,1},{5,13},{13,5},{2,10},{10,2},... | collective-permute-start | bytes 9437192 | tf_op jit(solution)/shard_map/ppermute | solution.py:455
  1486.7 39.3 %collective-permute-start.90 = (bf16[512,1024]{1,0:T(8,128)(2,1)}, bf16[512,1024]{1,0:T(8,128)(2,1)S(1)}, u32[]{:S(2)}, u32[]{:S(2)}) collective-permute-start(bf16[512,1024]{1,0:T(8,128)(2,1)} %get-tuple-element.332.refs_4_.refs_2_.refs_0_), channel_id=1, source_target_pairs={{0,1},{1,2},{2,3},{4,5},{5,6},{6,7},{8,9},{9,10},{10,11},{12,13},{... | collective-permute-start | bytes 3145736 | tf_op jit(solution)/shard_map/ppermute | solution.py:628
  1498.9 68.8 %collective-permute-start.95 = (bf16[512,2048]{1,0:T(8,128)(2,1)}, bf16[512,2048]{1,0:T(8,128)(2,1)}, u32[]{:S(2)}, u32[]{:S(2)}) collective-permute-start(bf16[512,2048]{1,0:T(8,128)(2,1)} %shard_map.250), channel_id=1, source_target_pairs={{0,8},{8,0},{4,12},{12,4},{1,9},{9,1},{5,13},{13,5},{2,10},{10,2},... | collective-permute-start | bytes 6291464 | tf_op jit(solution)/shard_map/ppermute | solution.py:455
  1508.9 39.0 %collective-permute-start.96 = (bf16[512,1024]{1,0:T(8,128)(2,1)}, bf16[512,1024]{1,0:T(8,128)(2,1)S(1)}, u32[]{:S(2)}, u32[]{:S(2)}) collective-permute-start(bf16[512,1024]{1,0:T(8,128)(2,1)} %get-tuple-element.341.refs_4_.refs_2_.refs_0_), channel_id=1, source_target_pairs={{0,1},{1,2},{2,3},{4,5},{5,6},{6,7},{8,9},{9,10},{10,11},{12,13},{... | collective-permute-start | bytes 3145736 | tf_op jit(solution)/shard_map/ppermute | solution.py:628
  1542.5 63.0 %collective-permute-start.102 = (bf16[512,2048]{1,0:T(8,128)(2,1)}, bf16[512,2048]{1,0:T(8,128)(2,1)}, u32[]{:S(2)}, u32[]{:S(2)}) collective-permute-start(bf16[512,2048]{1,0:T(8,128)(2,1)} %shard_map.259), channel_id=1, source_target_pairs={{0,8},{8,0},{4,12},{12,4},{1,9},{9,1},{5,13},{13,5},{2,10},{10,2},... | collective-permute-start | bytes 6291464 | tf_op jit(solution)/shard_map/ppermute | solution.py:455
  1567.7 93.5 %collective-permute-start.94 = (bf16[512,2048]{1,0:T(8,128)(2,1)}, bf16[512,2048]{1,0:T(8,128)(2,1)}, u32[]{:S(2)}, u32[]{:S(2)}) collective-permute-start(bf16[512,2048]{1,0:T(8,128)(2,1)} %shard_map.249), channel_id=1, source_target_pairs={{0,8},{8,0},{4,12},{12,4},{1,9},{9,1},{5,13},{13,5},{2,10},{10,2},... | collective-permute-start | bytes 6291464 | tf_op jit(solution)/shard_map/ppermute | solution.py:455
  1623.7 38.9 %collective-permute-start.105 = (bf16[512,1024]{1,0:T(8,128)(2,1)}, bf16[512,1024]{1,0:T(8,128)(2,1)S(1)}, u32[]{:S(2)}, u32[]{:S(2)}) collective-permute-start(bf16[512,1024]{1,0:T(8,128)(2,1)} %get-tuple-element.361.refs_4_.refs_2_.refs_0_), channel_id=1, source_target_pairs={{0,1},{1,2},{2,3},{4,5},{5,6},{6,7},{8,9},{9,10},{10,11},{12,13},{... | collective-permute-start | bytes 3145736 | tf_op jit(solution)/shard_map/ppermute | solution.py:628
  1660.4 51.4 %collective-permute-start.110 = (bf16[512,2048]{1,0:T(8,128)(2,1)}, bf16[512,2048]{1,0:T(8,128)(2,1)}, u32[]{:S(2)}, u32[]{:S(2)}) collective-permute-start(bf16[512,2048]{1,0:T(8,128)(2,1)} %shard_map.268), channel_id=1, source_target_pairs={{0,8},{8,0},{4,12},{12,4},{1,9},{9,1},{5,13},{13,5},{2,10},{10,2},... | collective-permute-start | bytes 6291464 | tf_op jit(solution)/shard_map/ppermute | solution.py:455
  1662.7 37.6 %collective-permute-start.119 = (bf16[256,2048]{1,0:T(8,128)(2,1)S(1)}, bf16[256,2048]{1,0:T(8,128)(2,1)}, u32[]{:S(2)}, u32[]{:S(2)}) collective-permute-start(bf16[256,2048]{1,0:T(8,128)(2,1)S(1)} %copy-done.77), channel_id=1, source_target_pairs={{0,4},{4,0},{8,12},{12,8},{1,5},{5,1},{9,13},{13,9},{2,6},{6,2},{1... | collective-permute-start | bytes 3145736 | tf_op jit(solution)/shard_map/ppermute | solution.py:451
  1702.3 47.8 %collective-permute-start.115 = (bf16[512,1024]{1,0:T(8,128)(2,1)}, bf16[512,1024]{1,0:T(8,128)(2,1)}, u32[]{:S(2)}, u32[]{:S(2)}) collective-permute-start(bf16[512,1024]{1,0:T(8,128)(2,1)} %get-tuple-element.378.refs_5_.refs_3_.refs_1_), channel_id=1, source_target_pairs={{1,0},{2,1},{3,2},{5,4},{6,5},{7,6},{9,8},{10,9},{11,10},{13,12},{... | collective-permute-start | bytes 3145736 | tf_op jit(solution)/shard_map/ppermute | solution.py:629
  1711.6 60.9 %collective-permute-start.75 = (bf16[256,3072]{1,0:T(8,128)(2,1)S(1)}, bf16[256,3072]{1,0:T(8,128)(2,1)S(1)}, u32[]{:S(2)}, u32[]{:S(2)}) collective-permute-start(bf16[256,3072]{1,0:T(8,128)(2,1)S(1)} %pad_maximum_fusion.refs_5_), channel_id=1, source_target_pairs={{0,4},{4,0},{8,12},{12,8},{1,5},{5,1},{9,13},{13,9},{2,6},{6,2},{1... | collective-permute-start | bytes 4718600 | tf_op jit(solution)/shard_map/ppermute | solution.py:451
  1711.9 83.7 %collective-permute-start.123 = (bf16[512,2048]{1,0:T(8,128)(2,1)}, bf16[512,2048]{1,0:T(8,128)(2,1)}, u32[]{:S(2)}, u32[]{:S(2)}) collective-permute-start(bf16[512,2048]{1,0:T(8,128)(2,1)} %shard_map.278), channel_id=1, source_target_pairs={{0,8},{8,0},{4,12},{12,4},{1,9},{9,1},{5,13},{13,5},{2,10},{10,2},... | collective-permute-start | bytes 6291464 | tf_op jit(solution)/shard_map/ppermute | solution.py:455
  1728.4 44.4 %collective-permute-start.74 = (bf16[256,3072]{1,0:T(8,128)(2,1)S(1)}, bf16[256,3072]{1,0:T(8,128)(2,1)S(1)}, u32[]{:S(2)}, u32[]{:S(2)}) collective-permute-start(bf16[256,3072]{1,0:T(8,128)(2,1)S(1)} %pad_maximum_fusion.1.refs_4_), channel_id=1, source_target_pairs={{0,4},{4,0},{8,12},{12,8},{1,5},{5,1},{9,13},{13,9},{2,6},{6,2},{1... | collective-permute-start | bytes 4718600 | tf_op jit(solution)/shard_map/ppermute | solution.py:451
  1728.4 40.9 %collective-permute-start.76 = (bf16[512,256]{1,0:T(8,128)(2,1)}, bf16[512,256]{1,0:T(8,128)(2,1)S(1)}, u32[]{:S(2)}, u32[]{:S(2)}) collective-permute-start(bf16[512,256]{1,0:T(8,128)(2,1)} %get-tuple-element.309), channel_id=1, source_target_pairs={{0,4},{4,0},{8,12},{12,8},{1,5},{5,1},{9,13},{13,9},{2,6},{6,2},{1... | collective-permute-start | bytes 786440 | tf_op jit(solution)/shard_map/ppermute | solution.py:451
  1784.3 67.1 %collective-permute-start.72 = (bf16[512,256]{1,0:T(8,128)(2,1)}, bf16[512,256]{1,0:T(8,128)(2,1)S(1)}, u32[]{:S(2)}, u32[]{:S(2)}) collective-permute-start(bf16[512,256]{1,0:T(8,128)(2,1)} %get-tuple-element.306), channel_id=1, source_target_pairs={{0,4},{4,0},{8,12},{12,8},{1,5},{5,1},{9,13},{13,9},{2,6},{6,2},{1... | collective-permute-start | bytes 786440 | tf_op jit(solution)/shard_map/ppermute | solution.py:451
  1784.5 68.2 %collective-permute-start.73 = (bf16[512,256]{1,0:T(8,128)(2,1)}, bf16[512,256]{1,0:T(8,128)(2,1)}, u32[]{:S(2)}, u32[]{:S(2)}) collective-permute-start(bf16[512,256]{1,0:T(8,128)(2,1)} %get-tuple-element.307), channel_id=1, source_target_pairs={{0,4},{4,0},{8,12},{12,8},{1,5},{5,1},{9,13},{13,9},{2,6},{6,2},{1... | collective-permute-start | bytes 786440 | tf_op jit(solution)/shard_map/ppermute | solution.py:451
  1794.4 64.3 %collective-permute-start.109 = (bf16[512,2048]{1,0:T(8,128)(2,1)}, bf16[512,2048]{1,0:T(8,128)(2,1)}, u32[]{:S(2)}, u32[]{:S(2)}) collective-permute-start(bf16[512,2048]{1,0:T(8,128)(2,1)} %shard_map.267), channel_id=1, source_target_pairs={{0,8},{8,0},{4,12},{12,4},{1,9},{9,1},{5,13},{13,5},{2,10},{10,2},... | collective-permute-start | bytes 6291464 | tf_op jit(solution)/shard_map/ppermute | solution.py:455
  1800.0 37.3 %collective-permute-start.126 = (bf16[512,1024]{1,0:T(8,128)(2,1)S(1)}, bf16[512,1024]{1,0:T(8,128)(2,1)S(1)}, u32[]{:S(2)}, u32[]{:S(2)}) collective-permute-start(bf16[512,1024]{1,0:T(8,128)(2,1)S(1)} %copy-done.66), channel_id=1, source_target_pairs={{1,0},{2,1},{3,2},{5,4},{6,5},{7,6},{9,8},{10,9},{11,10},{13,12},{... | collective-permute-start | bytes 3145736 | tf_op jit(solution)/shard_map/ppermute | solution.py:629
  1842.4 36.1 %collective-permute-start.127 = (bf16[512,1024]{1,0:T(8,128)(2,1)}, bf16[512,1024]{1,0:T(8,128)(2,1)S(1)}, u32[]{:S(2)}, u32[]{:S(2)}) collective-permute-start(bf16[512,1024]{1,0:T(8,128)(2,1)} %get-tuple-element.400.refs_4_.refs_2_.refs_0_), channel_id=1, source_target_pairs={{0,1},{1,2},{2,3},{4,5},{5,6},{6,7},{8,9},{9,10},{10,11},{12,13},{... | collective-permute-start | bytes 3145736 | tf_op jit(solution)/shard_map/ppermute | solution.py:628
  1852.7 39.7 %collective-permute-start.129 = (bf16[512,1024]{1,0:T(8,128)(2,1)}, bf16[512,1024]{1,0:T(8,128)(2,1)S(1)}, u32[]{:S(2)}, u32[]{:S(2)}) collective-permute-start(bf16[512,1024]{1,0:T(8,128)(2,1)} %get-tuple-element.404.refs_4_.refs_2_.refs_0_), channel_id=1, source_target_pairs={{0,1},{1,2},{2,3},{4,5},{5,6},{6,7},{8,9},{9,10},{10,11},{12,13},{... | collective-permute-start | bytes 3145736 | tf_op jit(solution)/shard_map/ppermute | solution.py:628
  1857.3 43.3 %collective-permute-start.130 = (bf16[512,1024]{1,0:T(8,128)(2,1)}, bf16[512,1024]{1,0:T(8,128)(2,1)S(1)}, u32[]{:S(2)}, u32[]{:S(2)}) collective-permute-start(bf16[512,1024]{1,0:T(8,128)(2,1)} %get-tuple-element.405.refs_5_.refs_3_.refs_1_), channel_id=1, source_target_pairs={{1,0},{2,1},{3,2},{5,4},{6,5},{7,6},{9,8},{10,9},{11,10},{13,12},{... | collective-permute-start | bytes 3145736 | tf_op jit(solution)/shard_map/ppermute | solution.py:629
  1858.7 59.6 %collective-permute-start.71 = (bf16[2,512]{1,0:T(2,128)(2,1)S(1)}, bf16[2,512]{1,0:T(2,128)(2,1)S(1)}, u32[]{:S(2)}, u32[]{:S(2)}) collective-permute-start(bf16[2,512]{1,0:T(2,128)(2,1)S(1)} %constant_dynamic-slice_fusion), channel_id=1, source_target_pairs={{0,8},{8,0},{4,12},{12,4},{1,9},{9,1},{5,13},{13,5},{2,10},{10,2},... | collective-permute-start | bytes 6152 | tf_op jit(solution)/shard_map/ppermute | solution.py:455
  1878.6 50.4 %collective-permute-start.137 = (bf16[512,1024]{1,0:T(8,128)(2,1)}, bf16[512,1024]{1,0:T(8,128)(2,1)}, u32[]{:S(2)}, u32[]{:S(2)}) collective-permute-start(bf16[512,1024]{1,0:T(8,128)(2,1)} %shard_map.292), channel_id=1, source_target_pairs={{0,8},{8,0},{4,12},{12,4},{1,9},{9,1},{5,13},{13,5},{2,10},{10,2},... | collective-permute-start | bytes 3145736 | tf_op jit(solution)/shard_map/ppermute | solution.py:455
  1913.7 38.8 %collective-permute-start.133 = (bf16[512,1024]{1,0:T(8,128)(2,1)}, bf16[512,1024]{1,0:T(8,128)(2,1)S(1)}, u32[]{:S(2)}, u32[]{:S(2)}) collective-permute-start(bf16[512,1024]{1,0:T(8,128)(2,1)} %get-tuple-element.412.refs_4_.refs_2_.refs_0_), channel_id=1, source_target_pairs={{0,1},{1,2},{2,3},{4,5},{5,6},{6,7},{8,9},{9,10},{10,11},{12,13},{... | collective-permute-start | bytes 3145736 | tf_op jit(solution)/shard_map/ppermute | solution.py:628
  1918.3 38.3 %collective-permute-start.134 = (bf16[512,1024]{1,0:T(8,128)(2,1)}, bf16[512,1024]{1,0:T(8,128)(2,1)S(1)}, u32[]{:S(2)}, u32[]{:S(2)}) collective-permute-start(bf16[512,1024]{1,0:T(8,128)(2,1)} %get-tuple-element.413.refs_5_.refs_3_.refs_1_), channel_id=1, source_target_pairs={{1,0},{2,1},{3,2},{5,4},{6,5},{7,6},{9,8},{10,9},{11,10},{13,12},{... | collective-permute-start | bytes 3145736 | tf_op jit(solution)/shard_map/ppermute | solution.py:629
  1969.6 37.7 %collective-permute-start.138 = (bf16[512,1024]{1,0:T(8,128)(2,1)}, bf16[512,1024]{1,0:T(8,128)(2,1)S(1)}, u32[]{:S(2)}, u32[]{:S(2)}) collective-permute-start(bf16[512,1024]{1,0:T(8,128)(2,1)} %get-tuple-element.420.refs_4_.refs_2_.refs_0_), channel_id=1, source_target_pairs={{0,1},{1,2},{2,3},{4,5},{5,6},{6,7},{8,9},{9,10},{10,11},{12,13},{... | collective-permute-start | bytes 3145736 | tf_op jit(solution)/shard_map/ppermute | solution.py:628
  1974.2 37.1 %collective-permute-start.139 = (bf16[512,1024]{1,0:T(8,128)(2,1)}, bf16[512,1024]{1,0:T(8,128)(2,1)S(1)}, u32[]{:S(2)}, u32[]{:S(2)}) collective-permute-start(bf16[512,1024]{1,0:T(8,128)(2,1)} %get-tuple-element.421.refs_5_.refs_3_.refs_1_), channel_id=1, source_target_pairs={{1,0},{2,1},{3,2},{5,4},{6,5},{7,6},{9,8},{10,9},{11,10},{13,12},{... | collective-permute-start | bytes 3145736 | tf_op jit(solution)/shard_map/ppermute | solution.py:629
  2022.9 41.0 %collective-permute-start.143 = (bf16[512,1024]{1,0:T(8,128)(2,1)}, bf16[512,1024]{1,0:T(8,128)(2,1)S(1)}, u32[]{:S(2)}, u32[]{:S(2)}) collective-permute-start(bf16[512,1024]{1,0:T(8,128)(2,1)} %get-tuple-element.429.refs_5_.refs_3_.refs_1_), channel_id=1, source_target_pairs={{1,0},{2,1},{5,4},{6,5},{9,8},{10,9},{13,12},{14,13},{17,16},{18,1... | collective-permute-start | bytes 3145736 | tf_op jit(solution)/shard_map/ppermute | solution.py:629
  2075.6 39.6 %collective-permute-start.147 = (bf16[512,1024]{1,0:T(8,128)(2,1)}, bf16[512,1024]{1,0:T(8,128)(2,1)}, u32[]{:S(2)}, u32[]{:S(2)}) collective-permute-start(bf16[512,1024]{1,0:T(8,128)(2,1)} %get-tuple-element.437.refs_5_.refs_3_.refs_1_), channel_id=1, source_target_pairs={{1,0},{5,4},{9,8},{13,12},{17,16},{21,20},{25,24},{29,28}} | collective-permute-start | bytes 3145736 | tf_op jit(solution)/shard_map/ppermute | solution.py:629
  (252 other events, 6408.0 us)
Sparse Core Ops, SparseCore 0:
  55.9 82.2 all-gather.7
  180.7 47.6 all-gather.5
  230.5 79.3 all-gather.9
  311.4 148.1 all-gather.11
